TPU v7x, 256 devices: a whole 4x4x8 slice. The times are simulated.
256 devices in a mesh: grp: 2 (over z_lo), wide: 32 (over z_hi, y, core), narrow: 4 (over x).
Axes of the slice: x: 4, y: 4, z: 8 (z_hi: 4, z_lo: 2; z = z_hi * 2 + z_lo), core: 2. Of those that a mesh axis runs over, the one named last changes fastest.
Arguments:
- tokens: bfloat16 [5120, 50, 384], P(('grp', 'wide', 'narrow')), may hold values from -21 to 21
- grad_out: bfloat16 [5120, 50, 384], P(('grp', 'wide', 'narrow')), may hold values from -21 to 21
- weight_qkv: float32 [2, 384, 1152], replicated, may hold values from -0.3125 to 0.3125
- weight_proj: float32 [2, 384, 384], replicated, may hold values from -0.625 to 0.625
- weight_up: float32 [2, 384, 1536], replicated, may hold values from -0.3125 to 0.3125
- weight_down: float32 [2, 1536, 384], replicated, may hold values from -0.15625 to 0.15625
- weight_vector: float32 [2, 4608], replicated, may hold values from 0.5 to 1.5
- old_first_qkv: float32 [2, 384, 1152], P(None, ('wide', 'narrow')), may hold values from -112 to 112
- old_first_proj: float32 [2, 384, 384], P(None, ('wide', 'narrow')), may hold values from -112 to 112
- old_first_up: float32 [2, 384, 1536], P(None, ('wide', 'narrow')), may hold values from -112 to 112
- old_first_down: float32 [2, 1536, 384], P(None, ('wide', 'narrow')), may hold values from -256 to 256
- old_first_vector: float32 [2, 4608], P(None, ('wide', 'narrow')), may hold values from -160 to 160
- old_second_qkv: float32 [2, 384, 1152], P(None, ('wide', 'narrow')), may hold values from 1696 to 6784
- old_second_proj: float32 [2, 384, 384], P(None, ('wide', 'narrow')), may hold values from 1696 to 6784
- old_second_up: float32 [2, 384, 1536], P(None, ('wide', 'narrow')), may hold values from 1696 to 6784
- old_second_down: float32 [2, 1536, 384], P(None, ('wide', 'narrow')), may hold values from 9768.96 to 39075.84
- old_second_vector: float32 [2, 4608], P(None, ('wide', 'narrow')), may hold values from 67840 to 271360
- old_outer_qkv: float32 [2, 384, 1152], P(None, ('wide', 'narrow')), may hold values from -0.15625 to 0.15625
- old_outer_proj: float32 [2, 384, 384], P(None, ('wide', 'narrow')), may hold values from -0.3125 to 0.3125
- old_outer_up: float32 [2, 384, 1536], P(None, ('wide', 'narrow')), may hold values from -0.15625 to 0.15625
- old_outer_down: float32 [2, 1536, 384], P(None, ('wide', 'narrow')), may hold values from -0.078125 to 0.078125
- old_outer_vector: float32 [2, 4608], P(None, ('wide', 'narrow')), may hold values from -1.25 to 1.25
Outputs:
- block_out: bfloat16 [5120, 50, 384], P(('grp', 'wide', 'narrow'))
- grad_tokens: float32 [5120, 50, 384], P(('grp', 'wide', 'narrow'))
- new_first_qkv: float32 [2, 2, 384, 1152], P('grp', None, ('wide', 'narrow'))
- new_first_proj: float32 [2, 2, 384, 384], P('grp', None, ('wide', 'narrow'))
- new_first_up: float32 [2, 2, 384, 1536], P('grp', None, ('wide', 'narrow'))
- new_first_down: float32 [2, 2, 1536, 384], P('grp', None, ('wide', 'narrow'))
- new_first_vector: float32 [2, 2, 4608], P('grp', None, ('wide', 'narrow'))
- new_second_qkv: float32 [2, 2, 384, 1152], P('grp', None, ('wide', 'narrow'))
- new_second_proj: float32 [2, 2, 384, 384], P('grp', None, ('wide', 'narrow'))
- new_second_up: float32 [2, 2, 384, 1536], P('grp', None, ('wide', 'narrow'))
- new_second_down: float32 [2, 2, 1536, 384], P('grp', None, ('wide', 'narrow'))
- new_second_vector: float32 [2, 2, 4608], P('grp', None, ('wide', 'narrow'))
- change_qkv: float32 [2, 384, 1152], P(None, ('wide', 'narrow'))
- change_proj: float32 [2, 384, 384], P(None, ('wide', 'narrow'))
- change_up: float32 [2, 384, 1536], P(None, ('wide', 'narrow'))
- change_down: float32 [2, 1536, 384], P(None, ('wide', 'narrow'))
- change_vector: float32 [2, 4608], P(None, ('wide', 'narrow'))
- new_outer_qkv: float32 [2, 384, 1152], P(None, ('wide', 'narrow'))
- new_outer_proj: float32 [2, 384, 384], P(None, ('wide', 'narrow'))
- new_outer_up: float32 [2, 384, 1536], P(None, ('wide', 'narrow'))
- new_outer_down: float32 [2, 1536, 384], P(None, ('wide', 'narrow'))
- new_outer_vector: float32 [2, 4608], P(None, ('wide', 'narrow'))
- final_qkv: float32 [2, 384, 1152], P(None, ('wide', 'narrow'))
- final_proj: float32 [2, 384, 384], P(None, ('wide', 'narrow'))
- final_up: float32 [2, 384, 1536], P(None, ('wide', 'narrow'))
- final_down: float32 [2, 1536, 384], P(None, ('wide', 'narrow'))
- final_vector: float32 [2, 4608], P(None, ('wide', 'narrow'))
- copy_qkv: bfloat16 [2, 384, 1152], P(None, ('wide', 'narrow'))
- copy_proj: bfloat16 [2, 384, 384], P(None, ('wide', 'narrow'))
- copy_up: bfloat16 [2, 384, 1536], P(None, ('wide', 'narrow'))
- copy_down: bfloat16 [2, 1536, 384], P(None, ('wide', 'narrow'))
- copy_vector: bfloat16 [2, 4608], P(None, ('wide', 'narrow'))
- stream_rms: float32 [2, 3], replicated
All inputs are finite; a program needn't handle non-finite values.
Results may differ from a plain program's by a relative error of at most 0.02.
Values sent between devices are 32-bit elements; how exact they have to be, the bound alone decides.
No kernel may reach another device: no remote copies, remote signals or barrier semaphores. Data moves between devices by JAX's collectives and lax.ppermute only.
A program may use at most 192 MiB of HBM per device.

v0:
```python
import jax
import jax.numpy as jnp
from jax import lax
from jax.experimental import pallas as pl
from jax.experimental.pallas import tpu as pltpu
from jax.sharding import PartitionSpec as P

D = 384
HEADS = 6
HEAD_DIM = 64
FF = 1536
SEQ = 50
STEP = 10


beta_one = 0.9
beta_two = 0.95
adam_eps = 1e-08
decay_rate = 0.1
outer_decay = 0.9
outer_rate = 0.7


def rates():
    return (1.5 * D ** (-0.5), 1.5 * (D // 4) ** (-0.5), 1.5 * D ** (-0.5), 1.5 * FF ** (-0.5), 2.0)


ROWS = 112
UP_AT, DOWN_AT, QKV_AT, PROJ_AT, SMALL_AT = 0, 36, 72, 99, 108
SUMS_AT = 64
VMEM_WHOLE = pl.BlockSpec(memory_space=pltpu.VMEM)
GROUP_AXES = ("wide", "narrow")


def place_of(owner):
    return owner // 32, owner // 8 % 4, owner // 4 % 2, owner % 4


def owner_of(deep, high, core, across):
    return ((deep * 4 + high) * 2 + core) * 4 + across


def core_pairs():
    return [(o, o ^ 4) for o in range(128)]


def ring_pairs(stage, shift):
    pairs = []
    for o in range(128):
        deep, high, core, across = place_of(o)
        if stage == 2:
            deep = (deep + shift) % 4
        elif core == stage:
            across = (across + shift) % 4
        else:
            high = (high + shift) % 4
        pairs.append((o, owner_of(deep, high, core, across)))
    return pairs


IMG = 10
CHUNKS = 2
RUN = 512
REAL = IMG * SEQ
STEP_ROWS = 512
TOGETHER = 5
TOGETHER_BACK = 5
G1, B1, BQ, BV, BO, G2, B2, BU, BD = 0, 384, 768, 1152, 1536, 1920, 2304, 2688, 4224
BF = jnp.bfloat16
F32 = jnp.float32


def dot(left, right, left_dim=1, right_dim=0):
    return lax.dot_general(
        left, right, (((left_dim,), (right_dim,)), ((), ())), preferred_element_type=F32
    )


def normalise(rows):
    center = rows - jnp.sum(rows, -1, keepdims=True) * (1 / D)
    rate = lax.rsqrt(jnp.sum(center * center, -1, keepdims=True) * (1 / D) + 1e-06)
    return center * rate, rate


def norm_back(grad, unit, rate, gain):
    scaled = grad * gain
    first = jnp.sum(scaled, -1, keepdims=True) * (1 / D)
    second = jnp.sum(scaled * unit, -1, keepdims=True) * (1 / D)
    return rate * (scaled - first - unit * second)


def gelu_parts(value):
    area = 0.5 + 0.5 * lax.erf(value * 0.7071067811865476)
    bell = jnp.exp(-0.5 * value * value)
    return value * area, area + value * bell * 0.3989422804014327


def fold(values):
    return jnp.sum(values.reshape(-1, 8, values.shape[-1]), 0)


def halves_of(rows, low, keep):
    zero = jnp.zeros_like(rows)
    top = jnp.where(keep & low, rows, zero)
    bottom = jnp.where(keep & ~low, rows, zero)
    return jnp.concatenate([top, bottom], 0).astype(BF)


def masks():
    low = lax.broadcasted_iota(jnp.int32, (64, 128), 1) < 64
    keep = lax.broadcasted_iota(jnp.int32, (64, 128), 0) < SEQ
    return low, keep


def forward_kernel(first, *refs):
    x_in, *masters, vec = refs[:6]
    outs = list(refs[6:-6])
    p_img, a_img, mixed, middle, act, slope, sums, w_attn, w_out, w_up, w_down, x_out = outs[:12]
    proj, heads, normed, hidden, stream, totals = refs[-6:]
    if first:
        stream = outs[12]
    step = pl.program_id(0)

    @pl.when(step == 0)
    def _():
        totals[...] = jnp.zeros_like(totals)
        for low, master in zip((w_attn, w_out, w_up, w_down), masters):
            low[...] = master[...].astype(BF)
        for block in range(9):
            proj[block, RUN : RUN + 16, :] = jnp.zeros((16, 128), F32)
        for block in range(3):
            heads[block, REAL - 4 : RUN + 16, :] = jnp.zeros((RUN + 20 - REAL, 128), F32)

    if first:
        stream[0, REAL - 4 : RUN, :] = jnp.zeros((RUN + 4 - REAL, D), F32)
        for image in range(IMG):
            stream[0, SEQ * image : SEQ * (image + 1), :] = x_in[image].astype(F32)
    else:
        stream = x_in

    def norm_block(i, carry):
        rows = pl.ds(pl.multiple_of(i * 64, 64), 64)
        unit, _ = normalise(stream[0, rows, :])
        normed[rows, :] = (unit * vec[0:1, G1:B1] + vec[0:1, B1:BQ]).astype(BF)
        return carry

    lax.fori_loop(0, RUN // 64, norm_block, 0)

    for third in range(3):
        result = dot(normed[...], w_attn[0, :, D * third : D * (third + 1)])
        if third == 0:
            result = result + vec[0:1, BQ:BV]
        if third == 2:
            result = result + vec[0:1, BV:BO]
        for block in range(3):
            proj[3 * third + block, 0:RUN, :] = result[:, 128 * block : 128 * (block + 1)]

    low, keep = masks()
    keep_keys = keep[0:56]

    def attend(i, carry):
        items = [(i * TOGETHER + k, pair) for k in range(TOGETHER) for pair in range(3)]
        loaded = []
        for image, pair in items:
            at = pl.ds(image * SEQ, 64)
            query = proj[pair, at, :]
            key = jnp.where(keep, proj[3 + pair, at, :], 0.0).astype(BF)
            value = jnp.where(keep, proj[6 + pair, at, :], 0.0).astype(BF)
            p_img[image, pair] = jnp.where(keep, query, 0.0).astype(BF)
            p_img[image, 3 + pair] = key
            p_img[image, 6 + pair] = value
            loaded.append((key, halves_of(query * 0.125, low, keep), value))
        scores = [dot(key, spread, 1, 1)[0:56] for key, spread, _ in loaded]
        weights = []
        for (image, pair), score in zip(items, scores):
            score = jnp.where(keep_keys, score, -1e30)
            raised = jnp.exp(score - jnp.max(score, 0, keepdims=True))
            weight = raised * (1.0 / jnp.sum(raised, 0, keepdims=True))
            weight = jnp.concatenate([weight, jnp.zeros((8, 128), F32)], 0).astype(BF)
            a_img[image, pair] = weight
            weights.append(weight)
        results = [dot(weight, value, 0, 0) for weight, (_, _, value) in zip(weights, loaded)]
        for (image, pair), both in zip(items, results):
            one = jnp.where(low, both[0:64], both[64:128])
            heads[pair, pl.ds(image * SEQ, SEQ), :] = one[0:SEQ]
        return carry

    lax.fori_loop(0, IMG // TOGETHER, attend, 0)

    for block in range(3):
        mixed[0, :, 128 * block : 128 * (block + 1)] = heads[block, 0:RUN, :].astype(BF)

    def mlp(i, carry):
        base = pl.multiple_of(i * STEP_ROWS, STEP_ROWS)
        rows = pl.ds(base, STEP_ROWS)
        real = lax.broadcasted_iota(jnp.int32, (STEP_ROWS, D), 0) + base < REAL
        before = stream[0, rows, :]
        branch = dot(mixed[0, rows, :], w_out[0]) + vec[0:1, BO:G2]
        between = before + branch
        middle[0, rows, :] = between
        unit, _ = normalise(between)
        normed_two = (unit * vec[0:1, G2:B2] + vec[0:1, B2:BU]).astype(BF)
        totals[0:8, :] += fold(jnp.where(real, before * before, 0.0))
        totals[8:16, :] += fold(jnp.where(real, branch * branch, 0.0))
        hidden[...] = dot(normed_two, w_up[0])
        for row in range(0, STEP_ROWS, 32):
            for column in range(0, FF, 256):
                part = hidden[row : row + 32, column : column + 256]
                part = part + vec[0:1, BU + column : BU + column + 256]
                bent, tilt = gelu_parts(part)
                at = pl.ds(base + row, 32)
                act[0, at, column : column + 256] = bent.astype(BF)
                slope[0, at, column : column + 256] = tilt.astype(BF)
        tail = dot(act[0, rows, :], w_down[0]) + vec[0:1, BD : BD + D]
        totals[16:24, :] += fold(jnp.where(real, tail * tail, 0.0))
        after = middle[0, rows, :] + tail
        if first:
            x_out[0, rows, :] = after
        else:
            hidden_stream[rows, :] = after
        return carry

    hidden_stream = refs[-2] if not first else None
    lax.fori_loop(0, RUN // STEP_ROWS, mlp, 0)

    if not first:
        for image in range(IMG):
            x_out[image] = hidden_stream[SEQ * image : SEQ * (image + 1), :].astype(BF)

    @pl.when(step == CHUNKS - 1)
    def _():
        lane = lax.broadcasted_iota(jnp.int32, (1, 128), 1)
        row = jnp.zeros((1, 128), F32)
        for k in range(3):
            row = jnp.where(lane == SUMS_AT + k, jnp.sum(totals[8 * k : 8 * k + 8, :]), row)
        sums[...] = row


def chunked(*dims):
    return pl.BlockSpec((1,) + dims, lambda c: (c,) + (0,) * len(dims))


def imaged(*dims):
    return pl.BlockSpec((IMG,) + dims, lambda c: (c,) + (0,) * len(dims))


WEIGHT_SIZES = ((D, 3 * D), (D, D), (D, FF), (FF, D))


def weight_specs(layer):
    return [
        pl.BlockSpec((1,) + s, lambda c: (layer, 0, 0), pipeline_mode=pl.Buffered(1))
        for s in WEIGHT_SIZES
    ] + [pl.BlockSpec((1, 12 * D), lambda c: (0, 0))]


def whole(*dims):
    return pl.BlockSpec(dims, lambda c: (0,) * len(dims))


def shape(kind, *dims):
    return jax.ShapeDtypeStruct(dims, kind)


def forward(layer, x_in, masters, vector):
    first = layer == 0
    out_shape = [
        shape(BF, IMG * CHUNKS, 9, 64, 128),
        shape(BF, IMG * CHUNKS, 3, 64, 128),
        shape(BF, CHUNKS, RUN, D),
        shape(F32, CHUNKS, RUN, D),
        shape(BF, CHUNKS, RUN, FF),
        shape(BF, CHUNKS, RUN, FF),
        shape(F32, 1, 128),
    ]
    out_specs = [
        imaged(9, 64, 128),
        imaged(3, 64, 128),
        chunked(RUN, D),
        chunked(RUN, D),
        chunked(RUN, FF),
        chunked(RUN, FF),
        whole(1, 128),
    ]
    out_shape += [shape(BF, 1, *size) for size in WEIGHT_SIZES]
    out_specs += [whole(1, *size) for size in WEIGHT_SIZES]
    if first:
        out_shape += [shape(F32, CHUNKS, RUN, D)] * 2
        out_specs += [chunked(RUN, D)] * 2
    else:
        out_shape += [shape(BF, IMG * CHUNKS, SEQ, D)]
        out_specs += [imaged(SEQ, D)]
    return pl.pallas_call(
        lambda *refs: forward_kernel(first, *refs),
        grid=(CHUNKS,),
        out_shape=out_shape,
        in_specs=[imaged(SEQ, D) if first else chunked(RUN, D)] + weight_specs(layer),
        out_specs=out_specs,
        scratch_shapes=[
            pltpu.VMEM((9, RUN + 16, 128), F32),
            pltpu.VMEM((3, RUN + 16, 128), F32),
            pltpu.VMEM((RUN, D), BF),
            pltpu.VMEM((STEP_ROWS, FF), F32),
            pltpu.VMEM((RUN, D), F32),
            pltpu.VMEM((24, D), F32),
        ],
        compiler_params=pltpu.CompilerParams(vmem_limit_bytes=56 * 2**20),
        name=f"forward_{layer}",
    )(x_in, *masters, vector[layer : layer + 1])


def emit_packed(core, plan, keep, send):
    def emit(halves):
        @pl.loop(0, 16)
        def _(block):
            deep, high = block // 4, block % 4

            def target(k):
                if k < 4:
                    return halves[0].at[k, high, deep]
                return halves[1].at[high, k - 4, deep]

            for source, start, each, width in plan:
                height = 8 * each
                base = pl.multiple_of(block * height, 8)
                for column in range(width):
                    rows = source[pl.ds(base, height), column * 128 : (column + 1) * 128]
                    at = start + each * column
                    for k in range(8):
                        target(k)[at : at + each, :] = rows[each * k : each * (k + 1)]

    @pl.when(core == 0)
    def _():
        emit((keep, send))

    @pl.when(core == 1)
    def _():
        emit((send, keep))


def back_mlp(r, grad):
    vec = r["vec"]

    def block(i, carry):
        base = pl.multiple_of(i * STEP_ROWS, STEP_ROWS)
        rows = pl.ds(base, STEP_ROWS)
        here = grad[0, rows, :]
        r["acc_vec"][:, BD : BD + D] += fold(here)
        here_low = here.astype(BF)
        r["low_grad"][rows, :] = here_low
        r["d_act"][...] = dot(here_low, r["w_down"][0], 1, 1)
        for column in range(0, FF, 256):
            total = jnp.zeros((8, 256), F32)
            for row in range(0, STEP_ROWS, 32):
                at = pl.ds(base + row, 32)
                part = r["d_act"][row : row + 32, column : column + 256]
                part = part * r["slope"][0, at, column : column + 256].astype(F32)
                r["d_hidden"][at, column : column + 256] = part.astype(BF)
                total = total + fold(part)
            r["acc_vec"][:, BU + column : BU + column + 256] += total
        d_normed = dot(r["d_hidden"][rows, :], r["w_up"][0], 1, 1)
        unit, rate = normalise(r["middle"][0, rows, :])
        gain = vec[0:1, G2:B2]
        r["normed"][rows, :] = (unit * gain + vec[0:1, B2:BU]).astype(BF)
        r["acc_vec"][:, G2:B2] += fold(d_normed * unit)
        r["acc_vec"][:, B2:BU] += fold(d_normed)
        between = grad[0, rows, :] + norm_back(d_normed, unit, rate, gain)
        r["d_mid"][0, rows, :] = between
        return carry

    lax.fori_loop(0, RUN // STEP_ROWS, block, 0)
    r["acc_down"][...] += dot(r["act"][0], r["low_grad"][...], 0, 0)
    r["acc_up"][...] += dot(r["normed"][...], r["d_hidden"][...], 0, 0)


def back_attention(r, d_mid, store):
    vec = r["vec"]

    def branch(i, carry):
        rows = pl.ds(pl.multiple_of(i * STEP_ROWS, STEP_ROWS), STEP_ROWS)
        between = d_mid[0, rows, :]
        r["acc_vec"][:, BO:G2] += fold(between)
        between = between.astype(BF)
        r["d_branch"][rows, :] = between
        result = dot(between, r["w_out"][0], 1, 1)
        for block in range(3):
            r["d_heads"][block, rows, :] = result[:, 128 * block : 128 * (block + 1)]
        return carry

    lax.fori_loop(0, RUN // STEP_ROWS, branch, 0)
    r["acc_out"][...] += dot(r["mixed"][0], r["d_branch"][...], 0, 0)
    low, keep = masks()
    p_img, a_img, d_heads, d_proj = r["p_img"], r["a_img"], r["d_heads"], r["d_proj"]

    def attend(i, carry):
        items = [(i * TOGETHER_BACK + k, pair) for k in range(TOGETHER_BACK) for pair in range(3)]
        loaded = []
        for image, pair in items:
            rows = d_heads[pair, pl.ds(image * SEQ, 64), :]
            spread = halves_of(p_img[image, pair].astype(F32) * 0.125, low, keep)
            loaded.append((spread, halves_of(rows, low, keep)))
        d_weights = [
            dot(p_img[image, 6 + pair], d_spread, 1, 1)
            for (image, pair), (_, d_spread) in zip(items, loaded)
        ]
        d_values = [
            dot(a_img[image, pair], d_spread) for (image, pair), (_, d_spread) in zip(items, loaded)
        ]
        d_scores = []
        for (image, pair), d_weight in zip(items, d_weights):
            weight = a_img[image, pair].astype(F32)
            product = weight * d_weight
            d_scores.append((product - weight * jnp.sum(product, 0, keepdims=True)).astype(BF))
        d_keys = [dot(d_score, spread) for d_score, (spread, _) in zip(d_scores, loaded)]
        d_both = [
            dot(d_score, p_img[image, 3 + pair], 0, 0)
            for (image, pair), d_score in zip(items, d_scores)
        ]
        for (image, pair), d_key, both, d_value in zip(items, d_keys, d_both, d_values):
            d_query = jnp.where(low, both[0:64], both[64:128]) * 0.125
            at = pl.ds(image * SEQ, SEQ)
            d_proj[pair, at, :] = d_query[0:SEQ]
            d_proj[3 + pair, at, :] = d_key[0:SEQ]
            d_proj[6 + pair, at, :] = d_value[0:SEQ]
        return carry

    lax.fori_loop(0, IMG // TOGETHER_BACK, attend, 0)

    def tail(i, carry):
        rows = pl.ds(pl.multiple_of(i * STEP_ROWS, STEP_ROWS), STEP_ROWS)
        for block in range(9):
            part = d_proj[block, rows, :]
            r["d_low"][rows, 128 * block : 128 * (block + 1)] = part.astype(BF)
            if block < 3:
                r["acc_vec"][:, BQ + 128 * block : BQ + 128 * (block + 1)] += fold(part)
            if block >= 6:
                r["acc_vec"][:, BV + 128 * (block - 6) : BV + 128 * (block - 5)] += fold(part)
        d_normed = dot(r["d_low"][rows, :], r["w_attn"][0], 1, 1)
        unit, rate = normalise(r["stream"][0, rows, :])
        gain = vec[0:1, G1:B1]
        r["normed"][rows, :] = (unit * gain + vec[0:1, B1:BQ]).astype(BF)
        r["acc_vec"][:, G1:B1] += fold(d_normed * unit)
        r["acc_vec"][:, B1:BQ] += fold(d_normed)
        store(rows, d_mid[0, rows, :] + norm_back(d_normed, unit, rate, gain))
        return carry

    lax.fori_loop(0, RUN // STEP_ROWS, tail, 0)
    r["acc_attn"][...] += dot(r["normed"][...], r["d_low"][...], 0, 0)


def backward_kernel(names, last, with_mlp, with_attention, *refs):
    r = dict(zip(names, refs))
    step = pl.program_id(0)

    @pl.when(step == 0)
    def _():
        for name in ("acc_attn", "acc_out", "acc_up", "acc_down", "acc_vec"):
            if name not in r:
                continue
            ref = r[name]

            @pl.loop(0, ref.shape[0] // 8)
            def _(i):
                rows = pl.ds(pl.multiple_of(i * 8, 8), 8)
                if name == "acc_vec" and not with_mlp:
                    ref[...] = r["vec_sums"][...]
                else:
                    ref[rows, :] = jnp.zeros((8, ref.shape[1]), F32)

        if with_attention:
            for block in range(3):
                r["d_heads"][block, RUN : RUN + 16, :] = jnp.zeros((16, 128), F32)
            for block in range(9):
                r["d_proj"][block, REAL - 4 : RUN + 16, :] = jnp.zeros((RUN + 20 - REAL, 128), F32)

    grad = r["grad_in"]
    if last:
        grad = r["grad"]
        grad[0, REAL - 4 : RUN, :] = jnp.zeros((RUN + 4 - REAL, D), F32)
        for image in range(IMG):
            grad[0, SEQ * image : SEQ * (image + 1), :] = r["grad_in"][image].astype(F32)
    plan = []
    if with_mlp:
        back_mlp(r, grad)
        plan += [(r["acc_up"], UP_AT, 3, 12), (r["acc_down"], DOWN_AT, 12, 3)]
    if with_attention:
        shift = 0 if with_mlp else QKV_AT
        plan += [(r["acc_attn"], QKV_AT - shift, 3, 9), (r["acc_out"], PROJ_AT - shift, 3, 3)]
        plan += [(r["small"], SMALL_AT - shift, 1, 1)]
        middle = r["d_mid"] if with_mlp else grad
        result = r["grad_out"] if last else r["grad"]

        def store(rows, value):
            result[0, rows, :] = value

        back_attention(r, middle, store)
        if not last:
            for image in range(IMG):
                r["grad_out"][image] = result[0, SEQ * image : SEQ * (image + 1), :]

    @pl.when(step == CHUNKS - 1)
    def _():
        if with_attention:
            small = r["small"]
            total = jnp.sum(r["acc_vec"][...], 0, keepdims=True)
            small[...] = jnp.broadcast_to(r["sums"][...], (128, 128))
            for owner in range(128):
                small[owner : owner + 1, 0:36] = total[:, 36 * owner : 36 * (owner + 1)]
        else:
            r["vec_sums"][...] = r["acc_vec"][...]
        emit_packed(r["core"][0], plan, r["keep"], r["send"])


def backward(layer, last, with_mlp, with_attention, core, grad_in, vector, saved):
    rows = (72 if with_mlp else 0) + (40 if with_attention else 0)
    half = shape(F32, 4, 4, 4, rows, 128)
    half_spec = whole(4, 4, 4, rows, 128)
    specs = weight_specs(0)
    ins = {
        "core": (core, pl.BlockSpec(memory_space=pltpu.SMEM)),
        "grad_in": (grad_in, imaged(SEQ, D) if last else chunked(RUN, D)),
        "vec": (vector[layer : layer + 1], specs[4]),
    }
    stream_shape, stream_spec = shape(F32, CHUNKS, RUN, D), chunked(RUN, D)
    outs = {"keep": (half, half_spec), "send": (half, half_spec)}
    scratch = {
        "grad": pltpu.VMEM((1, RUN, D), F32),
        "normed": pltpu.VMEM((RUN, D), BF),
        "acc_vec": pltpu.VMEM((8, 12 * D), F32),
    }
    if with_mlp:
        ins["w_up"] = (saved["w_up"], specs[2])
        ins["w_down"] = (saved["w_down"], specs[3])
        ins["middle"] = (saved["middle"], chunked(RUN, D))
        ins["act"] = (saved["act"], chunked(RUN, FF))
        ins["slope"] = (saved["slope"], chunked(RUN, FF))
        scratch["low_grad"] = pltpu.VMEM((RUN, D), BF)
        scratch["d_act"] = pltpu.VMEM((STEP_ROWS, FF), F32)
        scratch["d_hidden"] = pltpu.VMEM((RUN, FF), BF)
        scratch["acc_up"] = pltpu.VMEM((D, FF), F32)
        scratch["acc_down"] = pltpu.VMEM((FF, D), F32)
        if with_attention:
            scratch["d_mid"] = pltpu.VMEM((1, RUN, D), F32)
        else:
            outs["d_mid"] = (stream_shape, stream_spec)
            outs["vec_sums"] = (shape(F32, 8, 12 * D), whole(8, 12 * D))
    if with_attention:
        ins["w_attn"] = (saved["w_attn"], specs[0])
        ins["w_out"] = (saved["w_out"], specs[1])
        ins["p_img"] = (saved["p_img"], imaged(9, 64, 128))
        ins["a_img"] = (saved["a_img"], imaged(3, 64, 128))
        ins["mixed"] = (saved["mixed"], chunked(RUN, D))
        ins["sums"] = (saved["sums"], whole(1, 128))
        ins["stream"] = (saved["stream"], chunked(RUN, D))
        if not with_mlp:
            ins["vec_sums"] = (saved["vec_sums"], whole(8, 12 * D))
        outs["grad_out"] = (
            (stream_shape, stream_spec)
            if last
            else (shape(F32, IMG * CHUNKS, SEQ, D), imaged(SEQ, D))
        )
        scratch["d_branch"] = pltpu.VMEM((RUN, D), BF)
        scratch["d_heads"] = pltpu.VMEM((3, RUN + 16, 128), F32)
        scratch["d_proj"] = pltpu.VMEM((9, RUN + 16, 128), F32)
        scratch["d_low"] = pltpu.VMEM((RUN, 3 * D), BF)
        scratch["acc_attn"] = pltpu.VMEM((D, 3 * D), F32)
        scratch["acc_out"] = pltpu.VMEM((D, D), F32)
        scratch["small"] = pltpu.VMEM((128, 128), F32)
    limit = 60 if with_mlp and with_attention else 44
    names = [*ins, *outs, *scratch]
    results = pl.pallas_call(
        lambda *refs: backward_kernel(names, last, with_mlp, with_attention, *refs),
        grid=(CHUNKS,),
        out_shape=[v[0] for v in outs.values()],
        in_specs=[v[1] for v in ins.values()],
        out_specs=[v[1] for v in outs.values()],
        scratch_shapes=list(scratch.values()),
        compiler_params=pltpu.CompilerParams(vmem_limit_bytes=limit * 2**20),
        name=f"backward_{layer}" + "m" * with_mlp + "a" * with_attention,
    )(*[v[0] for v in ins.values()])
    return dict(zip(outs, results))


def forward_saved(layer, x_in, masters, vector):
    names = ["p_img", "a_img", "mixed", "middle", "act", "slope", "sums"]
    names += ["w_attn", "w_out", "w_up", "w_down", "x_out", "stream"]
    saved = dict(zip(names, forward(layer, x_in, masters, vector)))
    saved.setdefault("stream", x_in)
    return saved


def local_step(core, tokens, grad_out, masters, vector, between=lambda packed: packed):
    zero = forward_saved(0, tokens, masters, vector)
    one = forward_saved(1, zero["x_out"], masters, vector)
    back_one = backward(1, True, True, True, core, grad_out, vector, one)
    packed_one = (back_one["keep"], back_one["send"])
    mlp = backward(0, False, True, False, core, back_one["grad_out"], vector, zero)
    zero["vec_sums"] = mlp["vec_sums"]
    d_mid, packed_one = lax.optimization_barrier((mlp["d_mid"], between(packed_one)))
    tail = backward(0, False, False, True, core, d_mid, vector, zero)
    packed_zero = [mlp["keep"], mlp["send"], tail["keep"], tail["send"]]
    return one["x_out"], tail["grad_out"], packed_zero, packed_one


def stage_position(stage):
    deep, high, core, across = place_of(lax.axis_index(GROUP_AXES))
    if stage == 2:
        return deep
    return jnp.where(core == stage, across, high)


def add_core_kernel(count, *refs):
    me = stage_position(0)
    outs = refs[2 * count :]
    for shift in range(4):
        at = (me + shift) % 4

        @pl.loop(0, 16)
        def _(i):
            row = 0
            for k in range(count):
                keep, got = refs[2 * k : 2 * k + 2]
                end = row + keep.shape[3]
                value = keep[at, i // 4, i % 4] + got[at, i // 4, i % 4]
                outs[shift][i // 4, i % 4, row:end] = value
                row = end


def add_ring_kernel(stage, count, *refs):
    values, outs = refs[: 4 * count], refs[4 * count :]
    if stage == 3:
        own, one, two, three = values
        outs[0][...] = (own[...] + one[...]) + (two[...] + three[...])
        return
    me = stage_position(stage)
    for shift in range(4):
        at = (me + shift) % 4
        if stage == 2:
            own, one, two, three = values
            outs[shift][...] = (own[at] + one[at]) + (two[at] + three[at])
        else:

            @pl.loop(0, 4)
            def _(i):
                for layer in range(2):
                    own, one, two, three = values[4 * layer : 4 * layer + 4]
                    outs[shift][i, layer] = (own[at, i] + one[at, i]) + (two[at, i] + three[at, i])


def call_add(kernel, values, out_dims, count, name):
    return pl.pallas_call(
        kernel,
        out_shape=[jax.ShapeDtypeStruct(out_dims + (ROWS, 128), jnp.float32)] * count,
        in_specs=[VMEM_WHOLE] * len(values),
        out_specs=[VMEM_WHOLE] * count,
        compiler_params=pltpu.CompilerParams(vmem_limit_bytes=32 * 2**20),
        name=name,
    )(*values)


def ring(stage, parts):
    got = [lax.ppermute(parts[s], GROUP_AXES, ring_pairs(stage, s)) for s in range(1, 4)]
    return [parts[0]] + got


def core_sums(packed, name):
    values = core_swap(packed)
    count = len(packed) // 2
    return call_add(lambda *a: add_core_kernel(count, *a), values, (4, 4), 4, name)


def core_swap(packed):
    values = []
    for keep, send in zip(packed[::2], packed[1::2]):
        values += [keep, lax.ppermute(send, GROUP_AXES, core_pairs())]
    return values


def start_one(packed):
    return core_sums(packed, "add_core_one")


def finish_sums(packed_zero, parts_one):
    parts_one = ring(0, parts_one)
    packed_zero[3], parts_one = lax.optimization_barrier((packed_zero[3], parts_one))
    parts_zero = ring(0, core_sums(packed_zero, "add_core_zero"))
    parts = parts_zero + parts_one
    parts = call_add(lambda *a: add_ring_kernel(1, 2, *a), parts, (4, 2), 4, "add_first")
    parts = ring(1, parts)
    parts = call_add(lambda *a: add_ring_kernel(2, 1, *a), parts, (2,), 4, "add_second")
    parts = ring(2, parts)
    return call_add(lambda *a: add_ring_kernel(3, 1, *a), parts, (2,), 1, "add_third")[0]


def adam_step(gradient, moment_one, moment_two, weight, rate):
    moment_one = beta_one * moment_one + (1 - beta_one) * gradient
    moment_two = beta_two * moment_two + (1 - beta_two) * gradient * gradient
    fix_one = 1 - beta_one**STEP
    fix_two = 1 - beta_two**STEP
    update = (
        moment_one / fix_one / (jnp.sqrt(moment_two / fix_two) + adam_eps) + decay_rate * weight
    )
    return (moment_one, moment_two, weight - rate * update)


def finish_kernel(*refs):
    own, other = ([ref.at[k] for k in range(2)] for ref in refs[:2])
    weights, firsts, seconds, outers = (refs[2 + 5 * k : 7 + 5 * k] for k in range(4))
    outs = refs[22:]
    new_firsts, new_seconds, changes, new_outers, finals, copies = (
        outs[5 * k : 5 * k + 5] for k in range(6)
    )
    rms = outs[30]

    def gathered(refs, kind, row):
        if kind == 4:
            return jnp.concatenate([ref[SMALL_AT : SMALL_AT + 1, 0:36] for ref in refs], 0)
        start, rows, width = (
            (QKV_AT, 3, 9),
            (PROJ_AT, 3, 3),
            (UP_AT, 3, 12),
            (DOWN_AT, 12, 3),
        )[kind]
        lines = [start + rows * c + row for c in range(width)]
        return jnp.concatenate(
            [
                jnp.concatenate([ref[line : line + 1, :] for ref in refs], 0)
                for line in lines
            ],
            1,
        )

    for kind in range(5):
        rate = rates()[kind]
        for row in range(1 if kind == 4 else weights[kind].shape[0]):
            at = slice(None) if kind == 4 else row
            weight = weights[kind][at]
            moments = (firsts[kind][at], seconds[kind][at])
            one, two, updated = adam_step(gathered(own, kind, row), *moments, weight, rate)
            updated_other = adam_step(gathered(other, kind, row), *moments, weight, rate)[2]
            change = ((weight - updated) + (weight - updated_other)) / 2
            outer = outer_decay * outers[kind][at] + change
            final = weight - outer_rate * (change + outer_decay * outer)
            new_firsts[kind][at] = one
            new_seconds[kind][at] = two
            changes[kind][at] = change
            new_outers[kind][at] = outer
            finals[kind][at] = final
            copies[kind][at] = final.astype(jnp.bfloat16)
    for layer in range(2):
        totals = [
            ref[SMALL_AT : SMALL_AT + 1, SUMS_AT : SUMS_AT + 3] for ref in (own[layer], other[layer])
        ]
        rms[layer : layer + 1, :] = jnp.sqrt((totals[0] + totals[1]) / ENTRIES)


ENTRIES = 98304000


def rows_first(value):
    return value if value.ndim == 2 else jnp.swapaxes(value, 0, 1)


def finish(own, other, weights, firsts, seconds, outers):
    given = [rows_first(v) for v in (*weights, *firsts, *seconds, *outers)]
    full = [jax.ShapeDtypeStruct(v.shape, jnp.float32) for v in given[:5]]
    low = [jax.ShapeDtypeStruct(v.shape, jnp.bfloat16) for v in given[:5]]
    results = pl.pallas_call(
        finish_kernel,
        out_shape=full * 5 + low + [jax.ShapeDtypeStruct((2, 3), jnp.float32)],
        in_specs=[VMEM_WHOLE] * 22,
        out_specs=[VMEM_WHOLE] * 31,
        name="finish",
    )(own, other, *given)
    results = [rows_first(v) for v in results[:30]] + [results[30]]
    return [v[None] for v in results[:10]] + results[10:]

def body(
    tokens,
    grad_out,
    weight_qkv,
    weight_proj,
    weight_up,
    weight_down,
    weight_vector,
    old_first_qkv,
    old_first_proj,
    old_first_up,
    old_first_down,
    old_first_vector,
    old_second_qkv,
    old_second_proj,
    old_second_up,
    old_second_down,
    old_second_vector,
    old_outer_qkv,
    old_outer_proj,
    old_outer_up,
    old_outer_down,
    old_outer_vector,
):
    masters = (weight_qkv, weight_proj, weight_up, weight_down, weight_vector)
    old_firsts = (old_first_qkv, old_first_proj, old_first_up, old_first_down, old_first_vector)
    old_seconds = (
        old_second_qkv,
        old_second_proj,
        old_second_up,
        old_second_down,
        old_second_vector,
    )
    old_outers = (old_outer_qkv, old_outer_proj, old_outer_up, old_outer_down, old_outer_vector)
    owner_index = lax.axis_index(GROUP_AXES)
    core = jnp.reshape(owner_index // 4 % 2, (1,)).astype(jnp.int32)
    block_out, grad_tokens, packed_zero, parts_one = local_step(
        core, tokens, grad_out, masters[:4], weight_vector, start_one
    )
    shares = []
    for kind_index in range(5):
        share_rows = old_firsts[kind_index].shape[1]
        shares.append(
            lax.dynamic_slice_in_dim(masters[kind_index], owner_index * share_rows, share_rows, 1)
        )
    own = finish_sums(packed_zero, parts_one)
    other = lax.ppermute(own, "grp", [(0, 1), (1, 0)])
    results = finish(own, other, shares, old_firsts, old_seconds, old_outers)
    return (block_out, grad_tokens, *results)


def solution(mesh):
    placed = (
        P(("grp", "wide", "narrow"), None, None),
        P(("grp", "wide", "narrow"), None, None),
        P(),
        P(),
        P(),
        P(),
        P(),
        P(None, ("wide", "narrow"), None),
        P(None, ("wide", "narrow"), None),
        P(None, ("wide", "narrow"), None),
        P(None, ("wide", "narrow"), None),
        P(None, ("wide", "narrow")),
        P(None, ("wide", "narrow"), None),
        P(None, ("wide", "narrow"), None),
        P(None, ("wide", "narrow"), None),
        P(None, ("wide", "narrow"), None),
        P(None, ("wide", "narrow")),
        P(None, ("wide", "narrow"), None),
        P(None, ("wide", "narrow"), None),
        P(None, ("wide", "narrow"), None),
        P(None, ("wide", "narrow"), None),
        P(None, ("wide", "narrow")),
    )
    return jax.shard_map(
        body,
        mesh=mesh,
        in_specs=placed,
        out_specs=(
            P(("grp", "wide", "narrow"), None, None),
            P(("grp", "wide", "narrow"), None, None),
            P("grp", None, ("wide", "narrow"), None),
            P("grp", None, ("wide", "narrow"), None),
            P("grp", None, ("wide", "narrow"), None),
            P("grp", None, ("wide", "narrow"), None),
            P("grp", None, ("wide", "narrow")),
            P("grp", None, ("wide", "narrow"), None),
            P("grp", None, ("wide", "narrow"), None),
            P("grp", None, ("wide", "narrow"), None),
            P("grp", None, ("wide", "narrow"), None),
            P("grp", None, ("wide", "narrow")),
            P(None, ("wide", "narrow"), None),
            P(None, ("wide", "narrow"), None),
            P(None, ("wide", "narrow"), None),
            P(None, ("wide", "narrow"), None),
            P(None, ("wide", "narrow")),
            P(None, ("wide", "narrow"), None),
            P(None, ("wide", "narrow"), None),
            P(None, ("wide", "narrow"), None),
            P(None, ("wide", "narrow"), None),
            P(None, ("wide", "narrow")),
            P(None, ("wide", "narrow"), None),
            P(None, ("wide", "narrow"), None),
            P(None, ("wide", "narrow"), None),
            P(None, ("wide", "narrow"), None),
            P(None, ("wide", "narrow")),
            P(None, ("wide", "narrow"), None),
            P(None, ("wide", "narrow"), None),
            P(None, ("wide", "narrow"), None),
            P(None, ("wide", "narrow"), None),
            P(None, ("wide", "narrow")),
            P(),
        ),
        check_vma=False,
    )
```

profile of v0, /device:TPU:1, one launch (start us, length us, event | category | flops | bytes accessed | tf_op | source)
XLA Modules:
  0.0 192.0 jit_solution(938872508276904574)
XLA Ops:
  0.7 1.5 fusion
  2.2 22.2 %forward_0.1 = (bf16[20,9,64,128]{3,2,1,0:T(8,128)(2,1)}, bf16[20,3,64,128]{3,2,1,0:T(8,128)(2,1)}, bf16[2,512,384]{2,1,0:T(8,128)(2,1)}, f32[2,512,384]{2,1,0:T...) custom-call(bf16[20,50,384]{2,1,0:T(8,128)(2,1)} %refs_0_.1, ...), custom_call_target="tpu_custom_call" | custom-call | tf_op jit(solution)/shard_map/forward_0/pallas_call | solution.py:293
  24.4 22.0 %forward_1.1 = (bf16[20,9,64,128]{3,2,1,0:T(8,128)(2,1)}, bf16[20,3,64,128]{3,2,1,0:T(8,128)(2,1)}, bf16[2,512,384]{2,1,0:T(8,128)(2,1)}, f32[2,512,384]{2,1,0:T...) custom-call(f32[2,512,384]{2,1,0:T(8,128)} %get-tuple-element.125.re, ...), custom_call_target="tpu_custom_call" | custom-call | tf_op jit(solution)/shard_map/forward_1/pallas_call | solution.py:293
  46.4 0.0 copy-start.11
  46.4 26.1 %backward_1ma.1 = (f32[4,4,4,112,128]{4,3,2,1,0:T(8,128)}, f32[4,4,4,112,128]{4,3,2,1,0:T(8,128)}, f32[2,512,384]{2,1,0:T(8,128)}) custom-call(s32[1]{0:T(128)} %bitcast.refs_0_, bf16[20,50,384]{2,1,0:T(8,128)(2,1)} %refs_1_.5, f32[1,4608]{1,0:T(1,128)} %get-tuple-element.217.refs_5_.refs_2_, bf16[1,384,1536]{2,1,0:T(8,128)(2,1)} %get-tuple-element.127.refs_3_, ...), custom_call_target="tpu_custom_call" | custom-call | tf_op jit(solution)/shard_map/backward_1ma/pallas_call | solution.py:571
  72.6 3.3 %collective-permute-start = (f32[4,4,4,112,128]{4,3,2,1,0:T(8,128)}, f32[4,4,4,112,128]{4,3,2,1,0:T(8,128)S(1)}, u32[]{:S(2)}, u32[]{:S(2)}) collective-permute-start(f32[4,4,4,112,128]{4,3,2,1,0:T(8,128)} %get-tuple-element.146), channel_id=1, source_target_pairs={{0,4},{1,5},{2,6},{3,7},{4,0},{5,1},{6,2},{7,3},{8,12},{9,13},{10,... | collective-permute-start | bytes 11010056 | tf_op jit(solution)/shard_map/ppermute | solution.py:675
  75.9 1.4 copy-done.2
  77.3 1.3 copy-done.4
  78.6 1.3 copy-done.5
  79.8 12.4 %backward_0m.1 = (f32[4,4,4,72,128]{4,3,2,1,0:T(8,128)S(1)}, f32[4,4,4,72,128]{4,3,2,1,0:T(8,128)}, f32[2,512,384]{2,1,0:T(8,128)S(1)}, f32[8,4608]{1,0:T(8,128)S(1)}) custom-call(s32[1]{0:T(128)} %bitcast.refs_0_, f32[2,512,384]{2,1,0:T(8,128)S(1)} %copy-done.2, f32[1,4608]{1,0:T(1,128)S(1)} %copy-done.11, bf16[1,384,1536]{2,1,0:T(8,128)(2,1)S(1)} %copy-done.4, ...), custom_call_target="tpu_custom_call" | custom-call | tf_op jit(solution)/shard_map/backward_0m/pallas_call | solution.py:571
  92.3 0.0 collective-permute-start.1
  92.4 2.7 %add_core_one.1 = (f32[4,4,112,128]{3,2,1,0:T(8,128)S(1)}, f32[4,4,112,128]{3,2,1,0:T(8,128)}, f32[4,4,112,128]{3,2,1,0:T(8,128)}, f32[4,4,112,128]{3,2,1,0:T(8,128)}) custom-call(f32[4,4,4,112,128]{4,3,2,1,0:T(8,128)S(1)} %copy-done, f32[4,4,4,112,128]{4,3,2,1,0:T(8,128)S(1)} %collective-permute-done.a_1_), custom_call_target="tpu_custom_call" | custom-call | tf_op jit(solution)/shard_map/add_core_one/pallas_call | solution.py:651
  95.1 2.2 %collective-permute-start.3 = (f32[4,4,112,128]{3,2,1,0:T(8,128)}, f32[4,4,112,128]{3,2,1,0:T(8,128)S(1)}, u32[]{:S(2)}, u32[]{:S(2)}) collective-permute-start(f32[4,4,112,128]{3,2,1,0:T(8,128)} %get-tuple-element.167), channel_id=1, source_target_pairs={{0,2},{1,3},{2,0},{3,1},{4,20},{5,21},{6,22},{7,23},{8,10},{9,11},... | collective-permute-start | bytes 2752520 | tf_op jit(solution)/shard_map/ppermute | solution.py:662
  97.3 1.1 collective-permute-start.4
  98.4 11.8 %backward_0a.1 = (f32[4,4,4,40,128]{4,3,2,1,0:T(8,128)S(1)}, f32[4,4,4,40,128]{4,3,2,1,0:T(8,128)S(1)}, f32[20,50,384]{2,1,0:T(8,128)}) custom-call(s32[1]{0:T(128)} %bitcast.refs_0_, f32[2,512,384]{2,1,0:T(8,128)S(1)} %get-tuple-element.151.refs_1_, f32[1,4608]{1,0:T(1,128)S(1)} %copy-done.11, bf16[1,384,1152]{2,1,0:T(8,128)(2,1)S(1)} %copy-done.7, ...), custom_call_target="tpu_custom_call" | custom-call | tf_op jit(solution)/shard_map/backward_0a/pallas_call | solution.py:571
  110.1 8.8 %collective-permute-done.2.a_5_ = f32[4,4,112,128]{3,2,1,0:T(8,128)S(1)} collective-permute-done((f32[4,4,112,128]{3,2,1,0:T(8,128)}, f32[4,4,112,128]{3,2,1,0:T(8,128)S(1)}, u32[]{:S(2)}, u32[]{:S(2)}) %collective-permute-start.2) | collective-permute-done | bytes 917536 | tf_op jit(solution)/shard_map/ppermute | solution.py:662
  118.9 0.6 collective-permute-done.4.a_7_
  119.5 1.6 collective-permute-start.5
  121.1 2.7 %collective-permute-done.5.a_3_ = f32[4,4,4,40,128]{4,3,2,1,0:T(8,128)S(1)} collective-permute-done((f32[4,4,4,40,128]{4,3,2,1,0:T(8,128)S(1)}, f32[4,4,4,40,128]{4,3,2,1,0:T(8,128)S(1)}, u32[]{:S(2)}, u32[]{:S(2)}) %collective-permute-start.5) | collective-permute-done | bytes 1310752 | tf_op jit(solution)/shard_map/ppermute | solution.py:675
  123.8 2.7 %add_core_zero.1 = (f32[4,4,112,128]{3,2,1,0:T(8,128)S(1)}, f32[4,4,112,128]{3,2,1,0:T(8,128)S(1)}, f32[4,4,112,128]{3,2,1,0:T(8,128)S(1)}, f32[4,4,112,128]{3,2,1,0:T(8,128)S(1)}) custom-call(f32[4,4,4,72,128]{4,3,2,1,0:T(8,128)S(1)} %get-tuple-element.161.a_0_, f32[4,4,4,72,128]{4,3,2,1,0:T(8,128)} %collective-permute-done.1.a_1_, ...), custom_call_target="tpu_custom_call" | custom-call | tf_op jit(solution)/shard_map/add_core_zero/pallas_call | solution.py:651
  126.5 0.1 collective-permute-start.6
  126.6 2.3 %collective-permute-start.7 = (f32[4,4,112,128]{3,2,1,0:T(8,128)S(1)}, f32[4,4,112,128]{3,2,1,0:T(8,128)S(1)}, u32[]{:S(2)}, u32[]{:S(2)}) collective-permute-start(f32[4,4,112,128]{3,2,1,0:T(8,128)S(1)} %get-tuple-element.172), channel_id=1, source_target_pairs={{0,2},{1,3},{2,0},{3,1},{4,20},{5,21},{6,22},{7,23},{8,10},{9,11},... | collective-permute-start | bytes 2752520 | tf_op jit(solution)/shard_map/ppermute | solution.py:662
  128.8 1.1 collective-permute-start.8
  129.9 20.2 %collective-permute-done.6.a_1_ = f32[4,4,112,128]{3,2,1,0:T(8,128)S(1)} collective-permute-done((f32[4,4,112,128]{3,2,1,0:T(8,128)S(1)}, f32[4,4,112,128]{3,2,1,0:T(8,128)S(1)}, u32[]{:S(2)}, u32[]{:S(2)}) %collective-permute-start.6) | collective-permute-done | bytes 917536 | tf_op jit(solution)/shard_map/ppermute | solution.py:662
  150.1 0.6 collective-permute-done.8.a_3_
  150.8 1.4 add_first.1
  152.2 0.4 collective-permute-start.9
  152.5 3.2 %collective-permute-start.10 = (f32[4,2,112,128]{3,2,1,0:T(8,128)}, f32[4,2,112,128]{3,2,1,0:T(8,128)S(1)}, u32[]{:S(2)}, u32[]{:S(2)}) collective-permute-start(f32[4,2,112,128]{3,2,1,0:T(8,128)} %get-tuple-element.180), channel_id=1, source_target_pairs={{0,16},{1,17},{2,18},{3,19},{4,6},{5,7},{6,4},{7,5},{8,24},{9,25},... | collective-permute-start | bytes 1376264 | tf_op jit(solution)/shard_map/ppermute | solution.py:662
  155.7 0.9 constant_dynamic-slice_fusion.4
  156.6 4.6 %collective-permute-done.9.a_1_ = f32[4,2,112,128]{3,2,1,0:T(8,128)S(1)} collective-permute-done((f32[4,2,112,128]{3,2,1,0:T(8,128)}, f32[4,2,112,128]{3,2,1,0:T(8,128)S(1)}, u32[]{:S(2)}, u32[]{:S(2)}) %collective-permute-start.9) | collective-permute-done | bytes 458784 | tf_op jit(solution)/shard_map/ppermute | solution.py:662
  161.2 5.8 %collective-permute-done.10.a_2_ = f32[4,2,112,128]{3,2,1,0:T(8,128)S(1)} collective-permute-done((f32[4,2,112,128]{3,2,1,0:T(8,128)}, f32[4,2,112,128]{3,2,1,0:T(8,128)S(1)}, u32[]{:S(2)}, u32[]{:S(2)}) %collective-permute-start.10) | collective-permute-done | bytes 458784 | tf_op jit(solution)/shard_map/ppermute | solution.py:662
  167.0 0.1 add_second.1
  167.1 1.8 collective-permute-start.12
  168.9 5.1 %collective-permute-start.13 = (f32[2,112,128]{2,1,0:T(8,128)S(1)}, f32[2,112,128]{2,1,0:T(8,128)S(1)}, u32[]{:S(2)}, u32[]{:S(2)}) collective-permute-start(f32[2,112,128]{2,1,0:T(8,128)S(1)} %get-tuple-element.184), channel_id=1, source_target_pairs={{0,64},{1,65},{2,66},{3,67},{4,68},{5,69},{6,70},{7,71},{8,72},{9,... | collective-permute-start | bytes 344072 | tf_op jit(solution)/shard_map/ppermute | solution.py:662
  174.0 2.4 %collective-permute-start.14 = (f32[2,112,128]{2,1,0:T(8,128)S(1)}, f32[2,112,128]{2,1,0:T(8,128)S(1)}, u32[]{:S(2)}, u32[]{:S(2)}) collective-permute-start(f32[2,112,128]{2,1,0:T(8,128)S(1)} %get-tuple-element.185), channel_id=1, source_target_pairs={{0,96},{1,97},{2,98},{3,99},{4,100},{5,101},{6,102},{7,103},{8,104... | collective-permute-start | bytes 344072 | tf_op jit(solution)/shard_map/ppermute | solution.py:662
  176.4 0.9 constant_dynamic-slice_fusion.2
  177.3 0.9 constant_dynamic-slice_fusion.1
  178.2 2.2 %collective-permute-done.13.a_2_ = f32[2,112,128]{2,1,0:T(8,128)S(1)} collective-permute-done((f32[2,112,128]{2,1,0:T(8,128)S(1)}, f32[2,112,128]{2,1,0:T(8,128)S(1)}, u32[]{:S(2)}, u32[]{:S(2)}) %collective-permute-start.13) | collective-permute-done | bytes 114720 | tf_op jit(solution)/shard_map/ppermute | solution.py:662
  180.5 3.6 %collective-permute-done.14.a_3_ = f32[2,112,128]{2,1,0:T(8,128)S(1)} collective-permute-done((f32[2,112,128]{2,1,0:T(8,128)S(1)}, f32[2,112,128]{2,1,0:T(8,128)S(1)}, u32[]{:S(2)}, u32[]{:S(2)}) %collective-permute-start.14) | collective-permute-done | bytes 114720 | tf_op jit(solution)/shard_map/ppermute | solution.py:662
  184.1 0.1 collective-permute-start.15
  184.2 0.8 constant_dynamic-slice_fusion.3
  185.0 0.6 copy.69
  185.7 0.6 copy.70
  186.3 0.6 copy.68
  186.9 0.6 copy.67
  187.5 1.3 constant_dynamic-slice_fusion.refs_6_
  188.9 0.6 copy-done.13
  189.5 2.3 %finish.1 = (f32[3,2,1152]{2,1,0:T(2,128)}, f32[3,2,384]{2,1,0:T(2,128)}, f32[3,2,1536]{2,1,0:T(2,128)}, f32[12,2,384]{2,1,0:T(2,128)}, f32[2,36]{1,0:T(2,128)},...) custom-call(f32[2,112,128]{2,1,0:T(8,128)} %copy-done.9, ...), custom_call_target="tpu_custom_call" | custom-call | tf_op jit(solution)/shard_map/finish/pallas_call | solution.py:768
  (33 shorter events, 0.1 us)
Async XLA Ops:
  46.4 29.5 %copy-start.1 = (f32[2,512,384]{2,1,0:T(8,128)S(1)}, f32[2,512,384]{2,1,0:T(8,128)}, u32[]{:S(2)}) copy-start(f32[2,512,384]{2,1,0:T(8,128)} %get-tuple-element.141.refs_5_) | copy-start | bytes 4718596
  46.4 29.5 %copy-start.11 = (f32[1,4608]{1,0:T(1,128)S(1)}, f32[1,4608]{1,0:T(1,128)}, u32[]{:S(2)}) copy-start(f32[1,4608]{1,0:T(1,128)} %get-tuple-element.218.refs_5_.refs_2_) | copy-start | bytes 55300
  72.6 19.8 %collective-permute-start = (f32[4,4,4,112,128]{4,3,2,1,0:T(8,128)}, f32[4,4,4,112,128]{4,3,2,1,0:T(8,128)S(1)}, u32[]{:S(2)}, u32[]{:S(2)}) collective-permute-start(f32[4,4,4,112,128]{4,3,2,1,0:T(8,128)} %get-tuple-element.146), channel_id=1, source_target_pairs={{0,4},{1,5},{2,6},{3,7},{4,0},{5,1},{6,2},{7,3},{8,12},{9,13},{10,... | collective-permute-start | bytes 11010056 | tf_op jit(solution)/shard_map/ppermute | solution.py:675
  75.9 1.4 copy-start.2
  77.3 1.3 copy-start.4
  78.6 1.3 copy-start.5
  79.8 12.5 %copy-start = (f32[4,4,4,112,128]{4,3,2,1,0:T(8,128)S(1)}, f32[4,4,4,112,128]{4,3,2,1,0:T(8,128)}, u32[]{:S(2)}) copy-start(f32[4,4,4,112,128]{4,3,2,1,0:T(8,128)} %get-tuple-element.145.a_0_) | copy-start | bytes 11010052
  92.3 28.8 %collective-permute-start.1 = (f32[4,4,4,72,128]{4,3,2,1,0:T(8,128)}, f32[4,4,4,72,128]{4,3,2,1,0:T(8,128)}, u32[]{:S(2)}, u32[]{:S(2)}) collective-permute-start(f32[4,4,4,72,128]{4,3,2,1,0:T(8,128)} %get-tuple-element.162), channel_id=1, source_target_pairs={{0,4},{1,5},{2,6},{3,7},{4,0},{5,1},{6,2},{7,3},{8,12},{9,13},{10,... | collective-permute-start | bytes 7077896 | tf_op jit(solution)/shard_map/ppermute | solution.py:675
  92.3 6.0 %copy-start.3 = (f32[2,512,384]{2,1,0:T(8,128)S(1)}, f32[2,512,384]{2,1,0:T(8,128)}, u32[]{:S(2)}) copy-start(f32[2,512,384]{2,1,0:T(8,128)} %get-tuple-element.158.refs_9_) | copy-start | bytes 4718596
  92.3 6.0 %copy-start.6 = (bf16[20,3,64,128]{3,2,1,0:T(8,128)(2,1)S(1)}, bf16[20,3,64,128]{3,2,1,0:T(8,128)(2,1)}, u32[]{:S(2)}) copy-start(bf16[20,3,64,128]{3,2,1,0:T(8,128)(2,1)} %get-tuple-element.155.refs_6_) | copy-start | bytes 2949124
  92.3 6.0 %copy-start.7 = (bf16[1,384,1152]{2,1,0:T(8,128)(2,1)S(1)}, bf16[1,384,1152]{2,1,0:T(8,128)(2,1)}, u32[]{:S(2)}) copy-start(bf16[1,384,1152]{2,1,0:T(8,128)(2,1)} %get-tuple-element.152.refs_3_) | copy-start | bytes 2654212
  92.3 6.0 %copy-start.8 = (bf16[2,512,384]{2,1,0:T(8,128)(2,1)S(1)}, bf16[2,512,384]{2,1,0:T(8,128)(2,1)}, u32[]{:S(2)}) copy-start(bf16[2,512,384]{2,1,0:T(8,128)(2,1)} %get-tuple-element.156.refs_7_) | copy-start | bytes 2359300
  92.3 6.0 %copy-start.10 = (bf16[1,384,384]{2,1,0:T(8,128)(2,1)S(1)}, bf16[1,384,384]{2,1,0:T(8,128)(2,1)}, u32[]{:S(2)}) copy-start(bf16[1,384,384]{2,1,0:T(8,128)(2,1)} %get-tuple-element.153.refs_4_) | copy-start | bytes 884740
  92.4 6.0 %copy-start.12 = (f32[1,128]{1,0:T(1,128)S(1)}, f32[1,128]{1,0:T(1,128)}, u32[]{:S(2)}) copy-start(f32[1,128]{1,0:T(1,128)} %get-tuple-element.157.refs_8_) | copy-start | bytes 1540
  95.1 23.8 %collective-permute-start.2 = (f32[4,4,112,128]{3,2,1,0:T(8,128)}, f32[4,4,112,128]{3,2,1,0:T(8,128)S(1)}, u32[]{:S(2)}, u32[]{:S(2)}) collective-permute-start(f32[4,4,112,128]{3,2,1,0:T(8,128)} %get-tuple-element.166), channel_id=1, source_target_pairs={{0,1},{1,2},{2,3},{3,0},{4,12},{5,13},{6,14},{7,15},{8,9},{9,10},{... | collective-permute-start | bytes 2752520 | tf_op jit(solution)/shard_map/ppermute | solution.py:662
  95.1 23.8 %collective-permute-start.3 = (f32[4,4,112,128]{3,2,1,0:T(8,128)}, f32[4,4,112,128]{3,2,1,0:T(8,128)S(1)}, u32[]{:S(2)}, u32[]{:S(2)}) collective-permute-start(f32[4,4,112,128]{3,2,1,0:T(8,128)} %get-tuple-element.167), channel_id=1, source_target_pairs={{0,2},{1,3},{2,0},{3,1},{4,20},{5,21},{6,22},{7,23},{8,10},{9,11},... | collective-permute-start | bytes 2752520 | tf_op jit(solution)/shard_map/ppermute | solution.py:662
  97.3 22.2 %collective-permute-start.4 = (f32[4,4,112,128]{3,2,1,0:T(8,128)}, f32[4,4,112,128]{3,2,1,0:T(8,128)S(1)}, u32[]{:S(2)}, u32[]{:S(2)}) collective-permute-start(f32[4,4,112,128]{3,2,1,0:T(8,128)} %get-tuple-element.168), channel_id=1, source_target_pairs={{0,3},{1,0},{2,1},{3,2},{4,28},{5,29},{6,30},{7,31},{8,11},{9,8},{... | collective-permute-start | bytes 2752520 | tf_op jit(solution)/shard_map/ppermute | solution.py:662
  119.5 4.3 %collective-permute-start.5 = (f32[4,4,4,40,128]{4,3,2,1,0:T(8,128)S(1)}, f32[4,4,4,40,128]{4,3,2,1,0:T(8,128)S(1)}, u32[]{:S(2)}, u32[]{:S(2)}) collective-permute-start(f32[4,4,4,40,128]{4,3,2,1,0:T(8,128)S(1)} %get-tuple-element.169), channel_id=1, source_target_pairs={{0,4},{1,5},{2,6},{3,7},{4,0},{5,1},{6,2},{7,3},{8,12},{9,13},{10,... | collective-permute-start | bytes 3932168 | tf_op jit(solution)/shard_map/ppermute | solution.py:675
  126.5 23.7 %collective-permute-start.6 = (f32[4,4,112,128]{3,2,1,0:T(8,128)S(1)}, f32[4,4,112,128]{3,2,1,0:T(8,128)S(1)}, u32[]{:S(2)}, u32[]{:S(2)}) collective-permute-start(f32[4,4,112,128]{3,2,1,0:T(8,128)S(1)} %get-tuple-element.171), channel_id=1, source_target_pairs={{0,1},{1,2},{2,3},{3,0},{4,12},{5,13},{6,14},{7,15},{8,9},{9,10},{... | collective-permute-start | bytes 2752520 | tf_op jit(solution)/shard_map/ppermute | solution.py:662
  126.6 23.6 %collective-permute-start.7 = (f32[4,4,112,128]{3,2,1,0:T(8,128)S(1)}, f32[4,4,112,128]{3,2,1,0:T(8,128)S(1)}, u32[]{:S(2)}, u32[]{:S(2)}) collective-permute-start(f32[4,4,112,128]{3,2,1,0:T(8,128)S(1)} %get-tuple-element.172), channel_id=1, source_target_pairs={{0,2},{1,3},{2,0},{3,1},{4,20},{5,21},{6,22},{7,23},{8,10},{9,11},... | collective-permute-start | bytes 2752520 | tf_op jit(solution)/shard_map/ppermute | solution.py:662
  128.8 21.9 %collective-permute-start.8 = (f32[4,4,112,128]{3,2,1,0:T(8,128)S(1)}, f32[4,4,112,128]{3,2,1,0:T(8,128)S(1)}, u32[]{:S(2)}, u32[]{:S(2)}) collective-permute-start(f32[4,4,112,128]{3,2,1,0:T(8,128)S(1)} %get-tuple-element.173), channel_id=1, source_target_pairs={{0,3},{1,0},{2,1},{3,2},{4,28},{5,29},{6,30},{7,31},{8,11},{9,8},{... | collective-permute-start | bytes 2752520 | tf_op jit(solution)/shard_map/ppermute | solution.py:662
  152.2 9.0 %collective-permute-start.9 = (f32[4,2,112,128]{3,2,1,0:T(8,128)}, f32[4,2,112,128]{3,2,1,0:T(8,128)S(1)}, u32[]{:S(2)}, u32[]{:S(2)}) collective-permute-start(f32[4,2,112,128]{3,2,1,0:T(8,128)} %get-tuple-element.179), channel_id=1, source_target_pairs={{0,8},{1,9},{2,10},{3,11},{4,5},{5,6},{6,7},{7,4},{8,16},{9,17},{1... | collective-permute-start | bytes 1376264 | tf_op jit(solution)/shard_map/ppermute | solution.py:662
  152.5 14.5 %collective-permute-start.10 = (f32[4,2,112,128]{3,2,1,0:T(8,128)}, f32[4,2,112,128]{3,2,1,0:T(8,128)S(1)}, u32[]{:S(2)}, u32[]{:S(2)}) collective-permute-start(f32[4,2,112,128]{3,2,1,0:T(8,128)} %get-tuple-element.180), channel_id=1, source_target_pairs={{0,16},{1,17},{2,18},{3,19},{4,6},{5,7},{6,4},{7,5},{8,24},{9,25},... | collective-permute-start | bytes 1376264 | tf_op jit(solution)/shard_map/ppermute | solution.py:662
  155.7 11.3 %collective-permute-start.11 = (f32[4,2,112,128]{3,2,1,0:T(8,128)S(1)}, f32[4,2,112,128]{3,2,1,0:T(8,128)S(1)}, u32[]{:S(2)}, u32[]{:S(2)}) collective-permute-start(f32[4,2,112,128]{3,2,1,0:T(8,128)S(1)} %get-tuple-element.181), channel_id=1, source_target_pairs={{0,24},{1,25},{2,26},{3,27},{4,7},{5,4},{6,5},{7,6},{8,0},{9,1},{1... | collective-permute-start | bytes 1376264 | tf_op jit(solution)/shard_map/ppermute | solution.py:662
  167.1 11.2 %collective-permute-start.12 = (f32[2,112,128]{2,1,0:T(8,128)S(1)}, f32[2,112,128]{2,1,0:T(8,128)S(1)}, u32[]{:S(2)}, u32[]{:S(2)}) collective-permute-start(f32[2,112,128]{2,1,0:T(8,128)S(1)} %get-tuple-element.183), channel_id=1, source_target_pairs={{0,32},{1,33},{2,34},{3,35},{4,36},{5,37},{6,38},{7,39},{8,40},{9,... | collective-permute-start | bytes 344072 | tf_op jit(solution)/shard_map/ppermute | solution.py:662
  168.9 11.6 %collective-permute-start.13 = (f32[2,112,128]{2,1,0:T(8,128)S(1)}, f32[2,112,128]{2,1,0:T(8,128)S(1)}, u32[]{:S(2)}, u32[]{:S(2)}) collective-permute-start(f32[2,112,128]{2,1,0:T(8,128)S(1)} %get-tuple-element.184), channel_id=1, source_target_pairs={{0,64},{1,65},{2,66},{3,67},{4,68},{5,69},{6,70},{7,71},{8,72},{9,... | collective-permute-start | bytes 344072 | tf_op jit(solution)/shard_map/ppermute | solution.py:662
  174.0 10.1 %collective-permute-start.14 = (f32[2,112,128]{2,1,0:T(8,128)S(1)}, f32[2,112,128]{2,1,0:T(8,128)S(1)}, u32[]{:S(2)}, u32[]{:S(2)}) collective-permute-start(f32[2,112,128]{2,1,0:T(8,128)S(1)} %get-tuple-element.185), channel_id=1, source_target_pairs={{0,96},{1,97},{2,98},{3,99},{4,100},{5,101},{6,102},{7,103},{8,104... | collective-permute-start | bytes 344072 | tf_op jit(solution)/shard_map/ppermute | solution.py:662
  184.1 4.8 %copy-start.9 = (f32[2,112,128]{2,1,0:T(8,128)}, f32[2,112,128]{2,1,0:T(8,128)S(1)}, u32[]{:S(2)}) copy-start(f32[2,112,128]{2,1,0:T(8,128)S(1)} %add_third.1.refs_0_) | copy-start | bytes 344068
  184.1 4.8 %collective-permute-start.15 = (f32[2,112,128]{2,1,0:T(8,128)S(1)}, f32[2,112,128]{2,1,0:T(8,128)S(1)}, u32[]{:S(2)}, u32[]{:S(2)}) collective-permute-start(f32[2,112,128]{2,1,0:T(8,128)S(1)} %add_third.1.refs_0_), channel_id=1, source_target_pairs={{0,128},{128,0},{1,129},{129,1},{2,130},{130,2},{3,131},{131,3},{4... | collective-permute-start | bytes 344072 | tf_op jit(solution)/shard_map/ppermute | solution.py:824
  188.9 0.6 copy-start.13
where the time goes:
time: 193 us; the launch traced here: 192 us
  Pallas kernels  104 us (54%)
  waiting for transfers between devices  49.1 us (25%)
  starting transfers between devices  24.6 us (13%)
  local copies, waits for them, and re-layouts  13.5 us (7%)
    pallas_call x3, Pallas kernels, backward(): pl.pallas_call(lambda *refs: backward_kernel(names, last, with_mlp, with_...  50.3 us
    ppermute x12, waiting for transfers between devices, ring(): lax.ppermute(parts[s], GROUP_AXES, ring_pairs(stage, s))  46.5 us
    pallas_call x2, Pallas kernels, forward(): pl.pallas_call(lambda *refs: forward_kernel(first, *refs), grid=(CHUNKS,)...  44.2 us
    ppermute x12, starting transfers between devices, ring(): lax.ppermute(parts[s], GROUP_AXES, ring_pairs(stage, s))  19.5 us
    unnamed x32, local copies, waits for them, and re-layouts  7.12 us
    pallas_call x5, Pallas kernels, call_add(): pl.pallas_call(kernel, out_shape=[jax.ShapeDtypeStruct(out_dims + (ROWS,...  6.94 us
    ppermute x3, starting transfers between devices, core_swap(): values += [keep, lax.ppermute(send, GROUP_AXES, core_pairs())]  4.98 us
    dynamic_slice x5, local copies, waits for them, and re-layouts, body(): lax.dynamic_slice_in_dim(masters[kind_index], owner_index * share_rows, s...  4.93 us
  transfers between devices with their start and end apart: 16, of which 9 were waited for; matrix products, arithmetic and copies ran while one was open for 4% of the time, Pallas kernels for 14%

commit v1 on v0

v1 whole, which is shorter than its diff:
```python
import types
import typing

import jax
import jax.numpy as jnp
from jax import lax
from jax.experimental import pallas as pl
from jax.experimental.pallas import tpu as pltpu
from jax.sharding import PartitionSpec as P

D = 384
HEADS = 6
HEAD_DIM = 64
FF = 1536
SEQ = 50
STEP = 10


beta_one = 0.9
beta_two = 0.95
adam_eps = 1e-08
decay_rate = 0.1
outer_decay = 0.9
outer_rate = 0.7

ROWS = 112
UP_AT, DOWN_AT, QKV_AT, PROJ_AT, SMALL_AT = 0, 36, 72, 99, 108
SUMS_AT = 64
ENTRIES = 98304000
VMEM_WHOLE = pl.BlockSpec(memory_space=pltpu.VMEM)
ANYWHERE = pl.BlockSpec(memory_space=pl.ANY)
GROUP_AXES = ("wide", "narrow")
IMG = 10
CHUNKS = 2
RUN = 512
REAL = IMG * SEQ
TOGETHER = 5
TOGETHER_BACK = 5
G1, B1, BQ, BV, BO, G2, B2, BU, BD = 0, 384, 768, 1152, 1536, 1920, 2304, 2688, 4224
BF = jnp.bfloat16
F32 = jnp.float32
WEIGHT_SIZES = ((D, 3 * D), (D, D), (D, FF), (FF, D))


def rates():
    return (1.5 * D ** (-0.5), 1.5 * (D // 4) ** (-0.5), 1.5 * D ** (-0.5), 1.5 * FF ** (-0.5), 2.0)


def place_of(owner):
    return owner // 32, owner // 8 % 4, owner // 4 % 2, owner % 4


def owner_of(deep, high, core, across):
    return ((deep * 4 + high) * 2 + core) * 4 + across


def core_pairs():
    return [(o, o ^ 4) for o in range(128)]


def ring_pairs(stage, shift):
    pairs = []
    for o in range(128):
        deep, high, core, across = place_of(o)
        if stage == 2:
            deep = deep ^ shift
        elif core == stage:
            across = across ^ shift
        else:
            high = high ^ shift
        pairs.append((o, owner_of(deep, high, core, across)))
    return pairs


def dot(left, right, left_dim=1, right_dim=0):
    return lax.dot_general(
        left, right, (((left_dim,), (right_dim,)), ((), ())), preferred_element_type=F32
    )


def normalise(rows):
    center = rows - jnp.sum(rows, -1, keepdims=True) * (1 / D)
    rate = lax.rsqrt(jnp.sum(center * center, -1, keepdims=True) * (1 / D) + 1e-06)
    return center * rate, rate


def norm_back(grad, unit, rate, gain):
    scaled = grad * gain
    first = jnp.sum(scaled, -1, keepdims=True) * (1 / D)
    second = jnp.sum(scaled * unit, -1, keepdims=True) * (1 / D)
    return rate * (scaled - first - unit * second)


def gelu_parts(value):
    area = 0.5 + 0.5 * lax.erf(value * 0.7071067811865476)
    bell = jnp.exp(-0.5 * value * value)
    return value * area, area + value * bell * 0.3989422804014327


def fold(values):
    return jnp.sum(values.reshape(-1, 8, values.shape[-1]), 0)


def halves_of(rows, low, keep):
    zero = jnp.zeros_like(rows)
    top = jnp.where(keep & low, rows, zero)
    bottom = jnp.where(keep & ~low, rows, zero)
    return jnp.concatenate([top, bottom], 0).astype(BF)


def masks():
    low = lax.broadcasted_iota(jnp.int32, (64, 128), 1) < 64
    keep = lax.broadcasted_iota(jnp.int32, (64, 128), 0) < SEQ
    return low, keep


def bias(r, start, stop):
    return r.vec[r.layer : r.layer + 1, start:stop]


def unpack(images, base, target):
    target[0, REAL - 4 : RUN, :] = jnp.zeros((RUN + 4 - REAL, D), F32)
    for image in range(IMG):
        target[0, SEQ * image : SEQ * (image + 1), :] = images[base + image].astype(F32)


def ahead_norm(r):
    def norm_block(i, carry):
        rows = pl.ds(pl.multiple_of(i * 64, 64), 64)
        unit, _ = normalise(r.stream[0, rows, :])
        r.normed[rows, :] = (unit * bias(r, G1, B1) + bias(r, B1, BQ)).astype(BF)
        return carry

    lax.fori_loop(0, RUN // 64, norm_block, 0)


def ahead_attention(r):
    proj, heads = r.proj, r.heads
    for third in range(3):
        result = dot(r.normed[...], r.w_attn[0, :, D * third : D * (third + 1)])
        if third == 0:
            result = result + bias(r, BQ, BV)
        if third == 2:
            result = result + bias(r, BV, BO)
        for block in range(3):
            proj[3 * third + block, 0:RUN, :] = result[:, 128 * block : 128 * (block + 1)]

    low, keep = masks()
    keep_keys = keep[0:56]

    def attend(i, carry):
        items = [(i * TOGETHER + k, pair) for k in range(TOGETHER) for pair in range(3)]
        loaded = []
        for image, pair in items:
            at = pl.ds(image * SEQ, 64)
            query = proj[pair, at, :]
            key = jnp.where(keep, proj[3 + pair, at, :], 0.0).astype(BF)
            value = jnp.where(keep, proj[6 + pair, at, :], 0.0).astype(BF)
            r.p_img[image, pair] = jnp.where(keep, query, 0.0).astype(BF)
            r.p_img[image, 3 + pair] = key
            r.p_img[image, 6 + pair] = value
            loaded.append((key, halves_of(query * 0.125, low, keep), value))
        scores = [dot(key, spread, 1, 1)[0:56] for key, spread, _ in loaded]
        weights = []
        for (image, pair), score in zip(items, scores):
            score = jnp.where(keep_keys, score, -1e30)
            raised = jnp.exp(score - jnp.max(score, 0, keepdims=True))
            weight = raised * (1.0 / jnp.sum(raised, 0, keepdims=True))
            weight = jnp.concatenate([weight, jnp.zeros((8, 128), F32)], 0).astype(BF)
            r.a_img[image, pair] = weight
            weights.append(weight)
        results = [dot(weight, value, 0, 0) for weight, (_, _, value) in zip(weights, loaded)]
        for (image, pair), both in zip(items, results):
            one = jnp.where(low, both[0:64], both[64:128])
            heads[pair, pl.ds(image * SEQ, SEQ), :] = one[0:SEQ]
        return carry

    lax.fori_loop(0, IMG // TOGETHER, attend, 0)
    for block in range(3):
        r.mixed[0, :, 128 * block : 128 * (block + 1)] = heads[block, 0:RUN, :].astype(BF)


def ahead_mlp(r):
    totals = r.totals
    real = lax.broadcasted_iota(jnp.int32, (RUN, D), 0) < REAL
    before = r.stream[0]
    branch = dot(r.mixed[0], r.w_out[0]) + bias(r, BO, G2)
    between = before + branch
    r.middle[0] = between
    totals[0:8, :] += fold(jnp.where(real, before * before, 0.0))
    totals[8:16, :] += fold(jnp.where(real, branch * branch, 0.0))

    def norm_block(i, carry):
        rows = pl.ds(pl.multiple_of(i * 64, 64), 64)
        unit, _ = normalise(r.middle[0, rows, :])
        r.normed[rows, :] = (unit * bias(r, G2, B2) + bias(r, B2, BU)).astype(BF)
        return carry

    lax.fori_loop(0, RUN // 64, norm_block, 0)
    r.hidden[...] = dot(r.normed[...], r.w_up[0])
    for row in range(0, RUN, 32):
        for column in range(0, FF, 256):
            part = r.hidden[row : row + 32, column : column + 256]
            part = part + bias(r, BU + column, BU + column + 256)
            bent, tilt = gelu_parts(part)
            r.act[0, row : row + 32, column : column + 256] = bent.astype(BF)
            r.slope[0, row : row + 32, column : column + 256] = tilt.astype(BF)
    tail = dot(r.act[0], r.w_down[0]) + bias(r, BD, BD + D)
    totals[16:24, :] += fold(jnp.where(real, tail * tail, 0.0))
    r.after[0] = r.middle[0] + tail


def total_row(totals):
    lane = lax.broadcasted_iota(jnp.int32, (1, 128), 1)
    row = jnp.zeros((1, 128), F32)
    for k in range(3):
        row = jnp.where(lane == SUMS_AT + k, jnp.sum(totals[8 * k : 8 * k + 8, :]), row)
    return row


def chunked(*dims):
    return pl.BlockSpec((1,) + dims, lambda c: (c,) + (0,) * len(dims))


def imaged(*dims):
    return pl.BlockSpec((IMG,) + dims, lambda c: (c,) + (0,) * len(dims))


def whole(*dims):
    return pl.BlockSpec(dims, lambda c: (0,) * len(dims))


def held(*dims):
    return pl.BlockSpec(dims, lambda c: (0,) * len(dims), pipeline_mode=pl.Buffered(1))


def shape(kind, *dims):
    return jax.ShapeDtypeStruct(dims, kind)


def emit_packed(core, plan):
    def emit(own):
        @pl.loop(0, 16)
        def _(block):
            deep, high = block // 4, block % 4
            for source, each, width, *targets in plan:
                height = 8 * each
                base = pl.multiple_of(block * height, 8)
                for column in range(width):
                    rows = source[pl.ds(base, height), column * 128 : (column + 1) * 128]
                    for k in range(8):
                        target, start = targets[0 if k // 4 == own else 1]
                        at = start + each * column
                        first, second = (k, high) if k < 4 else (high, k - 4)
                        target.at[first, second, deep][at : at + each, :] = rows[
                            each * k : each * (k + 1)
                        ]

    for own in range(2):

        @pl.when(core == own)
        def _():
            emit(own)


def back_mlp(r, grad):
    here = grad[0]
    r.acc_vec[:, BD : BD + D] += fold(here)
    r.low_grad[...] = here.astype(BF)
    r.hidden[...] = dot(r.low_grad[...], r.w_down[0], 1, 1)
    for column in range(0, FF, 256):
        total = jnp.zeros((8, 256), F32)
        for row in range(0, RUN, 32):
            at = slice(row, row + 32)
            part = r.hidden[at, column : column + 256]
            part = part * r.slope[0, at, column : column + 256].astype(F32)
            r.d_hidden[at, column : column + 256] = part.astype(BF)
            total = total + fold(part)
        r.acc_vec[:, BU + column : BU + column + 256] += total
    d_normed = dot(r.d_hidden[...], r.w_up[0], 1, 1)
    unit, rate = normalise(r.middle[0])
    gain = bias(r, G2, B2)
    r.normed[...] = (unit * gain + bias(r, B2, BU)).astype(BF)
    r.acc_vec[:, G2:B2] += fold(d_normed * unit)
    r.acc_vec[:, B2:BU] += fold(d_normed)
    r.d_mid[0] = grad[0] + norm_back(d_normed, unit, rate, gain)
    r.acc_down[...] = jnp.where(r.first, 0.0, r.acc_down[...]) + dot(r.act[0], r.low_grad[...], 0, 0)
    r.acc_up[...] = jnp.where(r.first, 0.0, r.acc_up[...]) + dot(r.normed[...], r.d_hidden[...], 0, 0)


def back_attention(r, d_mid, result):
    between = d_mid[0]
    r.acc_vec[:, BO:G2] += fold(between)
    r.d_branch[...] = between.astype(BF)
    product = dot(r.d_branch[...], r.w_out[0], 1, 1)
    for block in range(3):
        r.d_heads[block, 0:RUN, :] = product[:, 128 * block : 128 * (block + 1)]
    r.acc_out[...] = jnp.where(r.first, 0.0, r.acc_out[...]) + dot(r.mixed[0], r.d_branch[...], 0, 0)
    low, keep = masks()
    p_img, a_img, d_heads, d_proj = r.p_img, r.a_img, r.d_heads, r.proj
    for block in range(9):
        d_proj[block, REAL - 4 : RUN + 16, :] = jnp.zeros((RUN + 20 - REAL, 128), F32)

    def attend(i, carry):
        items = [(i * TOGETHER_BACK + k, pair) for k in range(TOGETHER_BACK) for pair in range(3)]
        loaded = []
        for image, pair in items:
            rows = d_heads[pair, pl.ds(image * SEQ, 64), :]
            spread = halves_of(p_img[image, pair].astype(F32) * 0.125, low, keep)
            loaded.append((spread, halves_of(rows, low, keep)))
        d_weights = [
            dot(p_img[image, 6 + pair], d_spread, 1, 1)
            for (image, pair), (_, d_spread) in zip(items, loaded)
        ]
        d_values = [
            dot(a_img[image, pair], d_spread) for (image, pair), (_, d_spread) in zip(items, loaded)
        ]
        d_scores = []
        for (image, pair), d_weight in zip(items, d_weights):
            weight = a_img[image, pair].astype(F32)
            product = weight * d_weight
            d_scores.append((product - weight * jnp.sum(product, 0, keepdims=True)).astype(BF))
        d_keys = [dot(d_score, spread) for d_score, (spread, _) in zip(d_scores, loaded)]
        d_both = [
            dot(d_score, p_img[image, 3 + pair], 0, 0)
            for (image, pair), d_score in zip(items, d_scores)
        ]
        for (image, pair), d_key, both, d_value in zip(items, d_keys, d_both, d_values):
            d_query = jnp.where(low, both[0:64], both[64:128]) * 0.125
            at = pl.ds(image * SEQ, SEQ)
            d_proj[pair, at, :] = d_query[0:SEQ]
            d_proj[3 + pair, at, :] = d_key[0:SEQ]
            d_proj[6 + pair, at, :] = d_value[0:SEQ]
        return carry

    lax.fori_loop(0, IMG // TOGETHER_BACK, attend, 0)
    for block in range(9):
        part = d_proj[block, 0:RUN, :]
        r.d_low[:, 128 * block : 128 * (block + 1)] = part.astype(BF)
        if block < 3:
            r.acc_vec[:, BQ + 128 * block : BQ + 128 * (block + 1)] += fold(part)
        if block >= 6:
            r.acc_vec[:, BV + 128 * (block - 6) : BV + 128 * (block - 5)] += fold(part)
    d_normed = dot(r.d_low[...], r.w_attn[0], 1, 1)
    unit, rate = normalise(r.stream[0])
    gain = bias(r, G1, B1)
    r.normed[...] = (unit * gain + bias(r, B1, BQ)).astype(BF)
    r.acc_vec[:, G1:B1] += fold(d_normed * unit)
    r.acc_vec[:, B1:BQ] += fold(d_normed)
    result[0] = d_mid[0] + norm_back(d_normed, unit, rate, gain)
    r.acc_attn[...] = jnp.where(r.first, 0.0, r.acc_attn[...]) + dot(r.normed[...], r.d_low[...], 0, 0)


def fill_small(small, acc_vec, row):
    total = jnp.sum(acc_vec[...], 0, keepdims=True)
    small[...] = jnp.broadcast_to(row, (128, 128))
    for owner in range(128):
        small[owner : owner + 1, 0:36] = total[:, 36 * owner : 36 * (owner + 1)]


def mlp_plan(r, keep, send_up, send_down, up_at, down_at):
    return [
        (r.acc_up, 3, 12, (keep, UP_AT), (send_up, up_at)),
        (r.acc_down, 12, 3, (keep, DOWN_AT), (send_down, down_at)),
    ]


def attention_plan(r, keep, send, shift):
    return [
        (r.acc_attn, 3, 9, (keep, QKV_AT - shift), (send, QKV_AT - shift)),
        (r.acc_out, 3, 3, (keep, PROJ_AT - shift), (send, PROJ_AT - shift)),
        (r.small, 1, 1, (keep, SMALL_AT - shift), (send, SMALL_AT - shift)),
    ]


def spaces(ins, outs, scratch, refs):
    return types.SimpleNamespace(**dict(zip([*ins, *outs, *scratch], refs)))


def call_kernel(kernel, ins, outs, scratch, limit, name):
    results = pl.pallas_call(
        lambda *refs: kernel(spaces(ins, outs, scratch, refs)),
        grid=(CHUNKS,),
        out_shape=[v[0] for v in outs.values()],
        in_specs=[v[1] for v in ins.values()],
        out_specs=[v[1] for v in outs.values()],
        scratch_shapes=list(scratch.values()),
        compiler_params=pltpu.CompilerParams(vmem_limit_bytes=limit * 2**20),
        name=name,
    )(*[v[0] for v in ins.values()])
    return types.SimpleNamespace(**dict(zip(outs, results)))


class Kept(typing.NamedTuple):
    p_img: typing.Any
    a_img: typing.Any
    mixed: typing.Any
    stream: typing.Any
    middle: typing.Any
    act: typing.Any
    slope: typing.Any


class Weights(typing.NamedTuple):
    w_attn: typing.Any
    w_out: typing.Any
    w_up: typing.Any
    w_down: typing.Any


KEPT_BLOCKS = Kept(
    ((IMG, 9, 64, 128), BF),
    ((IMG, 3, 64, 128), BF),
    ((1, RUN, D), BF),
    ((1, RUN, D), F32),
    ((1, RUN, D), F32),
    ((1, RUN, FF), BF),
    ((1, RUN, FF), BF),
)


def front_kernel(r):
    step = pl.program_id(0)
    first, final = step == 0, step == CHUNKS - 1
    kept = [Kept(*[getattr(r, n + s) for n in Kept._fields]) for s in ("_a", "_b")]
    weights = [Weights(*[getattr(r, n + s) for n in Weights._fields]) for s in ("_a", "_b")]
    kept_out = [getattr(r, n) for n in Kept._fields]
    weights_out = [getattr(r, n) for n in Weights._fields]
    masters = (r.m_attn, r.m_out, r.m_up, r.m_down)
    stages = (r.acc_attn, r.acc_out, r.acc_up, r.acc_down)

    def load(layer, k):
        return pltpu.make_async_copy(masters[k].at[layer], stages[k], r.load_sem.at[k])

    def save(k, chunk):
        size = kept[0][k].shape[0]
        target = kept_out[k].at[pl.ds(chunk * size, size)]
        return pltpu.make_async_copy(kept[0][k], target, r.save_sem.at[k])

    def save_weight(k):
        return pltpu.make_async_copy(weights[0][k], weights_out[k], r.weight_sem.at[k])

    def take(layer, k):
        load(layer, k).wait()
        weights[layer][k][0] = stages[k][...].astype(BF)

    def fetch(k):
        source, target = ((r.tokens, r.tokens_in), (r.grad_in, r.grad_low))[k]
        return pltpu.make_async_copy(source, target, r.fetch_sem.at[k])

    @pl.when(first)
    def _():
        fetch(0).start()
        for k in range(4):
            load(0, k).start()
        fetch(1).start()
        r.totals_a[...] = jnp.zeros_like(r.totals_a)
        r.totals_b[...] = jnp.zeros_like(r.totals_b)
        r.acc_vec[...] = jnp.zeros_like(r.acc_vec)
        for block in range(9):
            r.proj[block, RUN : RUN + 16, :] = jnp.zeros((16, 128), F32)
        for block in range(3):
            r.heads[block, REAL - 4 : RUN + 16, :] = jnp.zeros((RUN + 20 - REAL, 128), F32)
            r.d_heads[block, RUN : RUN + 16, :] = jnp.zeros((16, 128), F32)
        fetch(0).wait()

    @pl.when(step > 0)
    def _():
        for k in range(7):
            save(k, step - 1).wait()

    shared = dict(
        first=first,
        vec=r.vec,
        normed=r.normed,
        proj=r.proj,
        heads=r.heads,
        hidden=r.hidden,
    )
    zero = types.SimpleNamespace(
        **shared,
        **kept[0]._asdict(),
        **weights[0]._asdict(),
        layer=0,
        totals=r.totals_a,
        after=kept[1].stream,
    )
    one = types.SimpleNamespace(
        **shared,
        **kept[1]._asdict(),
        **weights[1]._asdict(),
        layer=1,
        totals=r.totals_b,
        after=r.d_mid,
        d_heads=r.d_heads,
        d_hidden=r.d_hidden,
        d_low=r.d_low,
        d_mid=r.d_mid,
        d_branch=r.d_branch,
        low_grad=r.low_grad,
        acc_vec=r.acc_vec,
        acc_attn=r.acc_attn,
        acc_out=r.acc_out,
        acc_up=r.acc_up,
        acc_down=r.acc_down,
        small=r.small,
    )
    unpack(r.tokens_in, step * IMG, zero.stream)
    ahead_norm(zero)

    @pl.when(first)
    def _():
        take(0, 0)

    ahead_attention(zero)
    for k in range(4):
        save(k, step).start()

    @pl.when(first)
    def _():
        for k in range(1, 4):
            take(0, k)
        for k in range(4):
            load(1, k).start()
            save_weight(k).start()

    ahead_mlp(zero)
    for k in range(4, 7):
        save(k, step).start()
    ahead_norm(one)

    @pl.when(first)
    def _():
        for k in range(4):
            take(1, k)
        fetch(1).wait()

    ahead_attention(one)
    ahead_mlp(one)
    for image in range(IMG):
        r.block_out[image] = one.after[0, SEQ * image : SEQ * (image + 1), :].astype(BF)
    unpack(r.grad_low, step * IMG, r.grad)
    back_mlp(one, r.grad)
    back_attention(one, one.d_mid, r.grad_out)

    @pl.when(final)
    def _():
        r.sums[...] = total_row(r.totals_a)
        fill_small(r.small, r.acc_vec, total_row(r.totals_b))
        plan = mlp_plan(r, r.keep, r.send, r.send, UP_AT, DOWN_AT)
        emit_packed(r.core[0], plan + attention_plan(r, r.keep, r.send, 0))
        for k in range(7):
            save(k, step).wait()
        for k in range(4):
            save_weight(k).wait()


def front(core, tokens, grad_out, masters, vector):
    smem = pl.BlockSpec(memory_space=pltpu.SMEM)
    ins = dict(
        core=(core, smem),
        tokens=(tokens, ANYWHERE),
        grad_in=(grad_out, ANYWHERE),
        vec=(vector, whole(2, 12 * D)),
        m_attn=(masters[0], ANYWHERE),
        m_out=(masters[1], ANYWHERE),
        m_up=(masters[2], ANYWHERE),
        m_down=(masters[3], ANYWHERE),
    )
    half = shape(F32, 4, 4, 4, ROWS, 128)
    outs = {
        n: (shape(kind, CHUNKS * dims[0], *dims[1:]), ANYWHERE)
        for n, (dims, kind) in KEPT_BLOCKS._asdict().items()
    }
    outs.update({n: (shape(BF, 1, *s), ANYWHERE) for n, s in zip(Weights._fields, WEIGHT_SIZES)})
    outs.update(
        sums=(shape(F32, 1, 128), whole(1, 128)),
        block_out=(shape(BF, IMG * CHUNKS, SEQ, D), imaged(SEQ, D)),
        grad_out=(shape(F32, CHUNKS, RUN, D), chunked(RUN, D)),
        keep=(half, VMEM_WHOLE),
        send=(half, VMEM_WHOLE),
    )
    scratch = {}
    for suffix in ("_a", "_b"):
        for n, (dims, kind) in KEPT_BLOCKS._asdict().items():
            scratch[n + suffix] = pltpu.VMEM(dims, kind)
        for n, size in zip(Weights._fields, WEIGHT_SIZES):
            scratch[n + suffix] = pltpu.VMEM((1,) + size, BF)
    scratch.update(
        totals_a=pltpu.VMEM((24, D), F32),
        totals_b=pltpu.VMEM((24, D), F32),
        heads=pltpu.VMEM((3, RUN + 16, 128), F32),
        **mlp_scratch(),
        **attention_scratch(),
        d_mid=pltpu.VMEM((1, RUN, D), F32),
        grad=pltpu.VMEM((1, RUN, D), F32),
        normed=pltpu.VMEM((RUN, D), BF),
        acc_vec=pltpu.VMEM((8, 12 * D), F32),
        tokens_in=pltpu.VMEM((IMG * CHUNKS, SEQ, D), BF),
        grad_low=pltpu.VMEM((IMG * CHUNKS, SEQ, D), BF),
        fetch_sem=pltpu.SemaphoreType.DMA((2,)),
        load_sem=pltpu.SemaphoreType.DMA((4,)),
        save_sem=pltpu.SemaphoreType.DMA((7,)),
        weight_sem=pltpu.SemaphoreType.DMA((4,)),
    )
    return call_kernel(front_kernel, ins, outs, scratch, FRONT_LIMIT, "front")


FRONT_LIMIT = 52


def mlp_scratch():
    return dict(
        low_grad=pltpu.VMEM((RUN, D), BF),
        hidden=pltpu.VMEM((RUN, FF), F32),
        d_hidden=pltpu.VMEM((RUN, FF), BF),
        acc_up=pltpu.VMEM((D, FF), F32),
        acc_down=pltpu.VMEM((FF, D), F32),
    )


def attention_scratch():
    return dict(
        d_branch=pltpu.VMEM((RUN, D), BF),
        d_heads=pltpu.VMEM((3, RUN + 16, 128), F32),
        proj=pltpu.VMEM((9, RUN + 16, 128), F32),
        d_low=pltpu.VMEM((RUN, 3 * D), BF),
        acc_attn=pltpu.VMEM((D, 3 * D), F32),
        acc_out=pltpu.VMEM((D, D), F32),
        small=pltpu.VMEM((128, 128), F32),
    )


def back_kernel(r):
    step = pl.program_id(0)
    r.layer = 0
    r.first = step == 0

    @pl.when(r.first)
    def _():
        r.acc_vec[...] = jnp.zeros_like(r.acc_vec)
        for block in range(3):
            r.d_heads[block, RUN : RUN + 16, :] = jnp.zeros((16, 128), F32)

    back_mlp(r, r.grad_in)
    back_attention(r, r.d_mid, r.grad)
    for image in range(IMG):
        r.grad_out[image] = r.grad[0, SEQ * image : SEQ * (image + 1), :]

    @pl.when(step == CHUNKS - 1)
    def _():
        fill_small(r.small, r.acc_vec, r.sums[...])
        plan = mlp_plan(r, r.keep, r.send, r.send, UP_AT, DOWN_AT)
        emit_packed(r.core[0], plan + attention_plan(r, r.keep, r.send, 0))


def back_call(core, grad, vector, ahead):
    half = shape(F32, 4, 4, 4, ROWS, 128)
    ins = dict(
        core=(core, pl.BlockSpec(memory_space=pltpu.SMEM)),
        grad_in=(grad, chunked(RUN, D)),
        vec=(vector, whole(2, 12 * D)),
        sums=(ahead.sums, whole(1, 128)),
    )
    for n, size in zip(Weights._fields, WEIGHT_SIZES):
        ins[n] = (getattr(ahead, n), held(1, *size))
    for n, (dims, _) in KEPT_BLOCKS._asdict().items():
        ins[n] = (getattr(ahead, n), imaged(*dims[1:]) if dims[0] == IMG else chunked(*dims[1:]))
    outs = dict(
        grad_out=(shape(F32, IMG * CHUNKS, SEQ, D), imaged(SEQ, D)),
        keep=(half, VMEM_WHOLE),
        send=(half, VMEM_WHOLE),
    )
    scratch = dict(
        **mlp_scratch(),
        **attention_scratch(),
        d_mid=pltpu.VMEM((1, RUN, D), F32),
        grad=pltpu.VMEM((1, RUN, D), F32),
        normed=pltpu.VMEM((RUN, D), BF),
        acc_vec=pltpu.VMEM((8, 12 * D), F32),
    )
    return call_kernel(back_kernel, ins, outs, scratch, BACK_LIMIT, "back")


BACK_LIMIT = 50


def local_step(core, tokens, grad_out, masters, vector):
    ahead = front(core, tokens, grad_out, masters, vector)
    parts = add_core(ahead.keep, swap_core(ahead.send))
    grad, parts = lax.optimization_barrier((ahead.grad_out, parts))
    parts_one = ring(0, parts)
    back = back_call(core, grad, vector, ahead)
    send, parts_one = lax.optimization_barrier((back.send, parts_one))
    parts_zero = ring(0, add_core(back.keep, swap_core(send)))
    return ahead.block_out, back.grad_out, parts_zero + parts_one


def stage_position(stage):
    deep, high, core, across = place_of(lax.axis_index(GROUP_AXES))
    if stage == 2:
        return deep
    return jnp.where(core == stage, across, high)


def add_core_kernel(keep, got, *outs):
    me = stage_position(0)
    for shift in range(4):
        at = me ^ shift

        @pl.loop(0, 16)
        def _(i):
            outs[shift][i // 4, i % 4] = keep[at, i // 4, i % 4] + got[at, i // 4, i % 4]


def add_first_kernel(*refs):
    sources = [refs[4 * k : 4 * k + 4] for k in range(2)]
    outs = refs[-4:]
    me = stage_position(1)
    for shift in range(4):
        at = me ^ shift

        @pl.loop(0, 4)
        def _(i):
            for layer, (own, one, two, three) in enumerate(sources):
                outs[shift][i, layer] = (own[at, i] + one[at, i]) + (two[at, i] + three[at, i])


def add_second_kernel(own, one, two, three, *outs):
    me = stage_position(2)
    for shift in range(4):
        at = me ^ shift
        outs[shift][...] = (own[at] + one[at]) + (two[at] + three[at])


def add_third_kernel(own, one, two, three, out):
    out[...] = (own[...] + one[...]) + (two[...] + three[...])


def call_add(kernel, values, out_dims, count, name):
    return pl.pallas_call(
        kernel,
        out_shape=[shape(F32, *out_dims, 128)] * count,
        in_specs=[VMEM_WHOLE] * len(values),
        out_specs=[VMEM_WHOLE] * count,
        compiler_params=pltpu.CompilerParams(vmem_limit_bytes=32 * 2**20),
        name=name,
    )(*values)


def ring(stage, parts):
    got = [lax.ppermute(parts[s], GROUP_AXES, ring_pairs(stage, s)) for s in range(1, 4)]
    return [parts[0]] + got


def swap_core(send):
    return lax.ppermute(send, GROUP_AXES, core_pairs())


def add_core(keep, got):
    return call_add(add_core_kernel, [keep, got], (4, 4, ROWS), 4, "add_core")


def finish_sums(parts):
    parts = call_add(add_first_kernel, parts, (4, 2, ROWS), 4, "add_first")
    parts = call_add(add_second_kernel, ring(1, parts), (2, ROWS), 4, "add_second")
    own = call_add(add_third_kernel, ring(2, parts), (2, ROWS), 1, "add_third")[0]
    return own, lax.ppermute(own, "grp", [(0, 1), (1, 0)])


def adam_step(gradient, moment_one, moment_two, weight, rate):
    moment_one = beta_one * moment_one + (1 - beta_one) * gradient
    moment_two = beta_two * moment_two + (1 - beta_two) * gradient * gradient
    fix_one = 1 - beta_one**STEP
    fix_two = 1 - beta_two**STEP
    update = (
        moment_one / fix_one / (jnp.sqrt(moment_two / fix_two) + adam_eps) + decay_rate * weight
    )
    return (moment_one, moment_two, weight - rate * update)


def finish_kernel(*refs):
    own, other = ([ref.at[k] for k in range(2)] for ref in refs[:2])
    weights, firsts, seconds, outers = (refs[2 + 5 * k : 7 + 5 * k] for k in range(4))
    outs = refs[22:]
    new_firsts, new_seconds, changes, new_outers, finals, copies = (
        outs[5 * k : 5 * k + 5] for k in range(6)
    )
    rms = outs[30]

    def gathered(refs, kind, row):
        if kind == 4:
            return jnp.concatenate([ref[SMALL_AT : SMALL_AT + 1, 0:36] for ref in refs], 0)
        start, rows, width = (
            (QKV_AT, 3, 9),
            (PROJ_AT, 3, 3),
            (UP_AT, 3, 12),
            (DOWN_AT, 12, 3),
        )[kind]
        lines = [start + rows * c + row for c in range(width)]
        return jnp.concatenate(
            [
                jnp.concatenate([ref[line : line + 1, :] for ref in refs], 0)
                for line in lines
            ],
            1,
        )

    for kind in range(5):
        rate = rates()[kind]
        for row in range(1 if kind == 4 else weights[kind].shape[0]):
            at = slice(None) if kind == 4 else row
            weight = weights[kind][at]
            moments = (firsts[kind][at], seconds[kind][at])
            one, two, updated = adam_step(gathered(own, kind, row), *moments, weight, rate)
            updated_other = adam_step(gathered(other, kind, row), *moments, weight, rate)[2]
            change = ((weight - updated) + (weight - updated_other)) / 2
            outer = outer_decay * outers[kind][at] + change
            final = weight - outer_rate * (change + outer_decay * outer)
            new_firsts[kind][at] = one
            new_seconds[kind][at] = two
            changes[kind][at] = change
            new_outers[kind][at] = outer
            finals[kind][at] = final
            copies[kind][at] = final.astype(jnp.bfloat16)
    for layer in range(2):
        totals = [
            ref[SMALL_AT : SMALL_AT + 1, SUMS_AT : SUMS_AT + 3] for ref in (own[layer], other[layer])
        ]
        rms[layer : layer + 1, :] = jnp.sqrt((totals[0] + totals[1]) / ENTRIES)


def rows_first(value):
    return value if value.ndim == 2 else jnp.swapaxes(value, 0, 1)


def finish(own, other, weights, firsts, seconds, outers):
    given = [rows_first(v) for v in (*weights, *firsts, *seconds, *outers)]
    full = [jax.ShapeDtypeStruct(v.shape, jnp.float32) for v in given[:5]]
    low = [jax.ShapeDtypeStruct(v.shape, jnp.bfloat16) for v in given[:5]]
    results = pl.pallas_call(
        finish_kernel,
        out_shape=full * 5 + low + [jax.ShapeDtypeStruct((2, 3), jnp.float32)],
        in_specs=[VMEM_WHOLE] * 22,
        out_specs=[VMEM_WHOLE] * 31,
        name="finish",
    )(own, other, *given)
    results = [rows_first(v) for v in results[:30]] + [results[30]]
    return [v[None] for v in results[:10]] + results[10:]

def body(
    tokens,
    grad_out,
    weight_qkv,
    weight_proj,
    weight_up,
    weight_down,
    weight_vector,
    old_first_qkv,
    old_first_proj,
    old_first_up,
    old_first_down,
    old_first_vector,
    old_second_qkv,
    old_second_proj,
    old_second_up,
    old_second_down,
    old_second_vector,
    old_outer_qkv,
    old_outer_proj,
    old_outer_up,
    old_outer_down,
    old_outer_vector,
):
    masters = (weight_qkv, weight_proj, weight_up, weight_down, weight_vector)
    old_firsts = (old_first_qkv, old_first_proj, old_first_up, old_first_down, old_first_vector)
    old_seconds = (
        old_second_qkv,
        old_second_proj,
        old_second_up,
        old_second_down,
        old_second_vector,
    )
    old_outers = (old_outer_qkv, old_outer_proj, old_outer_up, old_outer_down, old_outer_vector)
    owner_index = lax.axis_index(GROUP_AXES)
    core = jnp.reshape(owner_index // 4 % 2, (1,)).astype(jnp.int32)
    block_out, grad_tokens, parts = local_step(
        core, tokens, grad_out, masters[:4], weight_vector
    )
    shares = []
    for kind_index in range(5):
        share_rows = old_firsts[kind_index].shape[1]
        shares.append(
            lax.dynamic_slice_in_dim(masters[kind_index], owner_index * share_rows, share_rows, 1)
        )
    own, other = finish_sums(parts)
    results = finish(own, other, shares, old_firsts, old_seconds, old_outers)
    return (block_out, grad_tokens, *results)


def solution(mesh):
    placed = (
        P(("grp", "wide", "narrow"), None, None),
        P(("grp", "wide", "narrow"), None, None),
        P(),
        P(),
        P(),
        P(),
        P(),
        P(None, ("wide", "narrow"), None),
        P(None, ("wide", "narrow"), None),
        P(None, ("wide", "narrow"), None),
        P(None, ("wide", "narrow"), None),
        P(None, ("wide", "narrow")),
        P(None, ("wide", "narrow"), None),
        P(None, ("wide", "narrow"), None),
        P(None, ("wide", "narrow"), None),
        P(None, ("wide", "narrow"), None),
        P(None, ("wide", "narrow")),
        P(None, ("wide", "narrow"), None),
        P(None, ("wide", "narrow"), None),
        P(None, ("wide", "narrow"), None),
        P(None, ("wide", "narrow"), None),
        P(None, ("wide", "narrow")),
    )
    return jax.shard_map(
        body,
        mesh=mesh,
        in_specs=placed,
        out_specs=(
            P(("grp", "wide", "narrow"), None, None),
            P(("grp", "wide", "narrow"), None, None),
            P("grp", None, ("wide", "narrow"), None),
            P("grp", None, ("wide", "narrow"), None),
            P("grp", None, ("wide", "narrow"), None),
            P("grp", None, ("wide", "narrow"), None),
            P("grp", None, ("wide", "narrow")),
            P("grp", None, ("wide", "narrow"), None),
            P("grp", None, ("wide", "narrow"), None),
            P("grp", None, ("wide", "narrow"), None),
            P("grp", None, ("wide", "narrow"), None),
            P("grp", None, ("wide", "narrow")),
            P(None, ("wide", "narrow"), None),
            P(None, ("wide", "narrow"), None),
            P(None, ("wide", "narrow"), None),
            P(None, ("wide", "narrow"), None),
            P(None, ("wide", "narrow")),
            P(None, ("wide", "narrow"), None),
            P(None, ("wide", "narrow"), None),
            P(None, ("wide", "narrow"), None),
            P(None, ("wide", "narrow"), None),
            P(None, ("wide", "narrow")),
            P(None, ("wide", "narrow"), None),
            P(None, ("wide", "narrow"), None),
            P(None, ("wide", "narrow"), None),
            P(None, ("wide", "narrow"), None),
            P(None, ("wide", "narrow")),
            P(None, ("wide", "narrow"), None),
            P(None, ("wide", "narrow"), None),
            P(None, ("wide", "narrow"), None),
            P(None, ("wide", "narrow"), None),
            P(None, ("wide", "narrow")),
            P(),
        ),
        check_vma=False,
    )
```

time: 193 us -> 176 us (0.912)
  Pallas kernels: 104 us -> 80.9 us
  waiting for transfers between devices: 49.1 us -> 54.8 us
    pallas_call x10 -> x7, Pallas kernels: 101 us -> 78.5 us  [the longest x2 75.9 us: call_kernel(): pl.pallas_call(lambda *refs: kernel(spaces(ins, outs, scratch, refs)), gr...]
    ppermute x4 -> x3, waiting for transfers between devices: 2.67 us -> 12.5 us  [the longest x2 12.5 us: swap_core(): return lax.ppermute(send, GROUP_AXES, core_pairs())]
    ppermute x12, waiting for transfers between devices: 46.5 us -> 42.3 us  [ring(): lax.ppermute(parts[s], GROUP_AXES, ring_pairs(stage, s))]
    unnamed x32 -> x22, local copies, waits for them, and re-layouts: 7.12 us -> 9.12 us
    ppermute x4 -> x3, starting transfers between devices: 5.07 us -> 5.6 us  [the longest x2 4.63 us: swap_core(): return lax.ppermute(send, GROUP_AXES, core_pairs())]
  transfers between devices with their start and end apart: 16 -> 15, of which waited for: 9 -> 10; matrix products, arithmetic and copies ran while one was open for 4% -> 4% of each run, Pallas kernels for 14% -> 13%
where the time goes in v1:
time: 176 us; the launch traced here: 175 us
  Pallas kernels  80.9 us (46%)
  waiting for transfers between devices  54.8 us (31%)
  starting transfers between devices  25.3 us (14%)
  local copies, waits for them, and re-layouts  13.3 us (8%)
    pallas_call x2, Pallas kernels, call_kernel(): pl.pallas_call(lambda *refs: kernel(spaces(ins, outs, scratch, refs)), gr...  75.9 us
    ppermute x12, waiting for transfers between devices, ring(): lax.ppermute(parts[s], GROUP_AXES, ring_pairs(stage, s))  42.3 us
    ppermute x12, starting transfers between devices, ring(): lax.ppermute(parts[s], GROUP_AXES, ring_pairs(stage, s))  19.7 us
    ppermute x2, waiting for transfers between devices, swap_core(): return lax.ppermute(send, GROUP_AXES, core_pairs())  12.5 us
    unnamed x22, local copies, waits for them, and re-layouts  9.12 us
    ppermute x2, starting transfers between devices, swap_core(): return lax.ppermute(send, GROUP_AXES, core_pairs())  4.63 us
    dynamic_slice x5, local copies, waits for them, and re-layouts, body(): lax.dynamic_slice_in_dim(masters[kind_index], owner_index * share_rows, s...  4.22 us
  transfers between devices with their start and end apart: 15, of which 10 were waited for; matrix products, arithmetic and copies ran while one was open for 4% of the time, Pallas kernels for 13%

profile of v1, /device:TPU:1, one launch (start us, length us, event | category | flops | bytes accessed | tf_op | source)
XLA Modules:
  0.0 175.3 jit_solution(1782341319209103168)
XLA Ops:
  0.7 1.1 copy-done.4
  1.9 0.8 copy-done.6
  2.6 52.3 %front.1 = (bf16[20,9,64,128]{3,2,1,0:T(8,128)(2,1)}, bf16[20,3,64,128]{3,2,1,0:T(8,128)(2,1)}, bf16[2,512,384]{2,1,0:T(8,128)(2,1)S(1)}, f32[2,512,384]{2,1,0:T...) custom-call(s32[1]{0:T(128)} %bitcast.refs_0_, ...), custom_call_target="tpu_custom_call" | custom-call | tf_op jit(solution)/shard_map/front/pallas_call | solution.py:381
  55.0 3.3 %collective-permute-start = (f32[4,4,4,112,128]{4,3,2,1,0:T(8,128)}, f32[4,4,4,112,128]{4,3,2,1,0:T(8,128)S(1)}, u32[]{:S(2)}, u32[]{:S(2)}) collective-permute-start(f32[4,4,4,112,128]{4,3,2,1,0:T(8,128)} %get-tuple-element.112), channel_id=1, source_target_pairs={{0,4},{1,5},{2,6},{3,7},{4,0},{5,1},{6,2},{7,3},{8,12},{9,13},{10,... | collective-permute-start | bytes 11010056 | tf_op jit(solution)/shard_map/ppermute | solution.py:757
  58.3 6.2 %collective-permute-done.got = f32[4,4,4,112,128]{4,3,2,1,0:T(8,128)S(1)} collective-permute-done((f32[4,4,4,112,128]{4,3,2,1,0:T(8,128)}, f32[4,4,4,112,128]{4,3,2,1,0:T(8,128)S(1)}, u32[]{:S(2)}, u32[]{:S(2)}) %collective-permute-start) | collective-permute-done | bytes 3670048 | tf_op jit(solution)/shard_map/ppermute | solution.py:757
  64.6 2.0 %copy-done.1 = f32[4,4,4,112,128]{4,3,2,1,0:T(8,128)S(1)} copy-done((f32[4,4,4,112,128]{4,3,2,1,0:T(8,128)S(1)}, f32[4,4,4,112,128]{4,3,2,1,0:T(8,128)}, u32[]{:S(2)}) %copy-start.1) | copy-done | bytes 3670040
  66.6 1.1 add_core.2
  67.7 0.1 collective-permute-start.1
  67.8 2.2 %collective-permute-start.2 = (f32[4,4,112,128]{3,2,1,0:T(8,128)S(1)}, f32[4,4,112,128]{3,2,1,0:T(8,128)S(1)}, u32[]{:S(2)}, u32[]{:S(2)}) collective-permute-start(f32[4,4,112,128]{3,2,1,0:T(8,128)S(1)} %get-tuple-element.135), channel_id=1, source_target_pairs={{0,2},{1,3},{2,0},{3,1},{4,20},{5,21},{6,22},{7,23},{8,10},{9,11},... | collective-permute-start | bytes 2752520 | tf_op jit(solution)/shard_map/ppermute | solution.py:752
  69.9 1.7 collective-permute-start.3
  71.6 23.6 %back.1 = (f32[20,50,384]{2,1,0:T(8,128)}, f32[4,4,4,112,128]{4,3,2,1,0:T(8,128)}, f32[4,4,4,112,128]{4,3,2,1,0:T(8,128)}) custom-call(s32[1]{0:T(128)} %bitcast.refs_0_, f32[2,512,384]{2,1,0:T(8,128)} %get-tuple-element.117.refs_1_, f32[2,4608]{1,0:T(2,128)S(1)} %copy-done.7, f32[1,128]{1,0:T(1,128)S(1)} %get-tuple-element.118.refs_3_, ...), custom_call_target="tpu_custom_call" | custom-call | tf_op jit(solution)/shard_map/back/pallas_call | solution.py:381
  95.2 0.0 collective-permute-done.2.refs_6_
  95.2 0.0 collective-permute-done.3.refs_7_
  95.2 1.3 collective-permute-start.4
  96.5 6.2 %collective-permute-done.4.got = f32[4,4,4,112,128]{4,3,2,1,0:T(8,128)S(1)} collective-permute-done((f32[4,4,4,112,128]{4,3,2,1,0:T(8,128)}, f32[4,4,4,112,128]{4,3,2,1,0:T(8,128)S(1)}, u32[]{:S(2)}, u32[]{:S(2)}) %collective-permute-start.4) | collective-permute-done | bytes 3670048 | tf_op jit(solution)/shard_map/ppermute | solution.py:757
  102.8 2.0 %copy-done = f32[4,4,4,112,128]{4,3,2,1,0:T(8,128)S(1)} copy-done((f32[4,4,4,112,128]{4,3,2,1,0:T(8,128)S(1)}, f32[4,4,4,112,128]{4,3,2,1,0:T(8,128)}, u32[]{:S(2)}) %copy-start) | copy-done | bytes 3670040
  104.8 1.0 add_core.3
  105.9 0.1 collective-permute-start.5
  106.0 2.4 %collective-permute-start.6 = (f32[4,4,112,128]{3,2,1,0:T(8,128)S(1)}, f32[4,4,112,128]{3,2,1,0:T(8,128)S(1)}, u32[]{:S(2)}, u32[]{:S(2)}) collective-permute-start(f32[4,4,112,128]{3,2,1,0:T(8,128)S(1)} %get-tuple-element.140), channel_id=1, source_target_pairs={{0,2},{1,3},{2,0},{3,1},{4,20},{5,21},{6,22},{7,23},{8,10},{9,11},... | collective-permute-start | bytes 2752520 | tf_op jit(solution)/shard_map/ppermute | solution.py:752
  108.4 1.4 collective-permute-start.7
  109.8 8.7 %collective-permute-done.5.refs_1_ = f32[4,4,112,128]{3,2,1,0:T(8,128)S(1)} collective-permute-done((f32[4,4,112,128]{3,2,1,0:T(8,128)S(1)}, f32[4,4,112,128]{3,2,1,0:T(8,128)S(1)}, u32[]{:S(2)}, u32[]{:S(2)}) %collective-permute-start.5) | collective-permute-done | bytes 917536 | tf_op jit(solution)/shard_map/ppermute | solution.py:752
  118.5 10.9 %collective-permute-done.6.refs_2_ = f32[4,4,112,128]{3,2,1,0:T(8,128)S(1)} collective-permute-done((f32[4,4,112,128]{3,2,1,0:T(8,128)S(1)}, f32[4,4,112,128]{3,2,1,0:T(8,128)S(1)}, u32[]{:S(2)}, u32[]{:S(2)}) %collective-permute-start.6) | collective-permute-done | bytes 917536 | tf_op jit(solution)/shard_map/ppermute | solution.py:752
  129.3 2.6 %collective-permute-done.7.refs_3_ = f32[4,4,112,128]{3,2,1,0:T(8,128)S(1)} collective-permute-done((f32[4,4,112,128]{3,2,1,0:T(8,128)S(1)}, f32[4,4,112,128]{3,2,1,0:T(8,128)S(1)}, u32[]{:S(2)}, u32[]{:S(2)}) %collective-permute-start.7) | collective-permute-done | bytes 917536 | tf_op jit(solution)/shard_map/ppermute | solution.py:752
  132.0 0.4 add_first.1
  132.4 0.1 collective-permute-start.8
  132.5 3.4 %collective-permute-start.9 = (f32[4,2,112,128]{3,2,1,0:T(8,128)S(1)}, f32[4,2,112,128]{3,2,1,0:T(8,128)S(1)}, u32[]{:S(2)}, u32[]{:S(2)}) collective-permute-start(f32[4,2,112,128]{3,2,1,0:T(8,128)S(1)} %get-tuple-element.148), channel_id=1, source_target_pairs={{0,16},{1,17},{2,18},{3,19},{4,6},{5,7},{6,4},{7,5},{8,24},{9,25},... | collective-permute-start | bytes 1376264 | tf_op jit(solution)/shard_map/ppermute | solution.py:752
  135.9 0.5 collective-permute-start.10
  136.4 0.9 constant_dynamic-slice_fusion.4
  137.3 2.8 %collective-permute-done.8.one = f32[4,2,112,128]{3,2,1,0:T(8,128)S(1)} collective-permute-done((f32[4,2,112,128]{3,2,1,0:T(8,128)S(1)}, f32[4,2,112,128]{3,2,1,0:T(8,128)S(1)}, u32[]{:S(2)}, u32[]{:S(2)}) %collective-permute-start.8) | collective-permute-done | bytes 458784 | tf_op jit(solution)/shard_map/ppermute | solution.py:752
  140.1 6.9 %collective-permute-done.9.two = f32[4,2,112,128]{3,2,1,0:T(8,128)S(1)} collective-permute-done((f32[4,2,112,128]{3,2,1,0:T(8,128)S(1)}, f32[4,2,112,128]{3,2,1,0:T(8,128)S(1)}, u32[]{:S(2)}, u32[]{:S(2)}) %collective-permute-start.9) | collective-permute-done | bytes 458784 | tf_op jit(solution)/shard_map/ppermute | solution.py:752
  147.0 2.6 %collective-permute-done.10.three = f32[4,2,112,128]{3,2,1,0:T(8,128)S(1)} collective-permute-done((f32[4,2,112,128]{3,2,1,0:T(8,128)S(1)}, f32[4,2,112,128]{3,2,1,0:T(8,128)S(1)}, u32[]{:S(2)}, u32[]{:S(2)}) %collective-permute-start.10) | collective-permute-done | bytes 458784 | tf_op jit(solution)/shard_map/ppermute | solution.py:752
  149.7 0.1 add_second.1
  149.7 2.8 %collective-permute-start.11 = (f32[2,112,128]{2,1,0:T(8,128)S(1)}, f32[2,112,128]{2,1,0:T(8,128)S(1)}, u32[]{:S(2)}, u32[]{:S(2)}) collective-permute-start(f32[2,112,128]{2,1,0:T(8,128)S(1)} %get-tuple-element.151), channel_id=1, source_target_pairs={{0,32},{1,33},{2,34},{3,35},{4,36},{5,37},{6,38},{7,39},{8,40},{9,... | collective-permute-start | bytes 344072 | tf_op jit(solution)/shard_map/ppermute | solution.py:752
  152.5 5.1 %collective-permute-start.12 = (f32[2,112,128]{2,1,0:T(8,128)S(1)}, f32[2,112,128]{2,1,0:T(8,128)S(1)}, u32[]{:S(2)}, u32[]{:S(2)}) collective-permute-start(f32[2,112,128]{2,1,0:T(8,128)S(1)} %get-tuple-element.152), channel_id=1, source_target_pairs={{0,64},{1,65},{2,66},{3,67},{4,68},{5,69},{6,70},{7,71},{8,72},{9,... | collective-permute-start | bytes 344072 | tf_op jit(solution)/shard_map/ppermute | solution.py:752
  157.6 0.9 constant_dynamic-slice_fusion.2
  158.6 0.9 constant_dynamic-slice_fusion.1
  159.5 0.0 collective-permute-done.11.one
  159.5 1.6 collective-permute-done.12.two
  161.2 6.1 %collective-permute-done.13.three = f32[2,112,128]{2,1,0:T(8,128)S(1)} collective-permute-done((f32[2,112,128]{2,1,0:T(8,128)S(1)}, f32[2,112,128]{2,1,0:T(8,128)S(1)}, u32[]{:S(2)}, u32[]{:S(2)}) %collective-permute-start.13) | collective-permute-done | bytes 114720 | tf_op jit(solution)/shard_map/ppermute | solution.py:752
  167.3 1.0 collective-permute-start.14
  168.2 0.8 constant_dynamic-slice_fusion.3
  169.0 0.6 copy.69
  169.7 0.6 copy.70
  170.3 0.6 copy.68
  170.9 0.6 copy.67
  171.5 0.6 constant_dynamic-slice_fusion.refs_6_
  172.2 0.6 copy-done.8
  172.8 2.3 %finish.1 = (f32[3,2,1152]{2,1,0:T(2,128)}, f32[3,2,384]{2,1,0:T(2,128)}, f32[3,2,1536]{2,1,0:T(2,128)}, f32[12,2,384]{2,1,0:T(2,128)}, f32[2,36]{1,0:T(2,128)},...) custom-call(f32[2,112,128]{2,1,0:T(8,128)} %copy-done.5, ...), custom_call_target="tpu_custom_call" | custom-call | tf_op jit(solution)/shard_map/finish/pallas_call | solution.py:841
  (17 shorter events, 0.1 us)
Async XLA Ops:
  0.7 1.2 copy-start.4
  1.9 0.8 copy-start.6
  55.0 9.6 %collective-permute-start = (f32[4,4,4,112,128]{4,3,2,1,0:T(8,128)}, f32[4,4,4,112,128]{4,3,2,1,0:T(8,128)S(1)}, u32[]{:S(2)}, u32[]{:S(2)}) collective-permute-start(f32[4,4,4,112,128]{4,3,2,1,0:T(8,128)} %get-tuple-element.112), channel_id=1, source_target_pairs={{0,4},{1,5},{2,6},{3,7},{4,0},{5,1},{6,2},{7,3},{8,12},{9,13},{10,... | collective-permute-start | bytes 11010056 | tf_op jit(solution)/shard_map/ppermute | solution.py:757
  64.6 2.0 %copy-start.1 = (f32[4,4,4,112,128]{4,3,2,1,0:T(8,128)S(1)}, f32[4,4,4,112,128]{4,3,2,1,0:T(8,128)}, u32[]{:S(2)}) copy-start(f32[4,4,4,112,128]{4,3,2,1,0:T(8,128)} %get-tuple-element.111.keep) | copy-start | bytes 11010052
  66.6 5.0 %copy-start.2 = (bf16[20,3,64,128]{3,2,1,0:T(8,128)(2,1)S(1)}, bf16[20,3,64,128]{3,2,1,0:T(8,128)(2,1)}, u32[]{:S(2)}) copy-start(bf16[20,3,64,128]{3,2,1,0:T(8,128)(2,1)} %get-tuple-element.124.refs_9_) | copy-start | bytes 2949124
  66.6 5.0 %copy-start.3 = (bf16[1,384,1152]{2,1,0:T(8,128)(2,1)S(1)}, bf16[1,384,1152]{2,1,0:T(8,128)(2,1)}, u32[]{:S(2)}) copy-start(bf16[1,384,1152]{2,1,0:T(8,128)(2,1)} %get-tuple-element.119.refs_4_) | copy-start | bytes 2654212
  66.6 5.0 %copy-start.7 = (f32[2,4608]{1,0:T(2,128)S(1)}, f32[2,4608]{1,0:T(2,128)}, u32[]{:S(2)}) copy-start(f32[2,4608]{1,0:T(2,128)} %refs_2_.3) | copy-start | bytes 110596
  67.7 27.5 %collective-permute-start.1 = (f32[4,4,112,128]{3,2,1,0:T(8,128)S(1)}, f32[4,4,112,128]{3,2,1,0:T(8,128)S(1)}, u32[]{:S(2)}, u32[]{:S(2)}) collective-permute-start(f32[4,4,112,128]{3,2,1,0:T(8,128)S(1)} %get-tuple-element.134), channel_id=1, source_target_pairs={{0,1},{1,0},{2,3},{3,2},{4,12},{5,13},{6,14},{7,15},{8,9},{9,8},{1... | collective-permute-start | bytes 2752520 | tf_op jit(solution)/shard_map/ppermute | solution.py:752
  67.8 27.4 %collective-permute-start.2 = (f32[4,4,112,128]{3,2,1,0:T(8,128)S(1)}, f32[4,4,112,128]{3,2,1,0:T(8,128)S(1)}, u32[]{:S(2)}, u32[]{:S(2)}) collective-permute-start(f32[4,4,112,128]{3,2,1,0:T(8,128)S(1)} %get-tuple-element.135), channel_id=1, source_target_pairs={{0,2},{1,3},{2,0},{3,1},{4,20},{5,21},{6,22},{7,23},{8,10},{9,11},... | collective-permute-start | bytes 2752520 | tf_op jit(solution)/shard_map/ppermute | solution.py:752
  69.9 25.3 %collective-permute-start.3 = (f32[4,4,112,128]{3,2,1,0:T(8,128)S(1)}, f32[4,4,112,128]{3,2,1,0:T(8,128)S(1)}, u32[]{:S(2)}, u32[]{:S(2)}) collective-permute-start(f32[4,4,112,128]{3,2,1,0:T(8,128)S(1)} %get-tuple-element.136), channel_id=1, source_target_pairs={{0,3},{1,2},{2,1},{3,0},{4,28},{5,29},{6,30},{7,31},{8,11},{9,10},... | collective-permute-start | bytes 2752520 | tf_op jit(solution)/shard_map/ppermute | solution.py:752
  95.2 7.5 %collective-permute-start.4 = (f32[4,4,4,112,128]{4,3,2,1,0:T(8,128)}, f32[4,4,4,112,128]{4,3,2,1,0:T(8,128)S(1)}, u32[]{:S(2)}, u32[]{:S(2)}) collective-permute-start(f32[4,4,4,112,128]{4,3,2,1,0:T(8,128)} %get-tuple-element.137), channel_id=1, source_target_pairs={{0,4},{1,5},{2,6},{3,7},{4,0},{5,1},{6,2},{7,3},{8,12},{9,13},{10,... | collective-permute-start | bytes 11010056 | tf_op jit(solution)/shard_map/ppermute | solution.py:757
  102.8 2.0 %copy-start = (f32[4,4,4,112,128]{4,3,2,1,0:T(8,128)S(1)}, f32[4,4,4,112,128]{4,3,2,1,0:T(8,128)}, u32[]{:S(2)}) copy-start(f32[4,4,4,112,128]{4,3,2,1,0:T(8,128)} %get-tuple-element.131.keep) | copy-start | bytes 11010052
  105.9 12.6 %collective-permute-start.5 = (f32[4,4,112,128]{3,2,1,0:T(8,128)S(1)}, f32[4,4,112,128]{3,2,1,0:T(8,128)S(1)}, u32[]{:S(2)}, u32[]{:S(2)}) collective-permute-start(f32[4,4,112,128]{3,2,1,0:T(8,128)S(1)} %get-tuple-element.139), channel_id=1, source_target_pairs={{0,1},{1,0},{2,3},{3,2},{4,12},{5,13},{6,14},{7,15},{8,9},{9,8},{1... | collective-permute-start | bytes 2752520 | tf_op jit(solution)/shard_map/ppermute | solution.py:752
  106.0 23.4 %collective-permute-start.6 = (f32[4,4,112,128]{3,2,1,0:T(8,128)S(1)}, f32[4,4,112,128]{3,2,1,0:T(8,128)S(1)}, u32[]{:S(2)}, u32[]{:S(2)}) collective-permute-start(f32[4,4,112,128]{3,2,1,0:T(8,128)S(1)} %get-tuple-element.140), channel_id=1, source_target_pairs={{0,2},{1,3},{2,0},{3,1},{4,20},{5,21},{6,22},{7,23},{8,10},{9,11},... | collective-permute-start | bytes 2752520 | tf_op jit(solution)/shard_map/ppermute | solution.py:752
  108.4 23.6 %collective-permute-start.7 = (f32[4,4,112,128]{3,2,1,0:T(8,128)S(1)}, f32[4,4,112,128]{3,2,1,0:T(8,128)S(1)}, u32[]{:S(2)}, u32[]{:S(2)}) collective-permute-start(f32[4,4,112,128]{3,2,1,0:T(8,128)S(1)} %get-tuple-element.141), channel_id=1, source_target_pairs={{0,3},{1,2},{2,1},{3,0},{4,28},{5,29},{6,30},{7,31},{8,11},{9,10},... | collective-permute-start | bytes 2752520 | tf_op jit(solution)/shard_map/ppermute | solution.py:752
  132.4 7.7 %collective-permute-start.8 = (f32[4,2,112,128]{3,2,1,0:T(8,128)S(1)}, f32[4,2,112,128]{3,2,1,0:T(8,128)S(1)}, u32[]{:S(2)}, u32[]{:S(2)}) collective-permute-start(f32[4,2,112,128]{3,2,1,0:T(8,128)S(1)} %get-tuple-element.147), channel_id=1, source_target_pairs={{0,8},{1,9},{2,10},{3,11},{4,5},{5,4},{6,7},{7,6},{8,0},{9,1},{10,... | collective-permute-start | bytes 1376264 | tf_op jit(solution)/shard_map/ppermute | solution.py:752
  132.5 14.5 %collective-permute-start.9 = (f32[4,2,112,128]{3,2,1,0:T(8,128)S(1)}, f32[4,2,112,128]{3,2,1,0:T(8,128)S(1)}, u32[]{:S(2)}, u32[]{:S(2)}) collective-permute-start(f32[4,2,112,128]{3,2,1,0:T(8,128)S(1)} %get-tuple-element.148), channel_id=1, source_target_pairs={{0,16},{1,17},{2,18},{3,19},{4,6},{5,7},{6,4},{7,5},{8,24},{9,25},... | collective-permute-start | bytes 1376264 | tf_op jit(solution)/shard_map/ppermute | solution.py:752
  135.9 13.8 %collective-permute-start.10 = (f32[4,2,112,128]{3,2,1,0:T(8,128)S(1)}, f32[4,2,112,128]{3,2,1,0:T(8,128)S(1)}, u32[]{:S(2)}, u32[]{:S(2)}) collective-permute-start(f32[4,2,112,128]{3,2,1,0:T(8,128)S(1)} %get-tuple-element.149), channel_id=1, source_target_pairs={{0,24},{1,25},{2,26},{3,27},{4,7},{5,6},{6,5},{7,4},{8,16},{9,17},... | collective-permute-start | bytes 1376264 | tf_op jit(solution)/shard_map/ppermute | solution.py:752
  149.7 9.8 %collective-permute-start.11 = (f32[2,112,128]{2,1,0:T(8,128)S(1)}, f32[2,112,128]{2,1,0:T(8,128)S(1)}, u32[]{:S(2)}, u32[]{:S(2)}) collective-permute-start(f32[2,112,128]{2,1,0:T(8,128)S(1)} %get-tuple-element.151), channel_id=1, source_target_pairs={{0,32},{1,33},{2,34},{3,35},{4,36},{5,37},{6,38},{7,39},{8,40},{9,... | collective-permute-start | bytes 344072 | tf_op jit(solution)/shard_map/ppermute | solution.py:752
  152.5 8.6 %collective-permute-start.12 = (f32[2,112,128]{2,1,0:T(8,128)S(1)}, f32[2,112,128]{2,1,0:T(8,128)S(1)}, u32[]{:S(2)}, u32[]{:S(2)}) collective-permute-start(f32[2,112,128]{2,1,0:T(8,128)S(1)} %get-tuple-element.152), channel_id=1, source_target_pairs={{0,64},{1,65},{2,66},{3,67},{4,68},{5,69},{6,70},{7,71},{8,72},{9,... | collective-permute-start | bytes 344072 | tf_op jit(solution)/shard_map/ppermute | solution.py:752
  157.6 9.6 %collective-permute-start.13 = (f32[2,112,128]{2,1,0:T(8,128)S(1)}, f32[2,112,128]{2,1,0:T(8,128)S(1)}, u32[]{:S(2)}, u32[]{:S(2)}) collective-permute-start(f32[2,112,128]{2,1,0:T(8,128)S(1)} %get-tuple-element.153), channel_id=1, source_target_pairs={{0,96},{1,97},{2,98},{3,99},{4,100},{5,101},{6,102},{7,103},{8,104... | collective-permute-start | bytes 344072 | tf_op jit(solution)/shard_map/ppermute | solution.py:752
  167.3 4.9 %copy-start.5 = (f32[2,112,128]{2,1,0:T(8,128)}, f32[2,112,128]{2,1,0:T(8,128)S(1)}, u32[]{:S(2)}) copy-start(f32[2,112,128]{2,1,0:T(8,128)S(1)} %add_third.1.refs_0_) | copy-start | bytes 344068
  167.3 4.9 %collective-permute-start.14 = (f32[2,112,128]{2,1,0:T(8,128)S(1)}, f32[2,112,128]{2,1,0:T(8,128)S(1)}, u32[]{:S(2)}, u32[]{:S(2)}) collective-permute-start(f32[2,112,128]{2,1,0:T(8,128)S(1)} %add_third.1.refs_0_), channel_id=1, source_target_pairs={{0,128},{128,0},{1,129},{129,1},{2,130},{130,2},{3,131},{131,3},{4... | collective-permute-start | bytes 344072 | tf_op jit(solution)/shard_map/ppermute | solution.py:768
  172.2 0.6 copy-start.8

commit v2 on v1

--- a/solution.py
+++ b/solution.py
@@ -263,11 +263,16 @@
             emit(own)
 
 
+HEADS_P, HEADS_A, MIXED, STREAM, MIDDLE, ACT, SLOPE, GRAD, ATTN, OUT, UP, DOWN = range(12)
+
+
 def back_mlp(r, grad):
+    r.ready(GRAD, DOWN)
     here = grad[0]
     r.acc_vec[:, BD : BD + D] += fold(here)
     r.low_grad[...] = here.astype(BF)
     r.hidden[...] = dot(r.low_grad[...], r.w_down[0], 1, 1)
+    r.ready(SLOPE)
     for column in range(0, FF, 256):
         total = jnp.zeros((8, 256), F32)
         for row in range(0, RUN, 32):
@@ -277,6 +282,7 @@
             r.d_hidden[at, column : column + 256] = part.astype(BF)
             total = total + fold(part)
         r.acc_vec[:, BU + column : BU + column + 256] += total
+    r.ready(UP, MIDDLE)
     d_normed = dot(r.d_hidden[...], r.w_up[0], 1, 1)
     unit, rate = normalise(r.middle[0])
     gain = bias(r, G2, B2)
@@ -284,6 +290,7 @@
     r.acc_vec[:, G2:B2] += fold(d_normed * unit)
     r.acc_vec[:, B2:BU] += fold(d_normed)
     r.d_mid[0] = grad[0] + norm_back(d_normed, unit, rate, gain)
+    r.ready(ACT)
     r.acc_down[...] = jnp.where(r.first, 0.0, r.acc_down[...]) + dot(r.act[0], r.low_grad[...], 0, 0)
     r.acc_up[...] = jnp.where(r.first, 0.0, r.acc_up[...]) + dot(r.normed[...], r.d_hidden[...], 0, 0)
 
@@ -292,6 +299,7 @@
     between = d_mid[0]
     r.acc_vec[:, BO:G2] += fold(between)
     r.d_branch[...] = between.astype(BF)
+    r.ready(OUT, MIXED)
     product = dot(r.d_branch[...], r.w_out[0], 1, 1)
     for block in range(3):
         r.d_heads[block, 0:RUN, :] = product[:, 128 * block : 128 * (block + 1)]
@@ -333,6 +341,7 @@
             d_proj[6 + pair, at, :] = d_value[0:SEQ]
         return carry
 
+    r.ready(HEADS_P, HEADS_A)
     lax.fori_loop(0, IMG // TOGETHER_BACK, attend, 0)
     for block in range(9):
         part = d_proj[block, 0:RUN, :]
@@ -341,6 +350,7 @@
             r.acc_vec[:, BQ + 128 * block : BQ + 128 * (block + 1)] += fold(part)
         if block >= 6:
             r.acc_vec[:, BV + 128 * (block - 6) : BV + 128 * (block - 5)] += fold(part)
+    r.ready(ATTN, STREAM)
     d_normed = dot(r.d_low[...], r.w_attn[0], 1, 1)
     unit, rate = normalise(r.stream[0])
     gain = bias(r, G1, B1)
@@ -471,6 +481,7 @@
 
     shared = dict(
         first=first,
+        ready=lambda *which: None,
         vec=r.vec,
         normed=r.normed,
         proj=r.proj,
@@ -606,7 +617,7 @@
     return call_kernel(front_kernel, ins, outs, scratch, FRONT_LIMIT, "front")
 
 
-FRONT_LIMIT = 52
+FRONT_LIMIT = 60
 
 
 def mlp_scratch():
@@ -633,17 +644,46 @@
 
 def back_kernel(r):
     step = pl.program_id(0)
-    r.layer = 0
-    r.first = step == 0
-
-    @pl.when(r.first)
+    first = step == 0
+    kept_in = [getattr(r, n + "_in") for n in Kept._fields] + [r.grad_in]
+    kept = [getattr(r, n) for n in Kept._fields] + [r.grad_all]
+    weights_in = [getattr(r, n + "_in") for n in Weights._fields]
+    weights = [getattr(r, n) for n in Weights._fields]
+
+    def load(k, chunk):
+        if k >= ATTN:
+            return pltpu.make_async_copy(weights_in[k - ATTN], weights[k - ATTN], r.sem.at[k, 0])
+        size = kept[k].shape[0] // CHUNKS
+        at = pl.ds(chunk * size, size)
+        return pltpu.make_async_copy(kept_in[k].at[at], kept[k].at[at], r.sem.at[k, chunk])
+
+    @pl.when(first)
     def _():
+        for chunk in range(CHUNKS):
+            for k in (GRAD, DOWN, SLOPE, UP, MIDDLE, ACT, OUT, MIXED, HEADS_P, HEADS_A, ATTN, STREAM):
+                if k < ATTN or chunk == 0:
+                    load(k, chunk).start()
         r.acc_vec[...] = jnp.zeros_like(r.acc_vec)
         for block in range(3):
             r.d_heads[block, RUN : RUN + 16, :] = jnp.zeros((16, 128), F32)
 
-    back_mlp(r, r.grad_in)
-    back_attention(r, r.d_mid, r.grad)
+    def ready(*which):
+        for k in which:
+            if k < ATTN:
+                load(k, step).wait()
+            else:
+
+                @pl.when(first)
+                def _():
+                    load(k, 0).wait()
+
+    views = {}
+    for n, ref in zip(Kept._fields, kept):
+        size = ref.shape[0] // CHUNKS
+        views[n] = ref.at[pl.ds(step * size, size)]
+    q = types.SimpleNamespace(**{**vars(r), **views}, layer=0, first=first, ready=ready)
+    back_mlp(q, r.grad_all.at[pl.ds(step, 1)])
+    back_attention(q, r.d_mid, r.grad)
     for image in range(IMG):
         r.grad_out[image] = r.grad[0, SEQ * image : SEQ * (image + 1), :]
 
@@ -658,42 +698,48 @@
     half = shape(F32, 4, 4, 4, ROWS, 128)
     ins = dict(
         core=(core, pl.BlockSpec(memory_space=pltpu.SMEM)),
-        grad_in=(grad, chunked(RUN, D)),
+        grad_in=(grad, ANYWHERE),
         vec=(vector, whole(2, 12 * D)),
         sums=(ahead.sums, whole(1, 128)),
     )
+    scratch = {}
     for n, size in zip(Weights._fields, WEIGHT_SIZES):
-        ins[n] = (getattr(ahead, n), held(1, *size))
-    for n, (dims, _) in KEPT_BLOCKS._asdict().items():
-        ins[n] = (getattr(ahead, n), imaged(*dims[1:]) if dims[0] == IMG else chunked(*dims[1:]))
+        ins[n + "_in"] = (getattr(ahead, n), ANYWHERE)
+        scratch[n] = pltpu.VMEM((1,) + size, BF)
+    for n, (dims, kind) in KEPT_BLOCKS._asdict().items():
+        ins[n + "_in"] = (getattr(ahead, n), ANYWHERE)
+        scratch[n] = pltpu.VMEM((CHUNKS * dims[0],) + dims[1:], kind)
     outs = dict(
         grad_out=(shape(F32, IMG * CHUNKS, SEQ, D), imaged(SEQ, D)),
         keep=(half, VMEM_WHOLE),
         send=(half, VMEM_WHOLE),
     )
-    scratch = dict(
+    scratch.update(
         **mlp_scratch(),
         **attention_scratch(),
+        grad_all=pltpu.VMEM((CHUNKS, RUN, D), F32),
         d_mid=pltpu.VMEM((1, RUN, D), F32),
         grad=pltpu.VMEM((1, RUN, D), F32),
         normed=pltpu.VMEM((RUN, D), BF),
         acc_vec=pltpu.VMEM((8, 12 * D), F32),
+        sem=pltpu.SemaphoreType.DMA((12, CHUNKS)),
     )
     return call_kernel(back_kernel, ins, outs, scratch, BACK_LIMIT, "back")
 
 
-BACK_LIMIT = 50
-
-
-def local_step(core, tokens, grad_out, masters, vector):
+BACK_LIMIT = 58
+
+
+def local_step(core, tokens, grad_out, masters, vector, shares):
     ahead = front(core, tokens, grad_out, masters, vector)
-    parts = add_core(ahead.keep, swap_core(ahead.send))
+    got, shares = lax.optimization_barrier((swap_core(ahead.send), shares))
+    parts = add_core(ahead.keep, got)
     grad, parts = lax.optimization_barrier((ahead.grad_out, parts))
     parts_one = ring(0, parts)
     back = back_call(core, grad, vector, ahead)
     send, parts_one = lax.optimization_barrier((back.send, parts_one))
     parts_zero = ring(0, add_core(back.keep, swap_core(send)))
-    return ahead.block_out, back.grad_out, parts_zero + parts_one
+    return ahead.block_out, back.grad_out, parts_zero + parts_one, shares
 
 
 def stage_position(stage):
@@ -703,14 +749,21 @@
     return jnp.where(core == stage, across, high)
 
 
-def add_core_kernel(keep, got, *outs):
+def add_core_kernel(keep, got, *refs):
+    outs, (local, sem) = refs[:4], refs[4:]
     me = stage_position(0)
+
+    def load(shift):
+        return pltpu.make_async_copy(keep.at[me ^ shift], local.at[shift], sem.at[shift])
+
     for shift in range(4):
-        at = me ^ shift
+        load(shift).start()
+    for shift in range(4):
+        load(shift).wait()
 
         @pl.loop(0, 16)
         def _(i):
-            outs[shift][i // 4, i % 4] = keep[at, i // 4, i % 4] + got[at, i // 4, i % 4]
+            outs[shift][i // 4, i % 4] = local[shift, i // 4, i % 4] + got[me ^ shift, i // 4, i % 4]
 
 
 def add_first_kernel(*refs):
@@ -749,7 +802,7 @@
 
 
 def ring(stage, parts):
-    got = [lax.ppermute(parts[s], GROUP_AXES, ring_pairs(stage, s)) for s in range(1, 4)]
+    got = [lax.ppermute(parts[s], GROUP_AXES, ring_pairs(stage, s)) for s in (2, 1, 3)]
     return [parts[0]] + got
 
 
@@ -758,7 +811,18 @@
 
 
 def add_core(keep, got):
-    return call_add(add_core_kernel, [keep, got], (4, 4, ROWS), 4, "add_core")
+    return pl.pallas_call(
+        add_core_kernel,
+        out_shape=[shape(F32, 4, 4, ROWS, 128)] * 4,
+        in_specs=[ANYWHERE, VMEM_WHOLE],
+        out_specs=[VMEM_WHOLE] * 4,
+        scratch_shapes=[
+            pltpu.VMEM((4, 4, 4, ROWS, 128), F32),
+            pltpu.SemaphoreType.DMA((4,)),
+        ],
+        compiler_params=pltpu.CompilerParams(vmem_limit_bytes=32 * 2**20),
+        name="add_core",
+    )(keep, got)
 
 
 def finish_sums(parts):
@@ -835,7 +899,7 @@
 
 
 def finish(own, other, weights, firsts, seconds, outers):
-    given = [rows_first(v) for v in (*weights, *firsts, *seconds, *outers)]
+    given = [*weights, *[rows_first(v) for v in (*firsts, *seconds, *outers)]]
     full = [jax.ShapeDtypeStruct(v.shape, jnp.float32) for v in given[:5]]
     low = [jax.ShapeDtypeStruct(v.shape, jnp.bfloat16) for v in given[:5]]
     results = pl.pallas_call(
@@ -884,15 +948,15 @@
     old_outers = (old_outer_qkv, old_outer_proj, old_outer_up, old_outer_down, old_outer_vector)
     owner_index = lax.axis_index(GROUP_AXES)
     core = jnp.reshape(owner_index // 4 % 2, (1,)).astype(jnp.int32)
-    block_out, grad_tokens, parts = local_step(
-        core, tokens, grad_out, masters[:4], weight_vector
-    )
     shares = []
     for kind_index in range(5):
         share_rows = old_firsts[kind_index].shape[1]
-        shares.append(
-            lax.dynamic_slice_in_dim(masters[kind_index], owner_index * share_rows, share_rows, 1)
-        )
+        at = owner_index * share_rows
+        share = lax.dynamic_slice_in_dim(masters[kind_index], at, share_rows, 1)
+        shares.append(rows_first(share))
+    block_out, grad_tokens, parts, shares = local_step(
+        core, tokens, grad_out, masters[:4], weight_vector, shares
+    )
     own, other = finish_sums(parts)
     results = finish(own, other, shares, old_firsts, old_seconds, old_outers)
     return (block_out, grad_tokens, *results)

time: 176 us -> 176 us (level)
  Pallas kernels: 80.9 us -> 88.5 us
  starting transfers between devices: 25.3 us -> 21.4 us
  waiting for transfers between devices: 54.8 us -> 52.1 us
    pallas_call x0 -> x2, Pallas kernels: none -> 6.82 us  [add_core(): pl.pallas_call(add_core_kernel, out_shape=[shape(F32, 4, 4, ROWS, 128)] *...]
    ppermute x2, waiting for transfers between devices: 12.5 us -> 6.25 us  [swap_core(): return lax.ppermute(send, GROUP_AXES, core_pairs())]
    ppermute x1, waiting for transfers between devices: 0.01 us -> 4.08 us  [finish_sums(): return (own, lax.ppermute(own, 'grp', [(0, 1), (1, 0)]))]
    pallas_call x2, Pallas kernels: 75.9 us -> 78.8 us  [call_kernel(): pl.pallas_call(lambda *refs: kernel(spaces(ins, outs, scratch, refs)), gr...]
    ppermute x12, starting transfers between devices: 19.7 us -> 17 us  [ring(): lax.ppermute(parts[s], GROUP_AXES, ring_pairs(stage, s))]
    pallas_call x5 -> x3, Pallas kernels: 2.65 us -> 0.55 us  [call_add(): pl.pallas_call(kernel, out_shape=[shape(F32, *out_dims, 128)] * count, in...]
    unnamed x22 -> x12, local copies, waits for them, and re-layouts: 9.12 us -> 7.18 us
  transfers between devices with their start and end apart: 15 -> 15, of which waited for: 10 -> 10; matrix products, arithmetic and copies ran while one was open for 4% -> 4% of each run, Pallas kernels for 13% -> 14%
where the time goes in v2:
time: 176 us; the launch traced here: 175 us
  Pallas kernels  88.5 us (50%)
  waiting for transfers between devices  52.1 us (30%)
  starting transfers between devices  21.4 us (12%)
  local copies, waits for them, and re-layouts  12 us (7%)
    pallas_call x2, Pallas kernels, call_kernel(): pl.pallas_call(lambda *refs: kernel(spaces(ins, outs, scratch, refs)), gr...  78.8 us
    ppermute x12, waiting for transfers between devices, ring(): lax.ppermute(parts[s], GROUP_AXES, ring_pairs(stage, s))  41.8 us
    ppermute x12, starting transfers between devices, ring(): lax.ppermute(parts[s], GROUP_AXES, ring_pairs(stage, s))  17 us
    unnamed x12, local copies, waits for them, and re-layouts  7.18 us
    pallas_call x2, Pallas kernels, add_core(): pl.pallas_call(add_core_kernel, out_shape=[shape(F32, 4, 4, ROWS, 128)] *...  6.82 us
    ppermute x2, waiting for transfers between devices, swap_core(): return lax.ppermute(send, GROUP_AXES, core_pairs())  6.25 us
    dynamic_slice x5, local copies, waits for them, and re-layouts, body(): share = lax.dynamic_slice_in_dim(masters[kind_index], at, share_rows, 1)  4.85 us
    ppermute x2, starting transfers between devices, swap_core(): return lax.ppermute(send, GROUP_AXES, core_pairs())  4.29 us
  transfers between devices with their start and end apart: 15, of which 10 were waited for; matrix products, arithmetic and copies ran while one was open for 4% of the time, Pallas kernels for 14%

profile of v2, /device:TPU:1, one launch (start us, length us, event | category | flops | bytes accessed | tf_op | source)
XLA Modules:
  0.0 175.0 jit_solution(17401353444240212545)
XLA Ops:
  0.7 54.4 %front.1 = (bf16[20,9,64,128]{3,2,1,0:T(8,128)(2,1)}, bf16[20,3,64,128]{3,2,1,0:T(8,128)(2,1)}, bf16[2,512,384]{2,1,0:T(8,128)(2,1)}, f32[2,512,384]{2,1,0:T(8,1...) custom-call(s32[1]{0:T(128)} %bitcast.refs_0_, ...), custom_call_target="tpu_custom_call" | custom-call | tf_op jit(solution)/shard_map/front/pallas_call | solution.py:391
  55.1 3.3 %collective-permute-start = (f32[4,4,4,112,128]{4,3,2,1,0:T(8,128)}, f32[4,4,4,112,128]{4,3,2,1,0:T(8,128)}, u32[]{:S(2)}, u32[]{:S(2)}) collective-permute-start(f32[4,4,4,112,128]{4,3,2,1,0:T(8,128)} %get-tuple-element.118), channel_id=1, source_target_pairs={{0,4},{1,5},{2,6},{3,7},{4,0},{5,1},{6,2},{7,3},{8,12},{9,13},{10,... | collective-permute-start | bytes 11010056 | tf_op jit(solution)/shard_map/ppermute | solution.py:810
  58.4 0.8 constant_dynamic-slice_fusion.3
  59.2 0.6 copy.70
  59.8 0.9 constant_dynamic-slice_fusion.4
  60.8 0.6 copy.69
  61.4 0.9 constant_dynamic-slice_fusion.2
  62.3 0.6 copy.68
  62.9 0.9 constant_dynamic-slice_fusion.1
  63.8 0.6 copy.67
  64.5 1.3 constant_dynamic-slice_fusion.refs_6_
  65.7 0.0 collective-permute-done.got
  65.8 2.0 %copy-done = f32[4,4,4,112,128]{4,3,2,1,0:T(8,128)S(1)} copy-done((f32[4,4,4,112,128]{4,3,2,1,0:T(8,128)S(1)}, f32[4,4,4,112,128]{4,3,2,1,0:T(8,128)}, u32[]{:S(2)}) %copy-start) | copy-done | bytes 3670040
  67.8 4.9 %add_core.2 = (f32[4,4,112,128]{3,2,1,0:T(8,128)S(1)}, f32[4,4,112,128]{3,2,1,0:T(8,128)S(1)}, f32[4,4,112,128]{3,2,1,0:T(8,128)}, f32[4,4,112,128]{3,2,1,0:T(8,128)S(1)}) custom-call(f32[4,4,4,112,128]{4,3,2,1,0:T(8,128)S(1)} %copy-done, f32[4,4,4,112,128]{4,3,2,1,0:T(8,128)} %collective-permute-done.got), custom_call_target="tpu_custom_call" | custom-call | tf_op jit(solution)/shard_map/add_core/pallas_call | solution.py:814
  72.7 1.3 collective-permute-start.1
  73.9 0.4 collective-permute-start.2
  74.3 1.7 collective-permute-start.3
  76.0 24.4 %back.1 = (f32[20,50,384]{2,1,0:T(8,128)}, f32[4,4,4,112,128]{4,3,2,1,0:T(8,128)}, f32[4,4,4,112,128]{4,3,2,1,0:T(8,128)}) custom-call(s32[1]{0:T(128)} %bitcast.refs_0_, f32[2,512,384]{2,1,0:T(8,128)} %get-tuple-element.124.refs_1_, f32[2,4608]{1,0:T(2,128)} %refs_2_.3, f32[1,128]{1,0:T(1,128)} %get-tuple-element.125.refs_3_, ...), custom_call_target="tpu_custom_call" | custom-call | tf_op jit(solution)/shard_map/back/pallas_call | solution.py:391
  100.4 0.0 collective-permute-done.1.refs_5_
  100.4 0.0 collective-permute-done.2.refs_6_
  100.5 0.0 collective-permute-done.3.refs_7_
  100.5 1.0 collective-permute-start.4
  101.4 6.2 %collective-permute-done.4.got = f32[4,4,4,112,128]{4,3,2,1,0:T(8,128)S(1)} collective-permute-done((f32[4,4,4,112,128]{4,3,2,1,0:T(8,128)}, f32[4,4,4,112,128]{4,3,2,1,0:T(8,128)S(1)}, u32[]{:S(2)}, u32[]{:S(2)}) %collective-permute-start.4) | collective-permute-done | bytes 3670048 | tf_op jit(solution)/shard_map/ppermute | solution.py:810
  107.7 2.0 %copy-done.1 = f32[4,4,4,112,128]{4,3,2,1,0:T(8,128)S(1)} copy-done((f32[4,4,4,112,128]{4,3,2,1,0:T(8,128)S(1)}, f32[4,4,4,112,128]{4,3,2,1,0:T(8,128)}, u32[]{:S(2)}) %copy-start.1) | copy-done | bytes 3670040
  109.7 1.9 %add_core.3 = (f32[4,4,112,128]{3,2,1,0:T(8,128)S(1)}, f32[4,4,112,128]{3,2,1,0:T(8,128)S(1)}, f32[4,4,112,128]{3,2,1,0:T(8,128)S(1)}, f32[4,4,112,128]{3,2,1,0:T(8,128)S(1)}) custom-call(f32[4,4,4,112,128]{4,3,2,1,0:T(8,128)S(1)} %copy-done.1, f32[4,4,4,112,128]{4,3,2,1,0:T(8,128)S(1)} %collective-permute-done.4.got), custom_call_target="tpu_custom_call" | custom-call | tf_op jit(solution)/shard_map/add_core/pallas_call | solution.py:814
  111.7 1.3 collective-permute-start.5
  113.0 0.4 collective-permute-start.6
  113.4 1.6 collective-permute-start.7
  115.0 10.8 %collective-permute-done.5.refs_1_ = f32[4,4,112,128]{3,2,1,0:T(8,128)S(1)} collective-permute-done((f32[4,4,112,128]{3,2,1,0:T(8,128)S(1)}, f32[4,4,112,128]{3,2,1,0:T(8,128)S(1)}, u32[]{:S(2)}, u32[]{:S(2)}) %collective-permute-start.5) | collective-permute-done | bytes 917536 | tf_op jit(solution)/shard_map/ppermute | solution.py:805
  125.8 8.5 %collective-permute-done.6.refs_2_ = f32[4,4,112,128]{3,2,1,0:T(8,128)S(1)} collective-permute-done((f32[4,4,112,128]{3,2,1,0:T(8,128)S(1)}, f32[4,4,112,128]{3,2,1,0:T(8,128)S(1)}, u32[]{:S(2)}, u32[]{:S(2)}) %collective-permute-start.6) | collective-permute-done | bytes 917536 | tf_op jit(solution)/shard_map/ppermute | solution.py:805
  134.3 1.3 collective-permute-done.7.refs_3_
  135.6 0.4 add_first.1
  136.1 1.5 collective-permute-start.8
  137.5 0.3 collective-permute-start.9
  137.8 1.5 collective-permute-start.10
  139.4 5.9 %collective-permute-done.8.one = f32[4,2,112,128]{3,2,1,0:T(8,128)S(1)} collective-permute-done((f32[4,2,112,128]{3,2,1,0:T(8,128)S(1)}, f32[4,2,112,128]{3,2,1,0:T(8,128)S(1)}, u32[]{:S(2)}, u32[]{:S(2)}) %collective-permute-start.8) | collective-permute-done | bytes 458784 | tf_op jit(solution)/shard_map/ppermute | solution.py:805
  145.3 3.6 %collective-permute-done.9.two = f32[4,2,112,128]{3,2,1,0:T(8,128)S(1)} collective-permute-done((f32[4,2,112,128]{3,2,1,0:T(8,128)S(1)}, f32[4,2,112,128]{3,2,1,0:T(8,128)S(1)}, u32[]{:S(2)}, u32[]{:S(2)}) %collective-permute-start.9) | collective-permute-done | bytes 458784 | tf_op jit(solution)/shard_map/ppermute | solution.py:805
  149.0 1.2 collective-permute-done.10.three
  150.2 0.1 add_second.1
  150.3 5.8 %collective-permute-start.11 = (f32[2,112,128]{2,1,0:T(8,128)S(1)}, f32[2,112,128]{2,1,0:T(8,128)S(1)}, u32[]{:S(2)}, u32[]{:S(2)}) collective-permute-start(f32[2,112,128]{2,1,0:T(8,128)S(1)} %get-tuple-element.158), channel_id=1, source_target_pairs={{0,64},{1,65},{2,66},{3,67},{4,68},{5,69},{6,70},{7,71},{8,72},{9,... | collective-permute-start | bytes 344072 | tf_op jit(solution)/shard_map/ppermute | solution.py:805
  156.1 1.2 collective-permute-start.12
  157.3 1.1 collective-permute-done.11.one
  158.4 9.3 %collective-permute-done.12.two = f32[2,112,128]{2,1,0:T(8,128)S(1)} collective-permute-done((f32[2,112,128]{2,1,0:T(8,128)S(1)}, f32[2,112,128]{2,1,0:T(8,128)S(1)}, u32[]{:S(2)}, u32[]{:S(2)}) %collective-permute-start.12) | collective-permute-done | bytes 114720 | tf_op jit(solution)/shard_map/ppermute | solution.py:805
  167.6 0.0 collective-permute-done.13.three
  167.7 0.1 collective-permute-start.14
  167.8 4.1 %collective-permute-done.14.refs_1_ = f32[2,112,128]{2,1,0:T(8,128)S(1)} collective-permute-done((f32[2,112,128]{2,1,0:T(8,128)S(1)}, f32[2,112,128]{2,1,0:T(8,128)S(1)}, u32[]{:S(2)}, u32[]{:S(2)}) %collective-permute-start.14) | collective-permute-done | bytes 114720 | tf_op jit(solution)/shard_map/ppermute | solution.py:832
  171.9 0.6 copy-done.3
  172.5 2.3 %finish.1 = (f32[3,2,1152]{2,1,0:T(2,128)}, f32[3,2,384]{2,1,0:T(2,128)}, f32[3,2,1536]{2,1,0:T(2,128)}, f32[12,2,384]{2,1,0:T(2,128)}, f32[2,36]{1,0:T(2,128)},...) custom-call(f32[2,112,128]{2,1,0:T(8,128)} %copy-done.2, ...), custom_call_target="tpu_custom_call" | custom-call | tf_op jit(solution)/shard_map/finish/pallas_call | solution.py:905
  (7 shorter events, 0.0 us)
Async XLA Ops:
  55.1 10.7 %collective-permute-start = (f32[4,4,4,112,128]{4,3,2,1,0:T(8,128)}, f32[4,4,4,112,128]{4,3,2,1,0:T(8,128)}, u32[]{:S(2)}, u32[]{:S(2)}) collective-permute-start(f32[4,4,4,112,128]{4,3,2,1,0:T(8,128)} %get-tuple-element.118), channel_id=1, source_target_pairs={{0,4},{1,5},{2,6},{3,7},{4,0},{5,1},{6,2},{7,3},{8,12},{9,13},{10,... | collective-permute-start | bytes 11010056 | tf_op jit(solution)/shard_map/ppermute | solution.py:810
  65.7 2.0 %copy-start = (f32[4,4,4,112,128]{4,3,2,1,0:T(8,128)S(1)}, f32[4,4,4,112,128]{4,3,2,1,0:T(8,128)}, u32[]{:S(2)}) copy-start(f32[4,4,4,112,128]{4,3,2,1,0:T(8,128)} %get-tuple-element.117.keep) | copy-start | bytes 11010052
  72.7 27.8 %collective-permute-start.1 = (f32[4,4,112,128]{3,2,1,0:T(8,128)}, f32[4,4,112,128]{3,2,1,0:T(8,128)S(1)}, u32[]{:S(2)}, u32[]{:S(2)}) collective-permute-start(f32[4,4,112,128]{3,2,1,0:T(8,128)} %get-tuple-element.141), channel_id=1, source_target_pairs={{0,2},{1,3},{2,0},{3,1},{4,20},{5,21},{6,22},{7,23},{8,10},{9,11},... | collective-permute-start | bytes 2752520 | tf_op jit(solution)/shard_map/ppermute | solution.py:805
  73.9 26.5 %collective-permute-start.2 = (f32[4,4,112,128]{3,2,1,0:T(8,128)S(1)}, f32[4,4,112,128]{3,2,1,0:T(8,128)S(1)}, u32[]{:S(2)}, u32[]{:S(2)}) collective-permute-start(f32[4,4,112,128]{3,2,1,0:T(8,128)S(1)} %get-tuple-element.142), channel_id=1, source_target_pairs={{0,1},{1,0},{2,3},{3,2},{4,12},{5,13},{6,14},{7,15},{8,9},{9,8},{1... | collective-permute-start | bytes 2752520 | tf_op jit(solution)/shard_map/ppermute | solution.py:805
  74.3 26.1 %collective-permute-start.3 = (f32[4,4,112,128]{3,2,1,0:T(8,128)S(1)}, f32[4,4,112,128]{3,2,1,0:T(8,128)S(1)}, u32[]{:S(2)}, u32[]{:S(2)}) collective-permute-start(f32[4,4,112,128]{3,2,1,0:T(8,128)S(1)} %get-tuple-element.143), channel_id=1, source_target_pairs={{0,3},{1,2},{2,1},{3,0},{4,28},{5,29},{6,30},{7,31},{8,11},{9,10},... | collective-permute-start | bytes 2752520 | tf_op jit(solution)/shard_map/ppermute | solution.py:805
  100.5 7.2 %collective-permute-start.4 = (f32[4,4,4,112,128]{4,3,2,1,0:T(8,128)}, f32[4,4,4,112,128]{4,3,2,1,0:T(8,128)S(1)}, u32[]{:S(2)}, u32[]{:S(2)}) collective-permute-start(f32[4,4,4,112,128]{4,3,2,1,0:T(8,128)} %get-tuple-element.144), channel_id=1, source_target_pairs={{0,4},{1,5},{2,6},{3,7},{4,0},{5,1},{6,2},{7,3},{8,12},{9,13},{10,... | collective-permute-start | bytes 11010056 | tf_op jit(solution)/shard_map/ppermute | solution.py:810
  107.7 2.0 %copy-start.1 = (f32[4,4,4,112,128]{4,3,2,1,0:T(8,128)S(1)}, f32[4,4,4,112,128]{4,3,2,1,0:T(8,128)}, u32[]{:S(2)}) copy-start(f32[4,4,4,112,128]{4,3,2,1,0:T(8,128)} %get-tuple-element.138.keep) | copy-start | bytes 11010052
  111.7 14.2 %collective-permute-start.5 = (f32[4,4,112,128]{3,2,1,0:T(8,128)S(1)}, f32[4,4,112,128]{3,2,1,0:T(8,128)S(1)}, u32[]{:S(2)}, u32[]{:S(2)}) collective-permute-start(f32[4,4,112,128]{3,2,1,0:T(8,128)S(1)} %get-tuple-element.146), channel_id=1, source_target_pairs={{0,2},{1,3},{2,0},{3,1},{4,20},{5,21},{6,22},{7,23},{8,10},{9,11},... | collective-permute-start | bytes 2752520 | tf_op jit(solution)/shard_map/ppermute | solution.py:805
  113.0 21.3 %collective-permute-start.6 = (f32[4,4,112,128]{3,2,1,0:T(8,128)S(1)}, f32[4,4,112,128]{3,2,1,0:T(8,128)S(1)}, u32[]{:S(2)}, u32[]{:S(2)}) collective-permute-start(f32[4,4,112,128]{3,2,1,0:T(8,128)S(1)} %get-tuple-element.147), channel_id=1, source_target_pairs={{0,1},{1,0},{2,3},{3,2},{4,12},{5,13},{6,14},{7,15},{8,9},{9,8},{1... | collective-permute-start | bytes 2752520 | tf_op jit(solution)/shard_map/ppermute | solution.py:805
  113.4 22.2 %collective-permute-start.7 = (f32[4,4,112,128]{3,2,1,0:T(8,128)S(1)}, f32[4,4,112,128]{3,2,1,0:T(8,128)S(1)}, u32[]{:S(2)}, u32[]{:S(2)}) collective-permute-start(f32[4,4,112,128]{3,2,1,0:T(8,128)S(1)} %get-tuple-element.148), channel_id=1, source_target_pairs={{0,3},{1,2},{2,1},{3,0},{4,28},{5,29},{6,30},{7,31},{8,11},{9,10},... | collective-permute-start | bytes 2752520 | tf_op jit(solution)/shard_map/ppermute | solution.py:805
  136.1 9.3 %collective-permute-start.8 = (f32[4,2,112,128]{3,2,1,0:T(8,128)S(1)}, f32[4,2,112,128]{3,2,1,0:T(8,128)S(1)}, u32[]{:S(2)}, u32[]{:S(2)}) collective-permute-start(f32[4,2,112,128]{3,2,1,0:T(8,128)S(1)} %get-tuple-element.154), channel_id=1, source_target_pairs={{0,16},{1,17},{2,18},{3,19},{4,6},{5,7},{6,4},{7,5},{8,24},{9,25},... | collective-permute-start | bytes 1376264 | tf_op jit(solution)/shard_map/ppermute | solution.py:805
  137.5 11.4 %collective-permute-start.9 = (f32[4,2,112,128]{3,2,1,0:T(8,128)S(1)}, f32[4,2,112,128]{3,2,1,0:T(8,128)S(1)}, u32[]{:S(2)}, u32[]{:S(2)}) collective-permute-start(f32[4,2,112,128]{3,2,1,0:T(8,128)S(1)} %get-tuple-element.155), channel_id=1, source_target_pairs={{0,8},{1,9},{2,10},{3,11},{4,5},{5,4},{6,7},{7,6},{8,0},{9,1},{10,... | collective-permute-start | bytes 1376264 | tf_op jit(solution)/shard_map/ppermute | solution.py:805
  137.8 12.3 %collective-permute-start.10 = (f32[4,2,112,128]{3,2,1,0:T(8,128)S(1)}, f32[4,2,112,128]{3,2,1,0:T(8,128)S(1)}, u32[]{:S(2)}, u32[]{:S(2)}) collective-permute-start(f32[4,2,112,128]{3,2,1,0:T(8,128)S(1)} %get-tuple-element.156), channel_id=1, source_target_pairs={{0,24},{1,25},{2,26},{3,27},{4,7},{5,6},{6,5},{7,4},{8,16},{9,17},... | collective-permute-start | bytes 1376264 | tf_op jit(solution)/shard_map/ppermute | solution.py:805
  150.3 8.1 %collective-permute-start.11 = (f32[2,112,128]{2,1,0:T(8,128)S(1)}, f32[2,112,128]{2,1,0:T(8,128)S(1)}, u32[]{:S(2)}, u32[]{:S(2)}) collective-permute-start(f32[2,112,128]{2,1,0:T(8,128)S(1)} %get-tuple-element.158), channel_id=1, source_target_pairs={{0,64},{1,65},{2,66},{3,67},{4,68},{5,69},{6,70},{7,71},{8,72},{9,... | collective-permute-start | bytes 344072 | tf_op jit(solution)/shard_map/ppermute | solution.py:805
  156.1 11.6 %collective-permute-start.12 = (f32[2,112,128]{2,1,0:T(8,128)S(1)}, f32[2,112,128]{2,1,0:T(8,128)S(1)}, u32[]{:S(2)}, u32[]{:S(2)}) collective-permute-start(f32[2,112,128]{2,1,0:T(8,128)S(1)} %get-tuple-element.159), channel_id=1, source_target_pairs={{0,32},{1,33},{2,34},{3,35},{4,36},{5,37},{6,38},{7,39},{8,40},{9,... | collective-permute-start | bytes 344072 | tf_op jit(solution)/shard_map/ppermute | solution.py:805
  157.3 10.4 %collective-permute-start.13 = (f32[2,112,128]{2,1,0:T(8,128)S(1)}, f32[2,112,128]{2,1,0:T(8,128)S(1)}, u32[]{:S(2)}, u32[]{:S(2)}) collective-permute-start(f32[2,112,128]{2,1,0:T(8,128)S(1)} %get-tuple-element.160), channel_id=1, source_target_pairs={{0,96},{1,97},{2,98},{3,99},{4,100},{5,101},{6,102},{7,103},{8,104... | collective-permute-start | bytes 344072 | tf_op jit(solution)/shard_map/ppermute | solution.py:805
  167.7 4.2 %copy-start.2 = (f32[2,112,128]{2,1,0:T(8,128)}, f32[2,112,128]{2,1,0:T(8,128)S(1)}, u32[]{:S(2)}) copy-start(f32[2,112,128]{2,1,0:T(8,128)S(1)} %add_third.1.refs_0_) | copy-start | bytes 344068
  167.7 4.2 %collective-permute-start.14 = (f32[2,112,128]{2,1,0:T(8,128)S(1)}, f32[2,112,128]{2,1,0:T(8,128)S(1)}, u32[]{:S(2)}, u32[]{:S(2)}) collective-permute-start(f32[2,112,128]{2,1,0:T(8,128)S(1)} %add_third.1.refs_0_), channel_id=1, source_target_pairs={{0,128},{128,0},{1,129},{129,1},{2,130},{130,2},{3,131},{131,3},{4... | collective-permute-start | bytes 344072 | tf_op jit(solution)/shard_map/ppermute | solution.py:832
  171.8 0.6 copy-start.3

commit v3 on v2

--- a/solution.py
+++ b/solution.py
@@ -732,14 +732,15 @@
 
 def local_step(core, tokens, grad_out, masters, vector, shares):
     ahead = front(core, tokens, grad_out, masters, vector)
-    got, shares = lax.optimization_barrier((swap_core(ahead.send), shares))
+    got, early = lax.optimization_barrier((swap_core(ahead.send), shares[:2]))
     parts = add_core(ahead.keep, got)
     grad, parts = lax.optimization_barrier((ahead.grad_out, parts))
     parts_one = ring(0, parts)
     back = back_call(core, grad, vector, ahead)
     send, parts_one = lax.optimization_barrier((back.send, parts_one))
-    parts_zero = ring(0, add_core(back.keep, swap_core(send)))
-    return ahead.block_out, back.grad_out, parts_zero + parts_one, shares
+    got, late = lax.optimization_barrier((swap_core(send), shares[2:]))
+    parts_zero = ring(0, add_core(back.keep, got))
+    return ahead.block_out, back.grad_out, parts_zero + parts_one, early + late
 
 
 def stage_position(stage):
@@ -749,21 +750,14 @@
     return jnp.where(core == stage, across, high)
 
 
-def add_core_kernel(keep, got, *refs):
-    outs, (local, sem) = refs[:4], refs[4:]
+def add_core_kernel(keep, got, *outs):
     me = stage_position(0)
-
-    def load(shift):
-        return pltpu.make_async_copy(keep.at[me ^ shift], local.at[shift], sem.at[shift])
-
     for shift in range(4):
-        load(shift).start()
-    for shift in range(4):
-        load(shift).wait()
+        at = me ^ shift
 
         @pl.loop(0, 16)
         def _(i):
-            outs[shift][i // 4, i % 4] = local[shift, i // 4, i % 4] + got[me ^ shift, i // 4, i % 4]
+            outs[shift][i // 4, i % 4] = keep[at, i // 4, i % 4] + got[at, i // 4, i % 4]
 
 
 def add_first_kernel(*refs):
@@ -811,18 +805,7 @@
 
 
 def add_core(keep, got):
-    return pl.pallas_call(
-        add_core_kernel,
-        out_shape=[shape(F32, 4, 4, ROWS, 128)] * 4,
-        in_specs=[ANYWHERE, VMEM_WHOLE],
-        out_specs=[VMEM_WHOLE] * 4,
-        scratch_shapes=[
-            pltpu.VMEM((4, 4, 4, ROWS, 128), F32),
-            pltpu.SemaphoreType.DMA((4,)),
-        ],
-        compiler_params=pltpu.CompilerParams(vmem_limit_bytes=32 * 2**20),
-        name="add_core",
-    )(keep, got)
+    return call_add(add_core_kernel, [keep, got], (4, 4, ROWS), 4, "add_core")
 
 
 def finish_sums(parts):

time: 176 us -> 177 us (level)
    pallas_call x3 -> x5, Pallas kernels: 0.55 us -> 8.14 us  [call_add(): pl.pallas_call(kernel, out_shape=[shape(F32, *out_dims, 128)] * count, in...]
    pallas_call x2 -> x0, Pallas kernels: 6.82 us -> none  [add_core(): pl.pallas_call(add_core_kernel, out_shape=[shape(F32, 4, 4, ROWS, 128)] *...]
    unnamed x12 -> x16, local copies, waits for them, and re-layouts: 7.18 us -> 8.1 us
  transfers between devices with their start and end apart: 15 -> 15, of which waited for: 10 -> 11; matrix products, arithmetic and copies ran while one was open for 4% -> 4% of each run, Pallas kernels for 14% -> 14%
where the time goes in v3:
time: 177 us; the launch traced here: 176 us
  Pallas kernels  89.1 us (50%)
  waiting for transfers between devices  51.2 us (29%)
  starting transfers between devices  21.8 us (12%)
  local copies, waits for them, and re-layouts  12.9 us (7%)
    pallas_call x2, Pallas kernels, call_kernel(): pl.pallas_call(lambda *refs: kernel(spaces(ins, outs, scratch, refs)), gr...  78.6 us
    ppermute x12, waiting for transfers between devices, ring(): lax.ppermute(parts[s], GROUP_AXES, ring_pairs(stage, s))  41.7 us
    ppermute x12, starting transfers between devices, ring(): lax.ppermute(parts[s], GROUP_AXES, ring_pairs(stage, s))  17.1 us
    pallas_call x5, Pallas kernels, call_add(): pl.pallas_call(kernel, out_shape=[shape(F32, *out_dims, 128)] * count, in...  8.14 us
    unnamed x16, local copies, waits for them, and re-layouts  8.1 us
    ppermute x2, waiting for transfers between devices, swap_core(): return lax.ppermute(send, GROUP_AXES, core_pairs())  5.44 us
    dynamic_slice x5, local copies, waits for them, and re-layouts, body(): share = lax.dynamic_slice_in_dim(masters[kind_index], at, share_rows, 1)  4.83 us
    ppermute x2, starting transfers between devices, swap_core(): return lax.ppermute(send, GROUP_AXES, core_pairs())  4.55 us
  transfers between devices with their start and end apart: 15, of which 11 were waited for; matrix products, arithmetic and copies ran while one was open for 4% of the time, Pallas kernels for 14%

profile of v3, /device:TPU:1, one launch (start us, length us, event | category | flops | bytes accessed | tf_op | source)
XLA Modules:
  0.0 176.0 jit_solution(8284634342022852403)
XLA Ops:
  0.7 54.3 %front.1 = (bf16[20,9,64,128]{3,2,1,0:T(8,128)(2,1)}, bf16[20,3,64,128]{3,2,1,0:T(8,128)(2,1)}, bf16[2,512,384]{2,1,0:T(8,128)(2,1)}, f32[2,512,384]{2,1,0:T(8,1...) custom-call(s32[1]{0:T(128)} %bitcast.refs_0_, ...), custom_call_target="tpu_custom_call" | custom-call | tf_op jit(solution)/shard_map/front/pallas_call | solution.py:391
  55.1 3.3 %collective-permute-start = (f32[4,4,4,112,128]{4,3,2,1,0:T(8,128)}, f32[4,4,4,112,128]{4,3,2,1,0:T(8,128)}, u32[]{:S(2)}, u32[]{:S(2)}) collective-permute-start(f32[4,4,4,112,128]{4,3,2,1,0:T(8,128)} %get-tuple-element.119), channel_id=1, source_target_pairs={{0,4},{1,5},{2,6},{3,7},{4,0},{5,1},{6,2},{7,3},{8,12},{9,13},{10,... | collective-permute-start | bytes 11010056 | tf_op jit(solution)/shard_map/ppermute | solution.py:804
  58.4 0.9 constant_dynamic-slice_fusion.4
  59.3 0.6 copy.69
  59.9 0.8 constant_dynamic-slice_fusion.3
  60.7 0.6 copy.70
  61.3 3.4 %collective-permute-done.got = f32[4,4,4,112,128]{4,3,2,1,0:T(8,128)} collective-permute-done((f32[4,4,4,112,128]{4,3,2,1,0:T(8,128)}, f32[4,4,4,112,128]{4,3,2,1,0:T(8,128)}, u32[]{:S(2)}, u32[]{:S(2)}) %collective-permute-start) | collective-permute-done | bytes 3670048 | tf_op jit(solution)/shard_map/ppermute | solution.py:804
  64.8 2.0 %copy-done.1 = f32[4,4,4,112,128]{4,3,2,1,0:T(8,128)S(1)} copy-done((f32[4,4,4,112,128]{4,3,2,1,0:T(8,128)S(1)}, f32[4,4,4,112,128]{4,3,2,1,0:T(8,128)}, u32[]{:S(2)}) %copy-start.1) | copy-done | bytes 3670040
  66.8 4.4 %add_core.2 = (f32[4,4,112,128]{3,2,1,0:T(8,128)S(1)}, f32[4,4,112,128]{3,2,1,0:T(8,128)}, f32[4,4,112,128]{3,2,1,0:T(8,128)}, f32[4,4,112,128]{3,2,1,0:T(8,128)S(1)}) custom-call(f32[4,4,4,112,128]{4,3,2,1,0:T(8,128)S(1)} %copy-done.1, f32[4,4,4,112,128]{4,3,2,1,0:T(8,128)} %collective-permute-done.got), custom_call_target="tpu_custom_call" | custom-call | tf_op jit(solution)/shard_map/add_core/pallas_call | solution.py:788
  71.2 1.2 collective-permute-start.1
  72.4 0.4 collective-permute-start.2
  72.8 1.7 collective-permute-start.3
  74.5 24.3 %back.1 = (f32[20,50,384]{2,1,0:T(8,128)}, f32[4,4,4,112,128]{4,3,2,1,0:T(8,128)}, f32[4,4,4,112,128]{4,3,2,1,0:T(8,128)}) custom-call(s32[1]{0:T(128)} %bitcast.refs_0_, f32[2,512,384]{2,1,0:T(8,128)} %get-tuple-element.125.refs_1_, f32[2,4608]{1,0:T(2,128)} %refs_2_.3, f32[1,128]{1,0:T(1,128)} %get-tuple-element.126.refs_3_, ...), custom_call_target="tpu_custom_call" | custom-call | tf_op jit(solution)/shard_map/back/pallas_call | solution.py:391
  98.8 0.0 collective-permute-done.1.refs_5_
  98.8 0.0 collective-permute-done.2.refs_6_
  98.8 0.0 collective-permute-done.3.refs_7_
  98.8 0.9 copy-done.2
  99.7 1.2 collective-permute-start.4
  101.0 0.9 constant_dynamic-slice_fusion.2
  101.9 0.6 copy.68
  102.5 0.9 constant_dynamic-slice_fusion.1
  103.4 0.6 copy.67
  104.1 1.3 constant_dynamic-slice_fusion.refs_6_
  105.3 2.0 %collective-permute-done.4.got = f32[4,4,4,112,128]{4,3,2,1,0:T(8,128)} collective-permute-done((f32[4,4,4,112,128]{4,3,2,1,0:T(8,128)}, f32[4,4,4,112,128]{4,3,2,1,0:T(8,128)}, u32[]{:S(2)}, u32[]{:S(2)}) %collective-permute-start.4) | collective-permute-done | bytes 3670048 | tf_op jit(solution)/shard_map/ppermute | solution.py:804
  107.3 2.0 %copy-done = f32[4,4,4,112,128]{4,3,2,1,0:T(8,128)S(1)} copy-done((f32[4,4,4,112,128]{4,3,2,1,0:T(8,128)S(1)}, f32[4,4,4,112,128]{4,3,2,1,0:T(8,128)}, u32[]{:S(2)}) %copy-start) | copy-done | bytes 3670040
  109.4 3.2 %add_core.3 = (f32[4,4,112,128]{3,2,1,0:T(8,128)S(1)}, f32[4,4,112,128]{3,2,1,0:T(8,128)S(1)}, f32[4,4,112,128]{3,2,1,0:T(8,128)S(1)}, f32[4,4,112,128]{3,2,1,0:T(8,128)S(1)}) custom-call(f32[4,4,4,112,128]{4,3,2,1,0:T(8,128)S(1)} %copy-done, f32[4,4,4,112,128]{4,3,2,1,0:T(8,128)} %collective-permute-done.4.got), custom_call_target="tpu_custom_call" | custom-call | tf_op jit(solution)/shard_map/add_core/pallas_call | solution.py:788
  112.6 1.3 collective-permute-start.5
  113.9 0.4 collective-permute-start.6
  114.3 1.6 collective-permute-start.7
  115.9 10.8 %collective-permute-done.5.refs_1_ = f32[4,4,112,128]{3,2,1,0:T(8,128)S(1)} collective-permute-done((f32[4,4,112,128]{3,2,1,0:T(8,128)S(1)}, f32[4,4,112,128]{3,2,1,0:T(8,128)S(1)}, u32[]{:S(2)}, u32[]{:S(2)}) %collective-permute-start.5) | collective-permute-done | bytes 917536 | tf_op jit(solution)/shard_map/ppermute | solution.py:799
  126.7 8.5 %collective-permute-done.6.refs_2_ = f32[4,4,112,128]{3,2,1,0:T(8,128)S(1)} collective-permute-done((f32[4,4,112,128]{3,2,1,0:T(8,128)S(1)}, f32[4,4,112,128]{3,2,1,0:T(8,128)S(1)}, u32[]{:S(2)}, u32[]{:S(2)}) %collective-permute-start.6) | collective-permute-done | bytes 917536 | tf_op jit(solution)/shard_map/ppermute | solution.py:799
  135.2 1.3 collective-permute-done.7.refs_3_
  136.5 0.4 add_first.1
  137.0 1.7 collective-permute-start.8
  138.7 0.3 collective-permute-start.9
  139.0 1.5 collective-permute-start.10
  140.5 5.9 %collective-permute-done.8.one = f32[4,2,112,128]{3,2,1,0:T(8,128)S(1)} collective-permute-done((f32[4,2,112,128]{3,2,1,0:T(8,128)S(1)}, f32[4,2,112,128]{3,2,1,0:T(8,128)S(1)}, u32[]{:S(2)}, u32[]{:S(2)}) %collective-permute-start.8) | collective-permute-done | bytes 458784 | tf_op jit(solution)/shard_map/ppermute | solution.py:799
  146.4 3.6 %collective-permute-done.9.two = f32[4,2,112,128]{3,2,1,0:T(8,128)S(1)} collective-permute-done((f32[4,2,112,128]{3,2,1,0:T(8,128)S(1)}, f32[4,2,112,128]{3,2,1,0:T(8,128)S(1)}, u32[]{:S(2)}, u32[]{:S(2)}) %collective-permute-start.9) | collective-permute-done | bytes 458784 | tf_op jit(solution)/shard_map/ppermute | solution.py:799
  150.1 1.2 collective-permute-done.10.three
  151.3 0.1 add_second.1
  151.4 5.8 %collective-permute-start.11 = (f32[2,112,128]{2,1,0:T(8,128)S(1)}, f32[2,112,128]{2,1,0:T(8,128)S(1)}, u32[]{:S(2)}, u32[]{:S(2)}) collective-permute-start(f32[2,112,128]{2,1,0:T(8,128)S(1)} %get-tuple-element.160), channel_id=1, source_target_pairs={{0,64},{1,65},{2,66},{3,67},{4,68},{5,69},{6,70},{7,71},{8,72},{9,... | collective-permute-start | bytes 344072 | tf_op jit(solution)/shard_map/ppermute | solution.py:799
  157.2 1.2 collective-permute-start.12
  158.4 1.1 collective-permute-done.11.one
  159.5 9.2 %collective-permute-done.12.two = f32[2,112,128]{2,1,0:T(8,128)S(1)} collective-permute-done((f32[2,112,128]{2,1,0:T(8,128)S(1)}, f32[2,112,128]{2,1,0:T(8,128)S(1)}, u32[]{:S(2)}, u32[]{:S(2)}) %collective-permute-start.12) | collective-permute-done | bytes 114720 | tf_op jit(solution)/shard_map/ppermute | solution.py:799
  168.8 0.1 collective-permute-start.14
  168.9 4.0 %collective-permute-done.14.refs_1_ = f32[2,112,128]{2,1,0:T(8,128)S(1)} collective-permute-done((f32[2,112,128]{2,1,0:T(8,128)S(1)}, f32[2,112,128]{2,1,0:T(8,128)S(1)}, u32[]{:S(2)}, u32[]{:S(2)}) %collective-permute-start.14) | collective-permute-done | bytes 114720 | tf_op jit(solution)/shard_map/ppermute | solution.py:815
  172.9 0.6 copy-done.5
  173.5 2.3 %finish.1 = (f32[3,2,1152]{2,1,0:T(2,128)}, f32[3,2,384]{2,1,0:T(2,128)}, f32[3,2,1536]{2,1,0:T(2,128)}, f32[12,2,384]{2,1,0:T(2,128)}, f32[2,36]{1,0:T(2,128)},...) custom-call(f32[2,112,128]{2,1,0:T(8,128)} %copy-done.4, ...), custom_call_target="tpu_custom_call" | custom-call | tf_op jit(solution)/shard_map/finish/pallas_call | solution.py:888
  (11 shorter events, 0.0 us)
Async XLA Ops:
  55.1 9.7 %collective-permute-start = (f32[4,4,4,112,128]{4,3,2,1,0:T(8,128)}, f32[4,4,4,112,128]{4,3,2,1,0:T(8,128)}, u32[]{:S(2)}, u32[]{:S(2)}) collective-permute-start(f32[4,4,4,112,128]{4,3,2,1,0:T(8,128)} %get-tuple-element.119), channel_id=1, source_target_pairs={{0,4},{1,5},{2,6},{3,7},{4,0},{5,1},{6,2},{7,3},{8,12},{9,13},{10,... | collective-permute-start | bytes 11010056 | tf_op jit(solution)/shard_map/ppermute | solution.py:804
  64.8 2.0 %copy-start.1 = (f32[4,4,4,112,128]{4,3,2,1,0:T(8,128)S(1)}, f32[4,4,4,112,128]{4,3,2,1,0:T(8,128)}, u32[]{:S(2)}) copy-start(f32[4,4,4,112,128]{4,3,2,1,0:T(8,128)} %get-tuple-element.118.keep) | copy-start | bytes 11010052
  71.2 27.6 %collective-permute-start.1 = (f32[4,4,112,128]{3,2,1,0:T(8,128)}, f32[4,4,112,128]{3,2,1,0:T(8,128)S(1)}, u32[]{:S(2)}, u32[]{:S(2)}) collective-permute-start(f32[4,4,112,128]{3,2,1,0:T(8,128)} %get-tuple-element.142), channel_id=1, source_target_pairs={{0,2},{1,3},{2,0},{3,1},{4,20},{5,21},{6,22},{7,23},{8,10},{9,11},... | collective-permute-start | bytes 2752520 | tf_op jit(solution)/shard_map/ppermute | solution.py:799
  72.4 26.4 %collective-permute-start.2 = (f32[4,4,112,128]{3,2,1,0:T(8,128)}, f32[4,4,112,128]{3,2,1,0:T(8,128)S(1)}, u32[]{:S(2)}, u32[]{:S(2)}) collective-permute-start(f32[4,4,112,128]{3,2,1,0:T(8,128)} %get-tuple-element.143), channel_id=1, source_target_pairs={{0,1},{1,0},{2,3},{3,2},{4,12},{5,13},{6,14},{7,15},{8,9},{9,8},{1... | collective-permute-start | bytes 2752520 | tf_op jit(solution)/shard_map/ppermute | solution.py:799
  72.8 26.0 %collective-permute-start.3 = (f32[4,4,112,128]{3,2,1,0:T(8,128)S(1)}, f32[4,4,112,128]{3,2,1,0:T(8,128)S(1)}, u32[]{:S(2)}, u32[]{:S(2)}) collective-permute-start(f32[4,4,112,128]{3,2,1,0:T(8,128)S(1)} %get-tuple-element.144), channel_id=1, source_target_pairs={{0,3},{1,2},{2,1},{3,0},{4,28},{5,29},{6,30},{7,31},{8,11},{9,10},... | collective-permute-start | bytes 2752520 | tf_op jit(solution)/shard_map/ppermute | solution.py:799
  98.8 0.9 copy-start.2
  99.7 7.6 %collective-permute-start.4 = (f32[4,4,4,112,128]{4,3,2,1,0:T(8,128)}, f32[4,4,4,112,128]{4,3,2,1,0:T(8,128)}, u32[]{:S(2)}, u32[]{:S(2)}) collective-permute-start(f32[4,4,4,112,128]{4,3,2,1,0:T(8,128)} %get-tuple-element.145), channel_id=1, source_target_pairs={{0,4},{1,5},{2,6},{3,7},{4,0},{5,1},{6,2},{7,3},{8,12},{9,13},{10,... | collective-permute-start | bytes 11010056 | tf_op jit(solution)/shard_map/ppermute | solution.py:804
  107.3 2.0 %copy-start = (f32[4,4,4,112,128]{4,3,2,1,0:T(8,128)S(1)}, f32[4,4,4,112,128]{4,3,2,1,0:T(8,128)}, u32[]{:S(2)}) copy-start(f32[4,4,4,112,128]{4,3,2,1,0:T(8,128)} %get-tuple-element.139.keep) | copy-start | bytes 11010052
  109.4 27.1 %copy-start.3 = (f32[4,4,112,128]{3,2,1,0:T(8,128)S(1)}, f32[4,4,112,128]{3,2,1,0:T(8,128)}, u32[]{:S(2)}) copy-start(f32[4,4,112,128]{3,2,1,0:T(8,128)} %copy-done.2) | copy-start | bytes 2752516
  112.6 14.2 %collective-permute-start.5 = (f32[4,4,112,128]{3,2,1,0:T(8,128)S(1)}, f32[4,4,112,128]{3,2,1,0:T(8,128)S(1)}, u32[]{:S(2)}, u32[]{:S(2)}) collective-permute-start(f32[4,4,112,128]{3,2,1,0:T(8,128)S(1)} %get-tuple-element.148), channel_id=1, source_target_pairs={{0,2},{1,3},{2,0},{3,1},{4,20},{5,21},{6,22},{7,23},{8,10},{9,11},... | collective-permute-start | bytes 2752520 | tf_op jit(solution)/shard_map/ppermute | solution.py:799
  113.9 21.3 %collective-permute-start.6 = (f32[4,4,112,128]{3,2,1,0:T(8,128)S(1)}, f32[4,4,112,128]{3,2,1,0:T(8,128)S(1)}, u32[]{:S(2)}, u32[]{:S(2)}) collective-permute-start(f32[4,4,112,128]{3,2,1,0:T(8,128)S(1)} %get-tuple-element.149), channel_id=1, source_target_pairs={{0,1},{1,0},{2,3},{3,2},{4,12},{5,13},{6,14},{7,15},{8,9},{9,8},{1... | collective-permute-start | bytes 2752520 | tf_op jit(solution)/shard_map/ppermute | solution.py:799
  114.3 22.2 %collective-permute-start.7 = (f32[4,4,112,128]{3,2,1,0:T(8,128)S(1)}, f32[4,4,112,128]{3,2,1,0:T(8,128)S(1)}, u32[]{:S(2)}, u32[]{:S(2)}) collective-permute-start(f32[4,4,112,128]{3,2,1,0:T(8,128)S(1)} %get-tuple-element.150), channel_id=1, source_target_pairs={{0,3},{1,2},{2,1},{3,0},{4,28},{5,29},{6,30},{7,31},{8,11},{9,10},... | collective-permute-start | bytes 2752520 | tf_op jit(solution)/shard_map/ppermute | solution.py:799
  137.0 9.5 %collective-permute-start.8 = (f32[4,2,112,128]{3,2,1,0:T(8,128)S(1)}, f32[4,2,112,128]{3,2,1,0:T(8,128)S(1)}, u32[]{:S(2)}, u32[]{:S(2)}) collective-permute-start(f32[4,2,112,128]{3,2,1,0:T(8,128)S(1)} %get-tuple-element.156), channel_id=1, source_target_pairs={{0,16},{1,17},{2,18},{3,19},{4,6},{5,7},{6,4},{7,5},{8,24},{9,25},... | collective-permute-start | bytes 1376264 | tf_op jit(solution)/shard_map/ppermute | solution.py:799
  138.7 11.4 %collective-permute-start.9 = (f32[4,2,112,128]{3,2,1,0:T(8,128)S(1)}, f32[4,2,112,128]{3,2,1,0:T(8,128)S(1)}, u32[]{:S(2)}, u32[]{:S(2)}) collective-permute-start(f32[4,2,112,128]{3,2,1,0:T(8,128)S(1)} %get-tuple-element.157), channel_id=1, source_target_pairs={{0,8},{1,9},{2,10},{3,11},{4,5},{5,4},{6,7},{7,6},{8,0},{9,1},{10,... | collective-permute-start | bytes 1376264 | tf_op jit(solution)/shard_map/ppermute | solution.py:799
  139.0 12.3 %collective-permute-start.10 = (f32[4,2,112,128]{3,2,1,0:T(8,128)S(1)}, f32[4,2,112,128]{3,2,1,0:T(8,128)S(1)}, u32[]{:S(2)}, u32[]{:S(2)}) collective-permute-start(f32[4,2,112,128]{3,2,1,0:T(8,128)S(1)} %get-tuple-element.158), channel_id=1, source_target_pairs={{0,24},{1,25},{2,26},{3,27},{4,7},{5,6},{6,5},{7,4},{8,16},{9,17},... | collective-permute-start | bytes 1376264 | tf_op jit(solution)/shard_map/ppermute | solution.py:799
  151.4 8.1 %collective-permute-start.11 = (f32[2,112,128]{2,1,0:T(8,128)S(1)}, f32[2,112,128]{2,1,0:T(8,128)S(1)}, u32[]{:S(2)}, u32[]{:S(2)}) collective-permute-start(f32[2,112,128]{2,1,0:T(8,128)S(1)} %get-tuple-element.160), channel_id=1, source_target_pairs={{0,64},{1,65},{2,66},{3,67},{4,68},{5,69},{6,70},{7,71},{8,72},{9,... | collective-permute-start | bytes 344072 | tf_op jit(solution)/shard_map/ppermute | solution.py:799
  157.2 11.5 %collective-permute-start.12 = (f32[2,112,128]{2,1,0:T(8,128)S(1)}, f32[2,112,128]{2,1,0:T(8,128)S(1)}, u32[]{:S(2)}, u32[]{:S(2)}) collective-permute-start(f32[2,112,128]{2,1,0:T(8,128)S(1)} %get-tuple-element.161), channel_id=1, source_target_pairs={{0,32},{1,33},{2,34},{3,35},{4,36},{5,37},{6,38},{7,39},{8,40},{9,... | collective-permute-start | bytes 344072 | tf_op jit(solution)/shard_map/ppermute | solution.py:799
  158.4 10.3 %collective-permute-start.13 = (f32[2,112,128]{2,1,0:T(8,128)S(1)}, f32[2,112,128]{2,1,0:T(8,128)S(1)}, u32[]{:S(2)}, u32[]{:S(2)}) collective-permute-start(f32[2,112,128]{2,1,0:T(8,128)S(1)} %get-tuple-element.162), channel_id=1, source_target_pairs={{0,96},{1,97},{2,98},{3,99},{4,100},{5,101},{6,102},{7,103},{8,104... | collective-permute-start | bytes 344072 | tf_op jit(solution)/shard_map/ppermute | solution.py:799
  168.7 4.1 %copy-start.4 = (f32[2,112,128]{2,1,0:T(8,128)}, f32[2,112,128]{2,1,0:T(8,128)S(1)}, u32[]{:S(2)}) copy-start(f32[2,112,128]{2,1,0:T(8,128)S(1)} %add_third.1.refs_0_) | copy-start | bytes 344068
  168.8 4.1 %collective-permute-start.14 = (f32[2,112,128]{2,1,0:T(8,128)S(1)}, f32[2,112,128]{2,1,0:T(8,128)S(1)}, u32[]{:S(2)}, u32[]{:S(2)}) collective-permute-start(f32[2,112,128]{2,1,0:T(8,128)S(1)} %add_third.1.refs_0_), channel_id=1, source_target_pairs={{0,128},{128,0},{1,129},{129,1},{2,130},{130,2},{3,131},{131,3},{4... | collective-permute-start | bytes 344072 | tf_op jit(solution)/shard_map/ppermute | solution.py:815
  172.9 0.6 copy-start.5

commit v4 on v3

--- a/solution.py
+++ b/solution.py
@@ -727,7 +727,7 @@
     return call_kernel(back_kernel, ins, outs, scratch, BACK_LIMIT, "back")
 
 
-BACK_LIMIT = 58
+BACK_LIMIT = 50
 
 
 def local_step(core, tokens, grad_out, masters, vector, shares):

time: 177 us -> 174 us (0.983)
  Pallas kernels: 89.1 us -> 87.2 us
    unnamed x16 -> x28, local copies, waits for them, and re-layouts: 8.1 us -> 8.16 us
where the time goes in v4:
time: 174 us
  Pallas kernels  87.2 us (50%)
  waiting for transfers between devices  51.8 us (30%)
  starting transfers between devices  21.6 us (12%)
  local copies, waits for them, and re-layouts  12.4 us (7%)
    pallas_call x2, Pallas kernels, call_kernel(): pl.pallas_call(lambda *refs: kernel(spaces(ins, outs, scratch, refs)), gr...  77.9 us
    ppermute x12, waiting for transfers between devices, ring(): lax.ppermute(parts[s], GROUP_AXES, ring_pairs(stage, s))  41.7 us
    ppermute x12, starting transfers between devices, ring(): lax.ppermute(parts[s], GROUP_AXES, ring_pairs(stage, s))  17 us
    unnamed x28, local copies, waits for them, and re-layouts  8.16 us
    pallas_call x5, Pallas kernels, call_add(): pl.pallas_call(kernel, out_shape=[shape(F32, *out_dims, 128)] * count, in...  6.95 us
    ppermute x2, waiting for transfers between devices, swap_core(): return lax.ppermute(send, GROUP_AXES, core_pairs())  6.04 us
    ppermute x2, starting transfers between devices, swap_core(): return lax.ppermute(send, GROUP_AXES, core_pairs())  4.55 us
    dynamic_slice x5, local copies, waits for them, and re-layouts, body(): share = lax.dynamic_slice_in_dim(masters[kind_index], at, share_rows, 1)  4.21 us
  transfers between devices with their start and end apart: 15, of which 11 were waited for; matrix products, arithmetic and copies ran while one was open for 4% of the time, Pallas kernels for 14%

profile of v4, /device:TPU:1, one launch (start us, length us, event | category | flops | bytes accessed | tf_op | source)
XLA Modules:
  0.0 174.1 jit_solution(2204500273087151768)
XLA Ops:
  0.7 54.3 %front.1 = (bf16[20,9,64,128]{3,2,1,0:T(8,128)(2,1)}, bf16[20,3,64,128]{3,2,1,0:T(8,128)(2,1)}, bf16[2,512,384]{2,1,0:T(8,128)(2,1)}, f32[2,512,384]{2,1,0:T(8,1...) custom-call(s32[1]{0:T(128)} %bitcast.refs_0_, ...), custom_call_target="tpu_custom_call" | custom-call | tf_op jit(solution)/shard_map/front/pallas_call | solution.py:391
  55.1 3.3 %collective-permute-start = (f32[4,4,4,112,128]{4,3,2,1,0:T(8,128)}, f32[4,4,4,112,128]{4,3,2,1,0:T(8,128)}, u32[]{:S(2)}, u32[]{:S(2)}) collective-permute-start(f32[4,4,4,112,128]{4,3,2,1,0:T(8,128)} %get-tuple-element.119), channel_id=1, source_target_pairs={{0,4},{1,5},{2,6},{3,7},{4,0},{5,1},{6,2},{7,3},{8,12},{9,13},{10,... | collective-permute-start | bytes 11010056 | tf_op jit(solution)/shard_map/ppermute | solution.py:804
  58.4 0.9 constant_dynamic-slice_fusion.4
  59.3 0.6 copy.69
  59.9 0.8 constant_dynamic-slice_fusion.3
  60.7 0.6 copy.70
  61.3 3.4 %collective-permute-done.got = f32[4,4,4,112,128]{4,3,2,1,0:T(8,128)} collective-permute-done((f32[4,4,4,112,128]{4,3,2,1,0:T(8,128)}, f32[4,4,4,112,128]{4,3,2,1,0:T(8,128)}, u32[]{:S(2)}, u32[]{:S(2)}) %collective-permute-start) | collective-permute-done | bytes 3670048 | tf_op jit(solution)/shard_map/ppermute | solution.py:804
  64.8 2.0 %copy-done.1 = f32[4,4,4,112,128]{4,3,2,1,0:T(8,128)S(1)} copy-done((f32[4,4,4,112,128]{4,3,2,1,0:T(8,128)S(1)}, f32[4,4,4,112,128]{4,3,2,1,0:T(8,128)}, u32[]{:S(2)}) %copy-start.1) | copy-done | bytes 3670040
  66.8 0.0 copy-start.9
  66.8 0.0 copy-start.10
  66.8 3.2 %add_core.2 = (f32[4,4,112,128]{3,2,1,0:T(8,128)S(1)}, f32[4,4,112,128]{3,2,1,0:T(8,128)S(1)}, f32[4,4,112,128]{3,2,1,0:T(8,128)S(1)}, f32[4,4,112,128]{3,2,1,0:T(8,128)S(1)}) custom-call(f32[4,4,4,112,128]{4,3,2,1,0:T(8,128)S(1)} %copy-done.1, f32[4,4,4,112,128]{4,3,2,1,0:T(8,128)} %collective-permute-done.got), custom_call_target="tpu_custom_call" | custom-call | tf_op jit(solution)/shard_map/add_core/pallas_call | solution.py:788
  70.1 1.3 collective-permute-start.1
  71.3 0.4 collective-permute-start.2
  71.7 1.7 collective-permute-start.3
  73.5 23.6 %back.1 = (f32[20,50,384]{2,1,0:T(8,128)}, f32[4,4,4,112,128]{4,3,2,1,0:T(8,128)}, f32[4,4,4,112,128]{4,3,2,1,0:T(8,128)}) custom-call(s32[1]{0:T(128)} %bitcast.refs_0_, f32[2,512,384]{2,1,0:T(8,128)} %get-tuple-element.125.refs_1_, f32[2,4608]{1,0:T(2,128)S(1)} %copy-done.9, f32[1,128]{1,0:T(1,128)S(1)} %copy-done.10, bf16[1,384,1152]{2,1,0:T(8,128)(2,1)S(1)} %copy-done.5, ...), custom_call_target="tpu_custom_call" | custom-call | tf_op jit(solution)/shard_map/back/pallas_call | solution.py:391
  97.1 0.0 collective-permute-done.3.refs_7_
  97.1 0.9 copy-done.3
  98.0 1.2 collective-permute-start.4
  99.2 0.9 constant_dynamic-slice_fusion.2
  100.1 0.6 copy.68
  100.8 0.9 constant_dynamic-slice_fusion.1
  101.7 0.7 copy.67
  102.3 0.6 constant_dynamic-slice_fusion.refs_6_
  103.0 2.6 %collective-permute-done.4.got = f32[4,4,4,112,128]{4,3,2,1,0:T(8,128)} collective-permute-done((f32[4,4,4,112,128]{4,3,2,1,0:T(8,128)}, f32[4,4,4,112,128]{4,3,2,1,0:T(8,128)}, u32[]{:S(2)}, u32[]{:S(2)}) %collective-permute-start.4) | collective-permute-done | bytes 3670048 | tf_op jit(solution)/shard_map/ppermute | solution.py:804
  105.6 2.0 %copy-done = f32[4,4,4,112,128]{4,3,2,1,0:T(8,128)S(1)} copy-done((f32[4,4,4,112,128]{4,3,2,1,0:T(8,128)S(1)}, f32[4,4,4,112,128]{4,3,2,1,0:T(8,128)}, u32[]{:S(2)}) %copy-start) | copy-done | bytes 3670040
  107.6 3.2 %add_core.3 = (f32[4,4,112,128]{3,2,1,0:T(8,128)S(1)}, f32[4,4,112,128]{3,2,1,0:T(8,128)S(1)}, f32[4,4,112,128]{3,2,1,0:T(8,128)S(1)}, f32[4,4,112,128]{3,2,1,0:T(8,128)S(1)}) custom-call(f32[4,4,4,112,128]{4,3,2,1,0:T(8,128)S(1)} %copy-done, f32[4,4,4,112,128]{4,3,2,1,0:T(8,128)} %collective-permute-done.4.got), custom_call_target="tpu_custom_call" | custom-call | tf_op jit(solution)/shard_map/add_core/pallas_call | solution.py:788
  110.8 1.3 collective-permute-start.5
  112.1 0.4 collective-permute-start.6
  112.5 1.6 collective-permute-start.7
  114.1 10.8 %collective-permute-done.5.refs_1_ = f32[4,4,112,128]{3,2,1,0:T(8,128)S(1)} collective-permute-done((f32[4,4,112,128]{3,2,1,0:T(8,128)S(1)}, f32[4,4,112,128]{3,2,1,0:T(8,128)S(1)}, u32[]{:S(2)}, u32[]{:S(2)}) %collective-permute-start.5) | collective-permute-done | bytes 917536 | tf_op jit(solution)/shard_map/ppermute | solution.py:799
  125.0 8.5 %collective-permute-done.6.refs_2_ = f32[4,4,112,128]{3,2,1,0:T(8,128)S(1)} collective-permute-done((f32[4,4,112,128]{3,2,1,0:T(8,128)S(1)}, f32[4,4,112,128]{3,2,1,0:T(8,128)S(1)}, u32[]{:S(2)}, u32[]{:S(2)}) %collective-permute-start.6) | collective-permute-done | bytes 917536 | tf_op jit(solution)/shard_map/ppermute | solution.py:799
  133.5 1.3 collective-permute-done.7.refs_3_
  134.8 0.4 add_first.1
  135.2 1.5 collective-permute-start.8
  136.7 0.3 collective-permute-start.9
  137.0 1.5 collective-permute-start.10
  138.5 5.9 %collective-permute-done.8.one = f32[4,2,112,128]{3,2,1,0:T(8,128)S(1)} collective-permute-done((f32[4,2,112,128]{3,2,1,0:T(8,128)S(1)}, f32[4,2,112,128]{3,2,1,0:T(8,128)S(1)}, u32[]{:S(2)}, u32[]{:S(2)}) %collective-permute-start.8) | collective-permute-done | bytes 458784 | tf_op jit(solution)/shard_map/ppermute | solution.py:799
  144.5 3.7 %collective-permute-done.9.two = f32[4,2,112,128]{3,2,1,0:T(8,128)S(1)} collective-permute-done((f32[4,2,112,128]{3,2,1,0:T(8,128)S(1)}, f32[4,2,112,128]{3,2,1,0:T(8,128)S(1)}, u32[]{:S(2)}, u32[]{:S(2)}) %collective-permute-start.9) | collective-permute-done | bytes 458784 | tf_op jit(solution)/shard_map/ppermute | solution.py:799
  148.1 1.2 collective-permute-done.10.three
  149.3 0.1 add_second.1
  149.4 5.8 %collective-permute-start.11 = (f32[2,112,128]{2,1,0:T(8,128)S(1)}, f32[2,112,128]{2,1,0:T(8,128)S(1)}, u32[]{:S(2)}, u32[]{:S(2)}) collective-permute-start(f32[2,112,128]{2,1,0:T(8,128)S(1)} %get-tuple-element.160), channel_id=1, source_target_pairs={{0,64},{1,65},{2,66},{3,67},{4,68},{5,69},{6,70},{7,71},{8,72},{9,... | collective-permute-start | bytes 344072 | tf_op jit(solution)/shard_map/ppermute | solution.py:799
  155.2 1.2 collective-permute-start.12
  156.4 1.1 collective-permute-done.11.one
  157.5 9.2 %collective-permute-done.12.two = f32[2,112,128]{2,1,0:T(8,128)S(1)} collective-permute-done((f32[2,112,128]{2,1,0:T(8,128)S(1)}, f32[2,112,128]{2,1,0:T(8,128)S(1)}, u32[]{:S(2)}, u32[]{:S(2)}) %collective-permute-start.12) | collective-permute-done | bytes 114720 | tf_op jit(solution)/shard_map/ppermute | solution.py:799
  166.8 0.1 collective-permute-start.14
  166.9 4.0 %collective-permute-done.14.refs_1_ = f32[2,112,128]{2,1,0:T(8,128)S(1)} collective-permute-done((f32[2,112,128]{2,1,0:T(8,128)S(1)}, f32[2,112,128]{2,1,0:T(8,128)S(1)}, u32[]{:S(2)}, u32[]{:S(2)}) %collective-permute-start.14) | collective-permute-done | bytes 114720 | tf_op jit(solution)/shard_map/ppermute | solution.py:815
  170.9 0.6 copy-done.11
  171.6 2.3 %finish.1 = (f32[3,2,1152]{2,1,0:T(2,128)}, f32[3,2,384]{2,1,0:T(2,128)}, f32[3,2,1536]{2,1,0:T(2,128)}, f32[12,2,384]{2,1,0:T(2,128)}, f32[2,36]{1,0:T(2,128)},...) custom-call(f32[2,112,128]{2,1,0:T(8,128)} %copy-done.7, ...), custom_call_target="tpu_custom_call" | custom-call | tf_op jit(solution)/shard_map/finish/pallas_call | solution.py:888
  (23 shorter events, 0.1 us)
Async XLA Ops:
  55.1 9.7 %collective-permute-start = (f32[4,4,4,112,128]{4,3,2,1,0:T(8,128)}, f32[4,4,4,112,128]{4,3,2,1,0:T(8,128)}, u32[]{:S(2)}, u32[]{:S(2)}) collective-permute-start(f32[4,4,4,112,128]{4,3,2,1,0:T(8,128)} %get-tuple-element.119), channel_id=1, source_target_pairs={{0,4},{1,5},{2,6},{3,7},{4,0},{5,1},{6,2},{7,3},{8,12},{9,13},{10,... | collective-permute-start | bytes 11010056 | tf_op jit(solution)/shard_map/ppermute | solution.py:804
  64.8 2.0 %copy-start.1 = (f32[4,4,4,112,128]{4,3,2,1,0:T(8,128)S(1)}, f32[4,4,4,112,128]{4,3,2,1,0:T(8,128)}, u32[]{:S(2)}) copy-start(f32[4,4,4,112,128]{4,3,2,1,0:T(8,128)} %get-tuple-element.118.keep) | copy-start | bytes 11010052
  66.8 6.6 %copy-start.2 = (bf16[20,3,64,128]{3,2,1,0:T(8,128)(2,1)S(1)}, bf16[20,3,64,128]{3,2,1,0:T(8,128)(2,1)}, u32[]{:S(2)}) copy-start(bf16[20,3,64,128]{3,2,1,0:T(8,128)(2,1)} %get-tuple-element.132.refs_9_) | copy-start | bytes 2949124
  66.8 6.6 %copy-start.5 = (bf16[1,384,1152]{2,1,0:T(8,128)(2,1)S(1)}, bf16[1,384,1152]{2,1,0:T(8,128)(2,1)}, u32[]{:S(2)}) copy-start(bf16[1,384,1152]{2,1,0:T(8,128)(2,1)} %get-tuple-element.127.refs_4_) | copy-start | bytes 2654212
  66.8 6.6 %copy-start.6 = (bf16[2,512,384]{2,1,0:T(8,128)(2,1)S(1)}, bf16[2,512,384]{2,1,0:T(8,128)(2,1)}, u32[]{:S(2)}) copy-start(bf16[2,512,384]{2,1,0:T(8,128)(2,1)} %get-tuple-element.133.refs_10_) | copy-start | bytes 2359300
  66.8 6.6 %copy-start.8 = (bf16[1,384,384]{2,1,0:T(8,128)(2,1)S(1)}, bf16[1,384,384]{2,1,0:T(8,128)(2,1)}, u32[]{:S(2)}) copy-start(bf16[1,384,384]{2,1,0:T(8,128)(2,1)} %get-tuple-element.128.refs_5_) | copy-start | bytes 884740
  66.8 6.6 %copy-start.9 = (f32[2,4608]{1,0:T(2,128)S(1)}, f32[2,4608]{1,0:T(2,128)}, u32[]{:S(2)}) copy-start(f32[2,4608]{1,0:T(2,128)} %refs_2_.3) | copy-start | bytes 110596
  66.8 6.6 %copy-start.10 = (f32[1,128]{1,0:T(1,128)S(1)}, f32[1,128]{1,0:T(1,128)}, u32[]{:S(2)}) copy-start(f32[1,128]{1,0:T(1,128)} %get-tuple-element.126.refs_3_) | copy-start | bytes 1540
  70.1 26.9 %collective-permute-start.1 = (f32[4,4,112,128]{3,2,1,0:T(8,128)S(1)}, f32[4,4,112,128]{3,2,1,0:T(8,128)S(1)}, u32[]{:S(2)}, u32[]{:S(2)}) collective-permute-start(f32[4,4,112,128]{3,2,1,0:T(8,128)S(1)} %get-tuple-element.142), channel_id=1, source_target_pairs={{0,2},{1,3},{2,0},{3,1},{4,20},{5,21},{6,22},{7,23},{8,10},{9,11},... | collective-permute-start | bytes 2752520 | tf_op jit(solution)/shard_map/ppermute | solution.py:799
  71.3 25.7 %collective-permute-start.2 = (f32[4,4,112,128]{3,2,1,0:T(8,128)S(1)}, f32[4,4,112,128]{3,2,1,0:T(8,128)S(1)}, u32[]{:S(2)}, u32[]{:S(2)}) collective-permute-start(f32[4,4,112,128]{3,2,1,0:T(8,128)S(1)} %get-tuple-element.143), channel_id=1, source_target_pairs={{0,1},{1,0},{2,3},{3,2},{4,12},{5,13},{6,14},{7,15},{8,9},{9,8},{1... | collective-permute-start | bytes 2752520 | tf_op jit(solution)/shard_map/ppermute | solution.py:799
  71.7 25.3 %collective-permute-start.3 = (f32[4,4,112,128]{3,2,1,0:T(8,128)S(1)}, f32[4,4,112,128]{3,2,1,0:T(8,128)S(1)}, u32[]{:S(2)}, u32[]{:S(2)}) collective-permute-start(f32[4,4,112,128]{3,2,1,0:T(8,128)S(1)} %get-tuple-element.144), channel_id=1, source_target_pairs={{0,3},{1,2},{2,1},{3,0},{4,28},{5,29},{6,30},{7,31},{8,11},{9,10},... | collective-permute-start | bytes 2752520 | tf_op jit(solution)/shard_map/ppermute | solution.py:799
  97.1 0.9 copy-start.3
  98.0 7.6 %collective-permute-start.4 = (f32[4,4,4,112,128]{4,3,2,1,0:T(8,128)}, f32[4,4,4,112,128]{4,3,2,1,0:T(8,128)}, u32[]{:S(2)}, u32[]{:S(2)}) collective-permute-start(f32[4,4,4,112,128]{4,3,2,1,0:T(8,128)} %get-tuple-element.145), channel_id=1, source_target_pairs={{0,4},{1,5},{2,6},{3,7},{4,0},{5,1},{6,2},{7,3},{8,12},{9,13},{10,... | collective-permute-start | bytes 11010056 | tf_op jit(solution)/shard_map/ppermute | solution.py:804
  105.6 2.0 %copy-start = (f32[4,4,4,112,128]{4,3,2,1,0:T(8,128)S(1)}, f32[4,4,4,112,128]{4,3,2,1,0:T(8,128)}, u32[]{:S(2)}) copy-start(f32[4,4,4,112,128]{4,3,2,1,0:T(8,128)} %get-tuple-element.139.keep) | copy-start | bytes 11010052
  107.6 27.1 %copy-start.4 = (f32[4,4,112,128]{3,2,1,0:T(8,128)S(1)}, f32[4,4,112,128]{3,2,1,0:T(8,128)}, u32[]{:S(2)}) copy-start(f32[4,4,112,128]{3,2,1,0:T(8,128)} %copy-done.3) | copy-start | bytes 2752516
  110.8 14.2 %collective-permute-start.5 = (f32[4,4,112,128]{3,2,1,0:T(8,128)S(1)}, f32[4,4,112,128]{3,2,1,0:T(8,128)S(1)}, u32[]{:S(2)}, u32[]{:S(2)}) collective-permute-start(f32[4,4,112,128]{3,2,1,0:T(8,128)S(1)} %get-tuple-element.148), channel_id=1, source_target_pairs={{0,2},{1,3},{2,0},{3,1},{4,20},{5,21},{6,22},{7,23},{8,10},{9,11},... | collective-permute-start | bytes 2752520 | tf_op jit(solution)/shard_map/ppermute | solution.py:799
  112.1 21.3 %collective-permute-start.6 = (f32[4,4,112,128]{3,2,1,0:T(8,128)S(1)}, f32[4,4,112,128]{3,2,1,0:T(8,128)S(1)}, u32[]{:S(2)}, u32[]{:S(2)}) collective-permute-start(f32[4,4,112,128]{3,2,1,0:T(8,128)S(1)} %get-tuple-element.149), channel_id=1, source_target_pairs={{0,1},{1,0},{2,3},{3,2},{4,12},{5,13},{6,14},{7,15},{8,9},{9,8},{1... | collective-permute-start | bytes 2752520 | tf_op jit(solution)/shard_map/ppermute | solution.py:799
  112.5 22.2 %collective-permute-start.7 = (f32[4,4,112,128]{3,2,1,0:T(8,128)S(1)}, f32[4,4,112,128]{3,2,1,0:T(8,128)S(1)}, u32[]{:S(2)}, u32[]{:S(2)}) collective-permute-start(f32[4,4,112,128]{3,2,1,0:T(8,128)S(1)} %get-tuple-element.150), channel_id=1, source_target_pairs={{0,3},{1,2},{2,1},{3,0},{4,28},{5,29},{6,30},{7,31},{8,11},{9,10},... | collective-permute-start | bytes 2752520 | tf_op jit(solution)/shard_map/ppermute | solution.py:799
  135.2 9.3 %collective-permute-start.8 = (f32[4,2,112,128]{3,2,1,0:T(8,128)S(1)}, f32[4,2,112,128]{3,2,1,0:T(8,128)S(1)}, u32[]{:S(2)}, u32[]{:S(2)}) collective-permute-start(f32[4,2,112,128]{3,2,1,0:T(8,128)S(1)} %get-tuple-element.156), channel_id=1, source_target_pairs={{0,16},{1,17},{2,18},{3,19},{4,6},{5,7},{6,4},{7,5},{8,24},{9,25},... | collective-permute-start | bytes 1376264 | tf_op jit(solution)/shard_map/ppermute | solution.py:799
  136.7 11.4 %collective-permute-start.9 = (f32[4,2,112,128]{3,2,1,0:T(8,128)S(1)}, f32[4,2,112,128]{3,2,1,0:T(8,128)S(1)}, u32[]{:S(2)}, u32[]{:S(2)}) collective-permute-start(f32[4,2,112,128]{3,2,1,0:T(8,128)S(1)} %get-tuple-element.157), channel_id=1, source_target_pairs={{0,8},{1,9},{2,10},{3,11},{4,5},{5,4},{6,7},{7,6},{8,0},{9,1},{10,... | collective-permute-start | bytes 1376264 | tf_op jit(solution)/shard_map/ppermute | solution.py:799
  137.0 12.3 %collective-permute-start.10 = (f32[4,2,112,128]{3,2,1,0:T(8,128)S(1)}, f32[4,2,112,128]{3,2,1,0:T(8,128)S(1)}, u32[]{:S(2)}, u32[]{:S(2)}) collective-permute-start(f32[4,2,112,128]{3,2,1,0:T(8,128)S(1)} %get-tuple-element.158), channel_id=1, source_target_pairs={{0,24},{1,25},{2,26},{3,27},{4,7},{5,6},{6,5},{7,4},{8,16},{9,17},... | collective-permute-start | bytes 1376264 | tf_op jit(solution)/shard_map/ppermute | solution.py:799
  149.4 8.1 %collective-permute-start.11 = (f32[2,112,128]{2,1,0:T(8,128)S(1)}, f32[2,112,128]{2,1,0:T(8,128)S(1)}, u32[]{:S(2)}, u32[]{:S(2)}) collective-permute-start(f32[2,112,128]{2,1,0:T(8,128)S(1)} %get-tuple-element.160), channel_id=1, source_target_pairs={{0,64},{1,65},{2,66},{3,67},{4,68},{5,69},{6,70},{7,71},{8,72},{9,... | collective-permute-start | bytes 344072 | tf_op jit(solution)/shard_map/ppermute | solution.py:799
  155.2 11.5 %collective-permute-start.12 = (f32[2,112,128]{2,1,0:T(8,128)S(1)}, f32[2,112,128]{2,1,0:T(8,128)S(1)}, u32[]{:S(2)}, u32[]{:S(2)}) collective-permute-start(f32[2,112,128]{2,1,0:T(8,128)S(1)} %get-tuple-element.161), channel_id=1, source_target_pairs={{0,32},{1,33},{2,34},{3,35},{4,36},{5,37},{6,38},{7,39},{8,40},{9,... | collective-permute-start | bytes 344072 | tf_op jit(solution)/shard_map/ppermute | solution.py:799
  156.4 10.3 %collective-permute-start.13 = (f32[2,112,128]{2,1,0:T(8,128)S(1)}, f32[2,112,128]{2,1,0:T(8,128)S(1)}, u32[]{:S(2)}, u32[]{:S(2)}) collective-permute-start(f32[2,112,128]{2,1,0:T(8,128)S(1)} %get-tuple-element.162), channel_id=1, source_target_pairs={{0,96},{1,97},{2,98},{3,99},{4,100},{5,101},{6,102},{7,103},{8,104... | collective-permute-start | bytes 344072 | tf_op jit(solution)/shard_map/ppermute | solution.py:799
  166.8 4.1 %copy-start.7 = (f32[2,112,128]{2,1,0:T(8,128)}, f32[2,112,128]{2,1,0:T(8,128)S(1)}, u32[]{:S(2)}) copy-start(f32[2,112,128]{2,1,0:T(8,128)S(1)} %add_third.1.refs_0_) | copy-start | bytes 344068
  166.8 4.1 %collective-permute-start.14 = (f32[2,112,128]{2,1,0:T(8,128)S(1)}, f32[2,112,128]{2,1,0:T(8,128)S(1)}, u32[]{:S(2)}, u32[]{:S(2)}) collective-permute-start(f32[2,112,128]{2,1,0:T(8,128)S(1)} %add_third.1.refs_0_), channel_id=1, source_target_pairs={{0,128},{128,0},{1,129},{129,1},{2,130},{130,2},{3,131},{131,3},{4... | collective-permute-start | bytes 344072 | tf_op jit(solution)/shard_map/ppermute | solution.py:815
  170.9 0.6 copy-start.11
